TPU v7x, 256 devices: a whole 4x4x8 slice. The times are simulated.
256 devices in a mesh: bx: 8 (over y_lo, x), by: 8 (over z), bz: 4 (over y_hi, core).
Axes of the slice: x: 4, y: 4 (y_hi: 2, y_lo: 2; y = y_hi * 2 + y_lo), z: 8, core: 2. Of those that a mesh axis runs over, the one named last changes fastest.
Arguments:
- estimate: float32 [128, 128, 512], P('bx', 'by', 'bz'), may hold values from 0.5 to 2
- raw_views: float32 [6, 128, 128, 512], P(None, 'bx', 'by', 'bz'), may hold values from 0.25 to 4
- psf: float32 [6, 3, 31], replicated, may hold values from 0.05 to 1
- offsets: int32 [6, 3], replicated, may hold values from -8 to 8, as said below
- coverage: int32 [6, 8, 8, 4], P(None, 'bx', 'by', 'bz'), may hold values from 0 to 1, as said below
Outputs:
- restored: float32 [128, 128, 512], P('bx', 'by', 'bz')
Inputs may be any that keep to these rules, and one draw needn't show every extreme that they name: `offsets`: one view has first component exactly 8 and the next view (cyclically) third component exactly -8. `coverage`: every output block is covered by at least one view.
All inputs are finite; a program needn't handle non-finite values.
Results may differ from a plain program's by a relative error of at most 0.0001.
Values sent between devices are 32-bit elements; how exact they have to be, the bound alone decides.
No kernel may reach another device: no remote copies, remote signals or barrier semaphores. Data moves between devices by JAX's collectives and lax.ppermute only.
A program may use at most 128 MiB of HBM per device.

v0:
```python
import jax
import jax.numpy as jnp
from jax import lax
from jax.experimental import pallas as pl
from jax.experimental.pallas import tpu as pltpu
from jax.sharding import PartitionSpec as P

V = 6
K = 31
R = 15
OFF = 8
C = 16
Z = 128
W = 3 * C
HIGH = lax.Precision.HIGH

VM = pl.BlockSpec(memory_space=pltpu.VMEM)
SM = pl.BlockSpec(memory_space=pltpu.SMEM)


def call(body, outs, specs, scratch=(), flops=0, moved=0, vmem=48, grid=()):
    return pl.pallas_call(
        body,
        grid=grid,
        out_shape=[jax.ShapeDtypeStruct(s, jnp.float32) for s in outs],
        in_specs=specs,
        out_specs=[VM] * len(outs),
        scratch_shapes=list(scratch),
        compiler_params=pltpu.CompilerParams(vmem_limit_bytes=vmem << 20),
        cost_estimate=pl.CostEstimate(
            flops=flops, bytes_accessed=moved, transcendentals=0
        ),
    )


def edges(axis):
    place = lax.axis_index(axis)
    return place > 0, place < lax.axis_size(axis) - 1


def shift(block, axis, step):
    count = lax.axis_size(axis)
    return lax.ppermute(block, axis, [(i, (i + step) % count) for i in range(count)])


def lanes(rows):
    return lax.broadcasted_iota(jnp.int32, (rows, Z), 1)


def build_bands(line_y, line_z, flip_z, band_y, band_t, forward_z, backward_z):
    for view in range(V):
        row = jnp.broadcast_to(line_y[view : view + 1, :], (C, Z))
        band_y[view * C : (view + 1) * C, :] = pltpu.roll(
            row, 1, 1, stride=1, stride_axis=0
        )
        row = jnp.broadcast_to(flip_z[view : view + 1, :], (2 * Z, 2 * Z))
        forward_z[view] = pltpu.roll(row, 2 * Z - R, 1, stride=1, stride_axis=0)
        row = jnp.broadcast_to(line_z[view : view + 1, :], (2 * Z, 2 * Z))
        backward_z[view] = pltpu.roll(row, 2 * Z - R, 1, stride=1, stride_axis=0)[:, :Z]
    band_t[...] = band_y[...].T[:W, :]


def pack_rows(cover, raw, up, down):
    for view in range(V):
        up[view, :C] = raw[view, :, OFF:, :]
        down[view, :C] = raw[view, :, :OFF, :]
        level = jnp.full((OFF, Z), cover[view, 0].astype(jnp.float32))
        up[view, C] = level
        down[view, C] = level


def shift_rows(offsets, cover, raw, low, high, moved, up, down, wide):
    has_low, has_high = edges("by")
    row = lax.broadcasted_iota(jnp.int32, (C, Z), 0)
    for view in range(V):
        wide[view, :, 0:OFF, :] = jnp.where(has_low, low[view, :C], 0.0)
        wide[view, :, OFF : OFF + C, :] = raw[view]
        wide[view, :, OFF + C :, :] = jnp.where(has_high, high[view, :C], 0.0)
        block = wide[view, :, pl.ds(OFF + offsets[view, 1], C), :]
        moved[view] = block
        own = jnp.full((C, Z), cover[view, 0].astype(jnp.float32))
        below = jnp.where(has_low, low[view, C], 0.0)
        above = jnp.where(has_high, high[view, C], 0.0)
        below = jnp.concatenate([below, below], axis=0)
        above = jnp.concatenate([above, above], axis=0)
        tile = jnp.where(row == 0, below, jnp.where(row == 1, own, above))
        up[view, :OFF] = block[OFF:]
        down[view, :OFF] = block[:OFF]
        up[view, OFF] = tile
        down[view, OFF] = tile


def join_planes(low, own, high, wide):
    has_low, has_high = edges("bx")
    wide[0:C] = jnp.where(has_low, low[...], 0.0)
    wide[C : 2 * C] = own[...]
    wide[2 * C :] = jnp.where(has_high, high[...], 0.0)


def pack_lanes(block, first):
    lane = lanes(64)
    packed = None
    for group in range(4):
        piece = block[4 * group : 4 * group + 4].reshape(64, Z)
        turn = (32 * group - first) % Z
        if turn:
            piece = pltpu.roll(piece, turn, 1)
        packed = piece if packed is None else jnp.where(lane >= 32 * group, piece, packed)
    return packed


def forward(
    offsets, taps_x, band_y, own, low, high, cover, rows, rows_low, rows_high,
    blurred, shifted, up, down, tiles, planes, wide,
):
    has_low, has_high = edges("by")
    left, right = edges("bx")
    band = band_y[:, :W]
    for pair in range(W // 2):
        sides = []
        for a in (2 * pair, 2 * pair + 1):
            sides.append(
                jnp.concatenate(
                    [
                        jnp.where(has_low, low[a], 0.0),
                        own[a],
                        jnp.where(has_high, high[a], 0.0),
                    ],
                    axis=0,
                )
            )
        both = jnp.dot(
            band, jnp.concatenate(sides, axis=1), precision=HIGH,
            preferred_element_type=jnp.float32,
        )
        planes[2 * pair] = both[:, :Z]
        planes[2 * pair + 1] = both[:, Z:]

    @pl.loop(0, V)
    def _(view):
        taps = [jnp.full((8, Z), taps_x[view * K + t]) for t in range(K)]
        for half in range(2):
            sums = [None] * C
            for a in range(1, W - 1):
                plane = planes[a, pl.ds(pl.multiple_of(view * C + 8 * half, 8), 8), :]
                for i in range(C):
                    t = a - i - 1
                    if 0 <= t < K:
                        term = taps[t] * plane
                        sums[i] = term if sums[i] is None else sums[i] + term
            for i in range(C):
                blurred[view, i, 8 * half : 8 * half + 8, :] = sums[i]
        block = blurred[view]
        up[view] = pack_lanes(block, 96)
        down[view] = pack_lanes(block, 0)
        wide[0:OFF] = jnp.where(left, rows_low[view, :OFF], 0.0)
        wide[OFF : OFF + C] = rows[view]
        wide[OFF + C :] = jnp.where(right, rows_high[view, :OFF], 0.0)
        block = wide[pl.ds(OFF + offsets[view, 0], C)]
        shifted[view] = block
        up[V + view] = pack_lanes(block, 96)
        down[V + view] = pack_lanes(block, 0)

    lane = lanes(8)
    up[2 * V] = jnp.zeros((64, Z), jnp.float32)
    down[2 * V] = jnp.zeros((64, Z), jnp.float32)
    for view in range(V):
        below = jnp.where(left, rows_low[view, OFF, :8], 0.0)
        above = jnp.where(right, rows_high[view, OFF, :8], 0.0)
        middle = cover[view, OFF, :8]
        tile = jnp.where(lane == 0, below, jnp.where(lane == 1, middle, above))
        up[2 * V, 8 * view : 8 * view + 8] = tile
        down[2 * V, 8 * view : 8 * view + 8] = tile
        tiles[8 * view : 8 * view + 8] = tile


def ring(block, low, high, has_low, has_high):
    lane = lanes(64)
    sides = []
    for group in range(4):
        before = pltpu.roll(low, 96 - 32 * group, 1) if group < 3 else low
        after = pltpu.roll(high, (Z - 32 * group) % Z, 1) if group else high
        before = jnp.where(jnp.logical_and(lane >= 96, has_low), before, 0.0)
        after = jnp.where(jnp.logical_and(lane < 32, has_high), after, 0.0)
        sides.append(before + after)
    return jnp.concatenate([block, jnp.concatenate(sides, axis=0)], axis=1)


def ratio_back(
    offsets, taps_x, band_t, forward_z, backward_z, blurred, shifted, low, high, tiles,
    out_low, out_mid, out_high, spread, planes,
):
    has_low, has_high = edges("bz")
    lane = lax.broadcasted_iota(jnp.int32, (1, 2 * Z), 1)

    @pl.loop(0, V)
    def _(view):
        block = ring(
            blurred[view].reshape(C * C, Z), low[view], high[view], has_low, has_high
        )
        model = jnp.dot(
            block, forward_z[view], precision=HIGH, preferred_element_type=jnp.float32
        )
        seen = ring(
            shifted[view].reshape(C * C, Z), low[V + view], high[V + view],
            has_low, has_high,
        )
        seen = pltpu.roll(seen, lax.rem(2 * Z - offsets[view, 2], 2 * Z), 1)
        row = pl.ds(pl.multiple_of(view * 8, 8), 8)
        own = jnp.broadcast_to(tiles[row, :][1:2, 1:2], (1, 2 * Z))
        after = jnp.broadcast_to(high[2 * V, row, :][1:2, 1:2], (1, 2 * Z))
        before = jnp.broadcast_to(low[2 * V, row, :][1:2, 1:2], (1, 2 * Z))
        after = jnp.where(jnp.logical_and(lane < Z + R, has_high), after, 0.0)
        before = jnp.where(
            jnp.logical_and(lane >= 2 * Z - R, has_low), before, 0.0
        )
        mask = jnp.where(lane < Z, own, after + before)
        ratio = jnp.where(mask > 0.0, mask * seen / model, 0.0)
        back = jnp.dot(
            ratio, backward_z[view], precision=HIGH, preferred_element_type=jnp.float32
        )
        spread[...] = back.reshape(C, C, Z)
        taps = [jnp.full((8, Z), taps_x[view * K + t]) for t in range(K)]
        for half in range(2):
            source = [spread[i, 8 * half : 8 * half + 8, :] for i in range(C)]
            for a in range(1, W - 1):
                total = None
                for i in range(C):
                    t = a - i - 1
                    if 0 <= t < K:
                        term = taps[t] * source[i]
                        total = term if total is None else total + term
                planes[a, pl.ds(pl.multiple_of(view * C + 8 * half, 8), 8), :] = total

    planes[0] = jnp.zeros((V * C, Z), jnp.float32)
    planes[W - 1] = jnp.zeros((V * C, Z), jnp.float32)
    for pair in range(W // 2):
        both = jnp.concatenate([planes[2 * pair], planes[2 * pair + 1]], axis=1)
        both = jnp.dot(
            band_t[...], both, precision=HIGH, preferred_element_type=jnp.float32
        )
        for side in range(2):
            part = both[:, side * Z : (side + 1) * Z]
            out_low[2 * pair + side] = part[:C]
            out_mid[2 * pair + side] = part[C : 2 * C]
            out_high[2 * pair + side] = part[2 * C :]


def add_rows(mid, from_low, from_high, out_low, out_mid, out_high):
    has_low, has_high = edges("by")
    total = (
        mid[...]
        + jnp.where(has_low, from_low[...], 0.0)
        + jnp.where(has_high, from_high[...], 0.0)
    )
    out_low[...] = total[:C]
    out_mid[...] = total[C : 2 * C]
    out_high[...] = total[2 * C :]


def weigh(part_x, part_y, part_z, tiles, low, high, weights):
    has_low, has_high = edges("bz")
    sums = [jnp.zeros((C, Z), jnp.float32) for _ in range(C)]
    for view in range(V):
        row = slice(8 * view, 8 * view + 8)
        near = [
            jnp.where(has_low, low[0, row], 0.0),
            tiles[row],
            jnp.where(has_high, high[0, row], 0.0),
        ]
        for p in range(3):
            term = None
            for r in range(3):
                level = None
                for q in range(3):
                    cell = jnp.broadcast_to(near[r][q : q + 1, p : p + 1], (C, Z))
                    cell = cell * part_y[view, q]
                    level = cell if level is None else level + cell
                level = level * part_z[view, r : r + 1, :]
                term = level if term is None else term + level
            for i in range(C):
                sums[i] = sums[i] + part_x[(view * C + i) * 3 + p] * term
    for i in range(C):
        weights[i] = sums[i]


def finish(estimate, mid, from_low, from_high, weights, out):
    has_low, has_high = edges("bx")
    total = (
        mid[...]
        + jnp.where(has_low, from_low[...], 0.0)
        + jnp.where(has_high, from_high[...], 0.0)
    )
    out[...] = estimate[...] * total / weights[...]


def block_parts(taps, count):
    cell = jnp.arange(count)[:, None]
    tap = jnp.arange(K)[None, :]
    before = (tap > cell + R).astype(jnp.float32)
    after = (tap < cell + R + 1 - count).astype(jnp.float32)
    which = jnp.stack([before, 1.0 - before - after, after])
    return jnp.einsum("vt,pit->vip", taps, which, precision=lax.Precision.HIGHEST)


def on_device(estimate, raw, psf, offsets, coverage):
    taps = psf / jnp.sum(psf, axis=2, keepdims=True)
    taps_x = taps[:, 0].reshape(V * K)
    line_y = jnp.pad(taps[:, 1], ((0, 0), (0, Z - K)))
    line_z = jnp.pad(taps[:, 2], ((0, 0), (0, 2 * Z - K)))
    flip_z = jnp.pad(jnp.flip(taps[:, 2], 1), ((0, 0), (0, 2 * Z - K)))
    part_x = block_parts(taps[:, 0], C).reshape(V * C * 3)
    part_y = jnp.broadcast_to(
        block_parts(taps[:, 1], C).transpose(0, 2, 1)[..., None], (V, 3, C, Z)
    )
    part_z = block_parts(taps[:, 2], Z).transpose(0, 2, 1)
    cover = coverage.reshape(V, 1)

    left = shift(estimate, "bx", 1)
    right = shift(estimate, "bx", -1)
    up, down = call(
        pack_rows, [(V, C + 1, OFF, Z)] * 2, [SM, VM], moved=3 << 19
    )(cover, raw)
    rows_low = shift(up, "by", 1)
    rows_high = shift(down, "by", -1)
    band_y, band_t, forward_z, backward_z = call(
        build_bands,
        [(V * C, Z), (W, V * C), (V, 2 * Z, 2 * Z), (V, 2 * Z, Z)],
        [VM, VM, VM],
        moved=3 << 20,
    )(line_y, line_z, flip_z)
    (wide,) = call(join_planes, [(W, C, Z)], [VM] * 3, moved=3 << 18)(
        left, estimate, right
    )
    low = shift(wide, "by", 1)
    high = shift(wide, "by", -1)
    moved, up, down = call(
        shift_rows,
        [(V, C, C, Z), (V, OFF + 1, C, Z), (V, OFF + 1, C, Z)],
        [SM, SM, VM, VM, VM],
        [pltpu.VMEM((V, C, 2 * C, Z), jnp.float32)],
        moved=3 << 20,
    )(offsets, cover, raw, rows_low, rows_high)
    shifted_low = shift(up, "bx", 1)
    shifted_high = shift(down, "bx", -1)
    blurred, shifted, pack_up, pack_down, tiles = call(
        forward,
        [
            (V, C, C, Z),
            (V, C, C, Z),
            (2 * V + 1, 64, Z),
            (2 * V + 1, 64, Z),
            (V * 8, Z),
        ],
        [SM, SM] + [VM] * 8,
        [
            pltpu.VMEM((W, V * C, Z), jnp.float32),
            pltpu.VMEM((2 * C, C, Z), jnp.float32),
        ],
        flops=1 << 28,
        moved=6 << 20,
    )(offsets, taps_x, band_y, wide, low, high, up, moved, shifted_low, shifted_high)
    from_low = shift(pack_up, "bz", 1)
    from_high = shift(pack_down, "bz", -1)
    out_low, out_mid, out_high = call(
        ratio_back,
        [(W, C, Z)] * 3,
        [SM, SM] + [VM] * 8,
        [
            pltpu.VMEM((C, C, Z), jnp.float32),
            pltpu.VMEM((W, V * C, Z), jnp.float32),
        ],
        flops=1 << 29,
        moved=8 << 20,
    )(
        offsets, taps_x, band_t, forward_z, backward_z, blurred, shifted,
        from_low, from_high, tiles,
    )
    sum_low = shift(out_high, "by", 1)
    sum_high = shift(out_low, "by", -1)
    last = pl.BlockSpec((1, 64, Z), lambda i: (2 * V, 0, 0))
    (weights,) = call(
        weigh, [(C, C, Z)], [SM, VM, VM, VM, last, last], moved=1 << 19, grid=(1,)
    )(part_x, part_y, part_z, tiles, from_low, from_high)
    out_low, out_mid, out_high = call(
        add_rows, [(C, C, Z)] * 3, [VM] * 3, moved=3 << 19
    )(out_mid, sum_low, sum_high)
    sum_low = shift(out_high, "bx", 1)
    sum_high = shift(out_low, "bx", -1)
    (out,) = call(finish, [(C, C, Z)], [VM] * 5, moved=3 << 18)(
        estimate, out_mid, sum_low, sum_high, weights
    )
    return out


def solution(mesh):
    return jax.shard_map(
        on_device,
        mesh=mesh,
        in_specs=(
            P("bx", "by", "bz"),
            P(None, "bx", "by", "bz"),
            P(),
            P(),
            P(None, "bx", "by", "bz"),
        ),
        out_specs=P("bx", "by", "bz"),
        check_vma=False,
    )
```

profile of v0, /device:TPU:38, one launch (start us, length us, event | category | flops | bytes accessed | tf_op | source)
XLA Modules:
  0.0 89.4 jit_solution(12766573927597398456)
XLA Ops:
  0.0 1.5 %collective-permute-start = (f32[16,16,128]{2,1,0:T(8,128)}, f32[16,16,128]{2,1,0:T(8,128)S(1)}, u32[]{:S(2)}, u32[]{:S(2)}) collective-permute-start(f32[16,16,128]{2,1,0:T(8,128)} %estimate.1), channel_id=1, source_target_pairs={{0,32},{32,64},{64,96},{96,128},{128,160},{160,192},{192,224},{224... | collective-permute-start | bytes 393224 | tf_op jit(solution)/shard_map/ppermute | solution.py:43
  1.5 0.5 collective-permute-start.1
  2.0 0.7 copy.27.cover
  2.8 0.0 copy-start
  2.8 1.1 %copy-done = f32[6,16,16,128]{3,2,1,0:T(8,128)S(1)} copy-done((f32[6,16,16,128]{3,2,1,0:T(8,128)S(1)}, f32[6,16,16,128]{3,2,1,0:T(8,128)}, u32[]{:S(2)}) %copy-start) | copy-done | bytes 786456
  3.9 0.0 copy-start.1
  3.9 1.6 %shard_map.57 = (f32[6,17,8,128]{3,2,1,0:T(8,128)}, f32[6,17,8,128]{3,2,1,0:T(8,128)}) custom-call(s32[6,1]{1,0:T(8,128)S(1)} %copy.27.cover, f32[6,16,16,128]{3,2,1,0:T(8,128)S(1)} %copy-done), custom_call_target="tpu_custom_call" | custom-call | bytes 1572864 | tf_op jit(solution)/shard_map/pallas_call | solution.py:321
  5.5 1.9 %collective-permute-start.4 = (f32[6,17,8,128]{3,2,1,0:T(8,128)}, f32[6,17,8,128]{3,2,1,0:T(8,128)}, u32[]{:S(2)}, u32[]{:S(2)}) collective-permute-start(f32[6,17,8,128]{3,2,1,0:T(8,128)} %get-tuple-element.29), channel_id=1, source_target_pairs={{0,4},{4,8},{8,12},{12,16},{16,20},{20,24},{24,28},{28,0},{1,5},{5... | collective-permute-start | bytes 1253384 | tf_op jit(solution)/shard_map/ppermute | solution.py:43
  7.4 0.1 collective-permute-start.5
  7.5 0.8 reduce_sum.9
  8.3 0.1 copy.23
  8.4 0.8 copy_divide_fusion
  9.2 0.1 rev.4
  9.3 0.8 copy.29.offsets
  10.0 0.1 reshape_squeeze.3.taps_x
  10.1 0.5 shard_map.55
  10.6 0.1 fusion.9
  10.7 0.0 collective-permute-done.low
  10.7 0.0 collective-permute-done.1.high
  10.7 0.0 copy-start.6
  10.7 0.9 %copy-done.6 = f32[16,16,128]{2,1,0:T(8,128)S(1)} copy-done((f32[16,16,128]{2,1,0:T(8,128)S(1)}, f32[16,16,128]{2,1,0:T(8,128)}, u32[]{:S(2)}) %copy-start.6) | copy-done | bytes 131096
  11.7 2.0 %collective-permute-start.2 = (f32[48,16,128]{2,1,0:T(8,128)S(1)}, f32[48,16,128]{2,1,0:T(8,128)S(1)}, u32[]{:S(2)}, u32[]{:S(2)}) collective-permute-start(f32[48,16,128]{2,1,0:T(8,128)S(1)} %shard_map.56.own), channel_id=1, source_target_pairs={{0,4},{4,8},{8,12},{12,16},{16,20},{20,24},{24,28},{28,0},{1,5},{5... | collective-permute-start | bytes 1179656 | tf_op jit(solution)/shard_map/ppermute | solution.py:43
  13.7 2.1 %collective-permute-start.3 = (f32[48,16,128]{2,1,0:T(8,128)S(1)}, f32[48,16,128]{2,1,0:T(8,128)S(1)}, u32[]{:S(2)}, u32[]{:S(2)}) collective-permute-start(f32[48,16,128]{2,1,0:T(8,128)S(1)} %shard_map.56.own), channel_id=1, source_target_pairs={{0,28},{4,0},{8,4},{12,8},{16,12},{20,16},{24,20},{28,24},{1,29},{... | collective-permute-start | bytes 1179656 | tf_op jit(solution)/shard_map/ppermute | solution.py:43
  15.8 2.0 %collective-permute-done.4.low = f32[6,17,8,128]{3,2,1,0:T(8,128)} collective-permute-done((f32[6,17,8,128]{3,2,1,0:T(8,128)}, f32[6,17,8,128]{3,2,1,0:T(8,128)}, u32[]{:S(2)}, u32[]{:S(2)}) %collective-permute-start.4) | collective-permute-done | bytes 417824 | tf_op jit(solution)/shard_map/ppermute | solution.py:43
  17.8 2.5 %collective-permute-done.5.high = f32[6,17,8,128]{3,2,1,0:T(8,128)} collective-permute-done((f32[6,17,8,128]{3,2,1,0:T(8,128)}, f32[6,17,8,128]{3,2,1,0:T(8,128)}, u32[]{:S(2)}, u32[]{:S(2)}) %collective-permute-start.5) | collective-permute-done | bytes 417824 | tf_op jit(solution)/shard_map/ppermute | solution.py:43
  20.3 0.0 copy-done.1
  20.3 1.4 %shard_map.58 = (f32[6,16,16,128]{3,2,1,0:T(8,128)S(1)}, f32[6,9,16,128]{3,2,1,0:T(8,128)S(1)}, f32[6,9,16,128]{3,2,1,0:T(8,128)S(1)}) custom-call(s32[6,3]{1,0:T(8,128)S(1)} %copy.29.offsets, s32[6,1]{1,0:T(8,128)S(1)} %copy.27.cover, f32[6,16,16,128]{3,2,1,0:T(8,128)S(1)} %copy-done.1, f32[6,17,8,128]{3,2,1,0:T(8,128)} %collective-permute-done.4.low, ...), custom_call_target="tpu_custom_call" | custom-call | bytes 3145728 | tf_op jit(solution)/shard_map/pallas_call | solution.py:337
  21.7 3.7 %collective-permute-start.6 = (f32[6,9,16,128]{3,2,1,0:T(8,128)S(1)}, f32[6,9,16,128]{3,2,1,0:T(8,128)S(1)}, u32[]{:S(2)}, u32[]{:S(2)}) collective-permute-start(f32[6,9,16,128]{3,2,1,0:T(8,128)S(1)} %get-tuple-element.31.cover), channel_id=1, source_target_pairs={{0,32},{32,64},{64,96},{96,128},{128,160},{160,192},{192,224},{224... | collective-permute-start | bytes 1327112 | tf_op jit(solution)/shard_map/ppermute | solution.py:43
  25.4 0.0 collective-permute-start.7
  25.4 0.1 subtract_subtract_fusion.1
  25.4 0.2 convolution_bitcast_fusion
  25.6 0.0 collective-permute-done.2.low
  25.7 1.1 %collective-permute-done.3.high = f32[48,16,128]{2,1,0:T(8,128)S(1)} collective-permute-done((f32[48,16,128]{2,1,0:T(8,128)S(1)}, f32[48,16,128]{2,1,0:T(8,128)S(1)}, u32[]{:S(2)}, u32[]{:S(2)}) %collective-permute-start.3) | collective-permute-done | bytes 393248 | tf_op jit(solution)/shard_map/ppermute | solution.py:43
  26.7 4.6 %collective-permute-done.6.rows_low = f32[6,9,16,128]{3,2,1,0:T(8,128)S(1)} collective-permute-done((f32[6,9,16,128]{3,2,1,0:T(8,128)S(1)}, f32[6,9,16,128]{3,2,1,0:T(8,128)S(1)}, u32[]{:S(2)}, u32[]{:S(2)}) %collective-permute-start.6) | collective-permute-done | bytes 442400 | tf_op jit(solution)/shard_map/ppermute | solution.py:43
  31.3 4.4 %collective-permute-done.7.rows_high = f32[6,9,16,128]{3,2,1,0:T(8,128)S(1)} collective-permute-done((f32[6,9,16,128]{3,2,1,0:T(8,128)S(1)}, f32[6,9,16,128]{3,2,1,0:T(8,128)S(1)}, u32[]{:S(2)}, u32[]{:S(2)}) %collective-permute-start.7) | collective-permute-done | bytes 442400 | tf_op jit(solution)/shard_map/ppermute | solution.py:43
  35.8 5.3 %shard_map.59 = (f32[6,16,16,128]{3,2,1,0:T(8,128)S(1)}, f32[6,16,16,128]{3,2,1,0:T(8,128)S(1)}, f32[13,64,128]{2,1,0:T(8,128)}, f32[13,64,128]{2,1,0:T(8,128)}, f32[48,128]{1,0:T(8,128)S(1)}) custom-call(s32[6,3]{1,0:T(8,128)S(1)} %copy.29.offsets, f32[186]{0:T(256)S(1)} %reshape_squeeze.3.taps_x, f32[96,128]{1,0:T(8,128)S(1)} %get-tuple-element.28.band_y, ...), custom_call_target="tpu_custom_call" | custom-call | flops 268435456 | bytes 6291456 | tf_op jit(solution)/shard_map/pallas_call | solution.py:346
  41.1 0.0 copy-start.2
  41.1 0.9 copy-done.2
  42.0 0.9 %copy-done.4 = f32[6,16,16,128]{3,2,1,0:T(8,128)} copy-done((f32[6,16,16,128]{3,2,1,0:T(8,128)}, f32[6,16,16,128]{3,2,1,0:T(8,128)S(1)}, u32[]{:S(2)}) %copy-start.4) | copy-done | bytes 786456
  42.9 0.0 collective-permute-start.8
  42.9 3.2 %collective-permute-start.9 = (f32[13,64,128]{2,1,0:T(8,128)}, f32[13,64,128]{2,1,0:T(8,128)S(1)}, u32[]{:S(2)}, u32[]{:S(2)}) collective-permute-start(f32[13,64,128]{2,1,0:T(8,128)} %get-tuple-element.37), channel_id=1, source_target_pairs={{0,3},{1,0},{2,1},{3,2},{4,7},{5,4},{6,5},{7,6},{8,11},{9,8},{10,9... | collective-permute-start | bytes 1277960 | tf_op jit(solution)/shard_map/ppermute | solution.py:43
  46.2 0.2 fusion.6
  46.4 0.1 copy.30
  46.5 0.2 reshape.249.part_x
  46.8 6.7 %collective-permute-done.8.low = f32[13,64,128]{2,1,0:T(8,128)S(1)} collective-permute-done((f32[13,64,128]{2,1,0:T(8,128)}, f32[13,64,128]{2,1,0:T(8,128)S(1)}, u32[]{:S(2)}, u32[]{:S(2)}) %collective-permute-start.8) | collective-permute-done | bytes 426016 | tf_op jit(solution)/shard_map/ppermute | solution.py:43
  53.5 2.3 %collective-permute-done.9.high = f32[13,64,128]{2,1,0:T(8,128)S(1)} collective-permute-done((f32[13,64,128]{2,1,0:T(8,128)}, f32[13,64,128]{2,1,0:T(8,128)S(1)}, u32[]{:S(2)}, u32[]{:S(2)}) %collective-permute-start.9) | collective-permute-done | bytes 426016 | tf_op jit(solution)/shard_map/ppermute | solution.py:43
  55.8 1.1 %copy-done.3 = f32[6,16,16,128]{3,2,1,0:T(8,128)S(1)} copy-done((f32[6,16,16,128]{3,2,1,0:T(8,128)S(1)}, f32[6,16,16,128]{3,2,1,0:T(8,128)}, u32[]{:S(2)}) %copy-start.3) | copy-done | bytes 786456
  56.9 1.1 %copy-done.5 = f32[6,16,16,128]{3,2,1,0:T(8,128)S(1)} copy-done((f32[6,16,16,128]{3,2,1,0:T(8,128)S(1)}, f32[6,16,16,128]{3,2,1,0:T(8,128)}, u32[]{:S(2)}) %copy-start.5) | copy-done | bytes 786456
  58.0 6.6 %shard_map.60 = (f32[48,16,128]{2,1,0:T(8,128)S(1)}, f32[48,16,128]{2,1,0:T(8,128)S(1)}, f32[48,16,128]{2,1,0:T(8,128)S(1)}) custom-call(s32[6,3]{1,0:T(8,128)S(1)} %copy.29.offsets, f32[186]{0:T(256)S(1)} %reshape_squeeze.3.taps_x, f32[48,96]{1,0:T(8,128)S(1)} %get-tuple-element.25.band_t, f32[6,256,256]{2,1,0:T(8,128)S(1)} %get-tuple-element.26.forward_z, ...), custom_call_target="tpu_custom_call" | custom-call | flops 536870912 | bytes 8388608 | tf_op jit(solution)/shard_map/pallas_call | solution.py:365
  64.6 0.0 copy-start.7
  64.6 3.4 %collective-permute-start.10 = (f32[48,16,128]{2,1,0:T(8,128)S(1)}, f32[48,16,128]{2,1,0:T(8,128)S(1)}, u32[]{:S(2)}, u32[]{:S(2)}) collective-permute-start(f32[48,16,128]{2,1,0:T(8,128)S(1)} %get-tuple-element.40), channel_id=1, source_target_pairs={{0,4},{4,8},{8,12},{12,16},{16,20},{20,24},{24,28},{28,0},{1,5},{5... | collective-permute-start | bytes 1179656 | tf_op jit(solution)/shard_map/ppermute | solution.py:43
  68.0 0.0 collective-permute-start.11
  68.0 9.4 %collective-permute-done.10.from_low = f32[48,16,128]{2,1,0:T(8,128)S(1)} collective-permute-done((f32[48,16,128]{2,1,0:T(8,128)S(1)}, f32[48,16,128]{2,1,0:T(8,128)S(1)}, u32[]{:S(2)}, u32[]{:S(2)}) %collective-permute-start.10) | collective-permute-done | bytes 393248 | tf_op jit(solution)/shard_map/ppermute | solution.py:43
  77.4 3.5 %collective-permute-done.11.from_high = f32[48,16,128]{2,1,0:T(8,128)S(1)} collective-permute-done((f32[48,16,128]{2,1,0:T(8,128)S(1)}, f32[48,16,128]{2,1,0:T(8,128)S(1)}, u32[]{:S(2)}, u32[]{:S(2)}) %collective-permute-start.11) | collective-permute-done | bytes 393248 | tf_op jit(solution)/shard_map/ppermute | solution.py:43
  81.0 0.1 shard_map.61
  81.1 0.1 collective-permute-start.12
  81.1 2.0 %collective-permute-start.13 = (f32[16,16,128]{2,1,0:T(8,128)S(1)}, f32[16,16,128]{2,1,0:T(8,128)S(1)}, u32[]{:S(2)}, u32[]{:S(2)}) collective-permute-start(f32[16,16,128]{2,1,0:T(8,128)S(1)} %get-tuple-element.44), channel_id=1, source_target_pairs={{0,224},{32,0},{64,32},{96,64},{128,96},{160,128},{192,160},{224,1... | collective-permute-start | bytes 393224 | tf_op jit(solution)/shard_map/ppermute | solution.py:43
  83.2 0.1 fusion
  83.3 0.1 broadcast_in_dim.2.part_y
  83.4 1.0 %shard_map.62.weights = f32[16,16,128]{2,1,0:T(8,128)S(1)} custom-call(f32[288]{0:T(512)S(1)} %reshape.249.part_x, f32[6,3,16,128]{3,2,1,0:T(8,128)S(1)} %broadcast_in_dim.2.part_y, f32[6,3,128]{2,1,0:T(4,128)S(1)} %copy.32.part_z, f32[48,128]{1,0:T(8,128)S(1)} %get-tuple-element.38.tiles, f32[13,64,128]{2,1,0:T(8,128)S(1)} %collective-permute-done.8.low, ...), custom_call_target="tpu_custom_call" | custom-call | bytes 524288 | tf_op jit(solution)/shard_map/pallas_call | solution.py:382
  84.4 2.0 %collective-permute-done.12.from_low = f32[16,16,128]{2,1,0:T(8,128)S(1)} collective-permute-done((f32[16,16,128]{2,1,0:T(8,128)S(1)}, f32[16,16,128]{2,1,0:T(8,128)S(1)}, u32[]{:S(2)}, u32[]{:S(2)}) %collective-permute-start.12) | collective-permute-done | bytes 131104 | tf_op jit(solution)/shard_map/ppermute | solution.py:43
  86.5 2.2 %collective-permute-done.13.from_high = f32[16,16,128]{2,1,0:T(8,128)S(1)} collective-permute-done((f32[16,16,128]{2,1,0:T(8,128)S(1)}, f32[16,16,128]{2,1,0:T(8,128)S(1)}, u32[]{:S(2)}, u32[]{:S(2)}) %collective-permute-start.13) | collective-permute-done | bytes 131104 | tf_op jit(solution)/shard_map/ppermute | solution.py:43
  88.7 0.0 copy-done.7
  88.7 0.7 shard_map.63
  (15 shorter events, 0.1 us)
Async XLA Ops:
  0.0 10.7 %collective-permute-start = (f32[16,16,128]{2,1,0:T(8,128)}, f32[16,16,128]{2,1,0:T(8,128)S(1)}, u32[]{:S(2)}, u32[]{:S(2)}) collective-permute-start(f32[16,16,128]{2,1,0:T(8,128)} %estimate.1), channel_id=1, source_target_pairs={{0,32},{32,64},{64,96},{96,128},{128,160},{160,192},{192,224},{224... | collective-permute-start | bytes 393224 | tf_op jit(solution)/shard_map/ppermute | solution.py:43
  1.5 9.2 %collective-permute-start.1 = (f32[16,16,128]{2,1,0:T(8,128)}, f32[16,16,128]{2,1,0:T(8,128)S(1)}, u32[]{:S(2)}, u32[]{:S(2)}) collective-permute-start(f32[16,16,128]{2,1,0:T(8,128)} %estimate.1), channel_id=1, source_target_pairs={{0,224},{32,0},{64,32},{96,64},{128,96},{160,128},{192,160},{224,1... | collective-permute-start | bytes 393224 | tf_op jit(solution)/shard_map/ppermute | solution.py:43
  2.8 1.1 %copy-start = (f32[6,16,16,128]{3,2,1,0:T(8,128)S(1)}, f32[6,16,16,128]{3,2,1,0:T(8,128)}, u32[]{:S(2)}) copy-start(f32[6,16,16,128]{3,2,1,0:T(8,128)} %raw.3) | copy-start | bytes 2359300
  3.9 16.4 %copy-start.1 = (f32[6,16,16,128]{3,2,1,0:T(8,128)S(1)}, f32[6,16,16,128]{3,2,1,0:T(8,128)}, u32[]{:S(2)}) copy-start(f32[6,16,16,128]{3,2,1,0:T(8,128)} %raw.3) | copy-start | bytes 2359300
  5.5 12.3 %collective-permute-start.4 = (f32[6,17,8,128]{3,2,1,0:T(8,128)}, f32[6,17,8,128]{3,2,1,0:T(8,128)}, u32[]{:S(2)}, u32[]{:S(2)}) collective-permute-start(f32[6,17,8,128]{3,2,1,0:T(8,128)} %get-tuple-element.29), channel_id=1, source_target_pairs={{0,4},{4,8},{8,12},{12,16},{16,20},{20,24},{24,28},{28,0},{1,5},{5... | collective-permute-start | bytes 1253384 | tf_op jit(solution)/shard_map/ppermute | solution.py:43
  7.4 12.9 %collective-permute-start.5 = (f32[6,17,8,128]{3,2,1,0:T(8,128)}, f32[6,17,8,128]{3,2,1,0:T(8,128)}, u32[]{:S(2)}, u32[]{:S(2)}) collective-permute-start(f32[6,17,8,128]{3,2,1,0:T(8,128)} %get-tuple-element.30), channel_id=1, source_target_pairs={{0,28},{4,0},{8,4},{12,8},{16,12},{20,16},{24,20},{28,24},{1,29},{... | collective-permute-start | bytes 1253384 | tf_op jit(solution)/shard_map/ppermute | solution.py:43
  10.7 0.9 %copy-start.6 = (f32[16,16,128]{2,1,0:T(8,128)S(1)}, f32[16,16,128]{2,1,0:T(8,128)}, u32[]{:S(2)}) copy-start(f32[16,16,128]{2,1,0:T(8,128)} %estimate.1) | copy-start | bytes 393220
  11.7 14.0 %collective-permute-start.2 = (f32[48,16,128]{2,1,0:T(8,128)S(1)}, f32[48,16,128]{2,1,0:T(8,128)S(1)}, u32[]{:S(2)}, u32[]{:S(2)}) collective-permute-start(f32[48,16,128]{2,1,0:T(8,128)S(1)} %shard_map.56.own), channel_id=1, source_target_pairs={{0,4},{4,8},{8,12},{12,16},{16,20},{20,24},{24,28},{28,0},{1,5},{5... | collective-permute-start | bytes 1179656 | tf_op jit(solution)/shard_map/ppermute | solution.py:43
  13.7 13.1 %collective-permute-start.3 = (f32[48,16,128]{2,1,0:T(8,128)S(1)}, f32[48,16,128]{2,1,0:T(8,128)S(1)}, u32[]{:S(2)}, u32[]{:S(2)}) collective-permute-start(f32[48,16,128]{2,1,0:T(8,128)S(1)} %shard_map.56.own), channel_id=1, source_target_pairs={{0,28},{4,0},{8,4},{12,8},{16,12},{20,16},{24,20},{28,24},{1,29},{... | collective-permute-start | bytes 1179656 | tf_op jit(solution)/shard_map/ppermute | solution.py:43
  21.7 9.6 %collective-permute-start.6 = (f32[6,9,16,128]{3,2,1,0:T(8,128)S(1)}, f32[6,9,16,128]{3,2,1,0:T(8,128)S(1)}, u32[]{:S(2)}, u32[]{:S(2)}) collective-permute-start(f32[6,9,16,128]{3,2,1,0:T(8,128)S(1)} %get-tuple-element.31.cover), channel_id=1, source_target_pairs={{0,32},{32,64},{64,96},{96,128},{128,160},{160,192},{192,224},{224... | collective-permute-start | bytes 1327112 | tf_op jit(solution)/shard_map/ppermute | solution.py:43
  25.4 10.4 %collective-permute-start.7 = (f32[6,9,16,128]{3,2,1,0:T(8,128)S(1)}, f32[6,9,16,128]{3,2,1,0:T(8,128)S(1)}, u32[]{:S(2)}, u32[]{:S(2)}) collective-permute-start(f32[6,9,16,128]{3,2,1,0:T(8,128)S(1)} %get-tuple-element.33), channel_id=1, source_target_pairs={{0,224},{32,0},{64,32},{96,64},{128,96},{160,128},{192,160},{224,1... | collective-permute-start | bytes 1327112 | tf_op jit(solution)/shard_map/ppermute | solution.py:43
  41.1 0.9 %copy-start.2 = (f32[6,16,16,128]{3,2,1,0:T(8,128)}, f32[6,16,16,128]{3,2,1,0:T(8,128)S(1)}, u32[]{:S(2)}) copy-start(f32[6,16,16,128]{3,2,1,0:T(8,128)S(1)} %get-tuple-element.34.blurred) | copy-start | bytes 2359300
  42.0 0.9 %copy-start.4 = (f32[6,16,16,128]{3,2,1,0:T(8,128)}, f32[6,16,16,128]{3,2,1,0:T(8,128)S(1)}, u32[]{:S(2)}) copy-start(f32[6,16,16,128]{3,2,1,0:T(8,128)S(1)} %get-tuple-element.35.shifted) | copy-start | bytes 2359300
  42.9 10.6 %collective-permute-start.8 = (f32[13,64,128]{2,1,0:T(8,128)}, f32[13,64,128]{2,1,0:T(8,128)S(1)}, u32[]{:S(2)}, u32[]{:S(2)}) collective-permute-start(f32[13,64,128]{2,1,0:T(8,128)} %get-tuple-element.36), channel_id=1, source_target_pairs={{0,1},{1,2},{2,3},{3,0},{4,5},{5,6},{6,7},{7,4},{8,9},{9,10},{10,1... | collective-permute-start | bytes 1277960 | tf_op jit(solution)/shard_map/ppermute | solution.py:43
  42.9 12.8 %collective-permute-start.9 = (f32[13,64,128]{2,1,0:T(8,128)}, f32[13,64,128]{2,1,0:T(8,128)S(1)}, u32[]{:S(2)}, u32[]{:S(2)}) collective-permute-start(f32[13,64,128]{2,1,0:T(8,128)} %get-tuple-element.37), channel_id=1, source_target_pairs={{0,3},{1,0},{2,1},{3,2},{4,7},{5,4},{6,5},{7,6},{8,11},{9,8},{10,9... | collective-permute-start | bytes 1277960 | tf_op jit(solution)/shard_map/ppermute | solution.py:43
  55.8 1.1 %copy-start.3 = (f32[6,16,16,128]{3,2,1,0:T(8,128)S(1)}, f32[6,16,16,128]{3,2,1,0:T(8,128)}, u32[]{:S(2)}) copy-start(f32[6,16,16,128]{3,2,1,0:T(8,128)} %copy-done.2) | copy-start | bytes 2359300
  56.9 1.1 %copy-start.5 = (f32[6,16,16,128]{3,2,1,0:T(8,128)S(1)}, f32[6,16,16,128]{3,2,1,0:T(8,128)}, u32[]{:S(2)}) copy-start(f32[6,16,16,128]{3,2,1,0:T(8,128)} %copy-done.4) | copy-start | bytes 2359300
  64.6 24.0 %copy-start.7 = (f32[16,16,128]{2,1,0:T(8,128)S(1)}, f32[16,16,128]{2,1,0:T(8,128)}, u32[]{:S(2)}) copy-start(f32[16,16,128]{2,1,0:T(8,128)} %estimate.1) | copy-start | bytes 393220
  64.6 12.8 %collective-permute-start.10 = (f32[48,16,128]{2,1,0:T(8,128)S(1)}, f32[48,16,128]{2,1,0:T(8,128)S(1)}, u32[]{:S(2)}, u32[]{:S(2)}) collective-permute-start(f32[48,16,128]{2,1,0:T(8,128)S(1)} %get-tuple-element.40), channel_id=1, source_target_pairs={{0,4},{4,8},{8,12},{12,16},{16,20},{20,24},{24,28},{28,0},{1,5},{5... | collective-permute-start | bytes 1179656 | tf_op jit(solution)/shard_map/ppermute | solution.py:43
  68.0 13.0 %collective-permute-start.11 = (f32[48,16,128]{2,1,0:T(8,128)S(1)}, f32[48,16,128]{2,1,0:T(8,128)S(1)}, u32[]{:S(2)}, u32[]{:S(2)}) collective-permute-start(f32[48,16,128]{2,1,0:T(8,128)S(1)} %get-tuple-element.41), channel_id=1, source_target_pairs={{0,28},{4,0},{8,4},{12,8},{16,12},{20,16},{24,20},{28,24},{1,29},{... | collective-permute-start | bytes 1179656 | tf_op jit(solution)/shard_map/ppermute | solution.py:43
  81.1 5.4 %collective-permute-start.12 = (f32[16,16,128]{2,1,0:T(8,128)S(1)}, f32[16,16,128]{2,1,0:T(8,128)S(1)}, u32[]{:S(2)}, u32[]{:S(2)}) collective-permute-start(f32[16,16,128]{2,1,0:T(8,128)S(1)} %get-tuple-element.43), channel_id=1, source_target_pairs={{0,32},{32,64},{64,96},{96,128},{128,160},{160,192},{192,224},{224... | collective-permute-start | bytes 393224 | tf_op jit(solution)/shard_map/ppermute | solution.py:43
  81.1 7.5 %collective-permute-start.13 = (f32[16,16,128]{2,1,0:T(8,128)S(1)}, f32[16,16,128]{2,1,0:T(8,128)S(1)}, u32[]{:S(2)}, u32[]{:S(2)}) collective-permute-start(f32[16,16,128]{2,1,0:T(8,128)S(1)} %get-tuple-element.44), channel_id=1, source_target_pairs={{0,224},{32,0},{64,32},{96,64},{128,96},{160,128},{192,160},{224,1... | collective-permute-start | bytes 393224 | tf_op jit(solution)/shard_map/ppermute | solution.py:43
where the time goes:
time: 89.7 us; the launch traced here: 89.4 us
  waiting for transfers between devices  40.8 us (45%)
  starting transfers between devices  20.5 us (23%)
  Pallas kernels  17.2 us (19%)
  local copies, waits for them, and re-layouts  8.34 us (9%)
  other arithmetic  1.75 us (2%)
    ppermute x14, waiting for transfers between devices, shift(): lax.ppermute(block, axis, [(i, (i + step) % count) for i in range(count)])  40.8 us
    ppermute x14, starting transfers between devices, shift(): lax.ppermute(block, axis, [(i, (i + step) % count) for i in range(count)])  20.5 us
    unnamed x17, local copies, waits for them, and re-layouts  6.89 us
    pallas_call x1, Pallas kernels, on_device(): call(ratio_back, [(W, C, Z)] * 3, [SM, SM] + [VM] * 8, [pltpu.VMEM((C, C,...  6.58 us
    pallas_call x1, Pallas kernels, on_device(): call(forward, [(V, C, C, Z), (V, C, C, Z), (2 * V + 1, 64, Z), (2 * V + 1...  5.34 us
  transfers between devices with their start and end apart: 14, of which 11 were waited for; matrix products, arithmetic and copies ran while one was open for 5% of the time, Pallas kernels for 5%

commit v1 on v0

v1 whole, which is shorter than its diff:
```python
import jax
import jax.numpy as jnp
from jax import lax
from jax.experimental import pallas as pl
from jax.experimental.pallas import tpu as pltpu
from jax.sharding import PartitionSpec as P

V = 6
K = 31
R = 15
OFF = 8
C = 16
Z = 128
W = 3 * C
HIGH = lax.Precision.HIGH
HIGHEST = lax.Precision.HIGHEST
F32 = jnp.float32

VM = pl.BlockSpec(memory_space=pltpu.VMEM)
SM = pl.BlockSpec(memory_space=pltpu.SMEM)
ANY = pl.BlockSpec(memory_space=pl.ANY)
HBM = pl.BlockSpec(memory_space=pltpu.HBM)


def call(
    body, outs, specs, scratch=(), out_specs=None, grid=(), alias=None,
    flops=0, moved=0, vmem=16,
):
    return pl.pallas_call(
        body,
        grid=grid,
        out_shape=[jax.ShapeDtypeStruct(s, F32) for s in outs],
        in_specs=specs,
        out_specs=out_specs or [VM] * len(outs),
        scratch_shapes=list(scratch),
        input_output_aliases=alias or {},
        compiler_params=pltpu.CompilerParams(vmem_limit_bytes=vmem << 20),
        cost_estimate=pl.CostEstimate(
            flops=flops, bytes_accessed=moved, transcendentals=0
        ),
    )


def edges(axis):
    place = lax.axis_index(axis)
    return place > 0, place < lax.axis_size(axis) - 1


def even():
    return lax.rem(lax.axis_index("bz"), 2) == 0


def shift(block, axis, step):
    count = lax.axis_size(axis)
    return lax.ppermute(block, axis, [(i, (i + step) % count) for i in range(count)])


def swap(block, first):
    count = lax.axis_size("bz")
    pairs = []
    for i in range(first, count, 2):
        a, b = i % count, (i + 1) % count
        pairs += [(a, b), (b, a)]
    return lax.ppermute(block, "bz", pairs)


def lanes(rows):
    return lax.broadcasted_iota(jnp.int32, (rows, Z), 1)


def dot(a, b, precision=HIGH):
    return jnp.dot(a, b, precision=precision, preferred_element_type=F32)


def pack_planes(cover, raw, up, down, flags, sem):
    tag = pltpu.make_async_copy(cover, flags, sem)
    tag.start()
    up[:, :OFF] = raw[:, OFF:]
    down[:, :OFF] = raw[:, :OFF]
    tag.wait()
    for view in range(V):
        tile = jnp.full((C, Z), flags[view].astype(F32))
        up[view, OFF] = tile
        down[view, OFF] = tile


def build(
    offsets, psf, after, norm, table, band_y, band_t, forward_z, backward_z
):
    norm[...] = jnp.zeros((3, 8, Z), F32)
    for view in range(V):
        for axis in range(3):
            line = psf[view, axis : axis + 1, :]
            norm[axis, view : view + 1, 0:K] = line / jnp.sum(
                line, axis=1, keepdims=True
            )
    for view in range(V):
        line = norm[0, view : view + 1, :]
        for t in range(K):
            table[view, t] = jnp.broadcast_to(line[:, t : t + 1], (8, Z))
        row = jnp.broadcast_to(norm[1, view : view + 1, :], (C, Z))
        band_y[view * C : (view + 1) * C, :] = pltpu.roll(
            row, 1, 1, stride=1, stride_axis=0
        )
        row = norm[2, view : view + 1, :]
        row = jnp.concatenate([row, jnp.zeros((1, Z), F32)], axis=1)
        row = jnp.broadcast_to(row, (2 * Z, 2 * Z))
        band = pltpu.roll(row, 2 * Z - R, 1, stride=1, stride_axis=0)
        band = pltpu.roll(band, lax.rem(2 * Z - offsets[2, view], 2 * Z), 1)
        backward_z[view] = band[:, :Z]
        forward_z[view] = band[:Z, :].T
    band_t[...] = band_y[...].T[:W, :]


def join_planes(low, own, high, wide, sem):
    copy = pltpu.make_async_copy(own, wide.at[pl.ds(C, C)], sem)
    copy.start()
    has_low, has_high = edges("bx")
    wide[0:C] = jnp.where(has_low, low[...], 0.0)
    wide[2 * C :] = jnp.where(has_high, high[...], 0.0)
    copy.wait()


def pack_lanes(block, first):
    lane = lanes(64)
    packed = None
    for group in range(4):
        piece = block[4 * group : 4 * group + 4].reshape(64, Z)
        turn = (32 * group - first) % Z
        if turn:
            piece = pltpu.roll(piece, turn, 1)
        packed = piece if packed is None else jnp.where(lane >= 32 * group, piece, packed)
    return packed


def pack_sides(block, near, far, view):
    up = pack_lanes(block, 96)
    down = pack_lanes(block, 0)
    near[view, :64] = jnp.where(even(), up, down)
    far[view, :64] = jnp.where(even(), down, up)


def forward(table, band_y, own, low, high, cover, after, blurred, near, far, planes):
    has_low, has_high = edges("by")
    band = band_y[:, :W]
    for pair in range(W // 2):
        sides = []
        for a in (2 * pair, 2 * pair + 1):
            sides.append(
                jnp.concatenate(
                    [
                        jnp.where(has_low, low[a], 0.0),
                        own[a],
                        jnp.where(has_high, high[a], 0.0),
                    ],
                    axis=0,
                )
            )
        both = dot(band, jnp.concatenate(sides, axis=1))
        planes[2 * pair] = both[:, :Z]
        planes[2 * pair + 1] = both[:, Z:]

    @pl.loop(0, V)
    def _(view):
        taps = [table[view, t] for t in range(K)]
        for half in range(2):
            sums = [None] * C
            for a in range(1, W - 1):
                plane = planes[a, pl.ds(pl.multiple_of(view * C + 8 * half, 8), 8), :]
                for i in range(C):
                    t = a - i - 1
                    if 0 <= t < K:
                        term = taps[t] * plane
                        sums[i] = term if sums[i] is None else sums[i] + term
            for i in range(C):
                blurred[view, i, 8 * half : 8 * half + 8, :] = sums[i]
        pack_sides(blurred[view], near, far, view)

    for view in range(V):
        tile = jnp.full((8, Z), cover[view].astype(F32))
        near[view, 64:] = tile
        far[view, 64:] = tile


def ring(block, near, far):
    has_low, has_high = edges("bz")
    lane = lanes(64)
    low = jnp.where(even(), far, near)
    high = jnp.where(even(), near, far)
    sides = []
    for group in range(4):
        before = pltpu.roll(low, 96 - 32 * group, 1) if group < 3 else low
        after = pltpu.roll(high, (Z - 32 * group) % Z, 1) if group else high
        before = jnp.where(jnp.logical_and(lane >= 96, has_low), before, 0.0)
        after = jnp.where(jnp.logical_and(lane < 32, has_high), after, 0.0)
        sides.append(before + after)
    return jnp.concatenate([block, jnp.concatenate(sides, axis=0)], axis=1)


def shift_planes(
    offsets, cover, raw, low, high, after, shifted, up, down, tiles, wide
):
    has_low, has_high = edges("bx")
    lane = lanes(8)
    for view in range(V):
        wide[view, 0:OFF] = jnp.where(has_low, low[view, :OFF], 0.0)
        wide[view, OFF : OFF + C] = raw[view]
        wide[view, OFF + C :] = jnp.where(has_high, high[view, :OFF], 0.0)
        block = wide[view, pl.ds(OFF + offsets[0, view], C)]
        shifted[view, :, OFF : OFF + C] = block
        up[view, :C] = block[:, OFF:]
        down[view, :C] = block[:, :OFF]
        below = jnp.where(has_low, low[view, OFF, 0:8], 0.0)
        above = jnp.where(has_high, high[view, OFF, 0:8], 0.0)
        own = jnp.full((8, Z), cover[view].astype(F32))
        tile = jnp.where(lane == 0, below, jnp.where(lane == 1, own, above))
        tiles[view] = tile
        up[view, C] = tile
        down[view, C] = tile


def shift_rows(offsets, held, low, high, tiles, after, out, marks, main):
    has_low, has_high = edges("by")
    lane = lanes(8)
    for view in range(V):
        main[view, :, 0:OFF] = jnp.where(has_low, low[view, :C], 0.0)
        main[view, :, OFF + C :] = jnp.where(has_high, high[view, :C], 0.0)
        out[view] = main[view, :, pl.ds(OFF + offsets[1, view], C)]
        below = jnp.where(has_low, low[view, C], 0.0)
        above = jnp.where(has_high, high[view, C], 0.0)
        middle = pltpu.roll(tiles[view], 3, 1)
        above = pltpu.roll(above, 6, 1)
        marks[view] = jnp.where(lane < 3, below, jnp.where(lane < 6, middle, above))


def divide(
    offsets, cover, forward_z, blurred, low, high, seen, marks, ratio, near, far
):
    has_low, has_high = edges("bz")
    lane = lanes(1)
    for view in range(V):
        block = ring(
            blurred[view].reshape(C * C, Z), low[view, :64], high[view, :64]
        )
        model = dot(block, forward_z[view]).reshape(C, C, Z)
        before = jnp.where(even(), high[view, 64:65], low[view, 64:65])
        after = jnp.where(even(), low[view, 64:65], high[view, 64:65])
        before = jnp.where(has_low, before, 0.0)
        after = jnp.where(has_high, after, 0.0)
        own = jnp.full((1, Z), cover[view].astype(F32))
        place = lane - offsets[2, view]
        mask = jnp.where(place < 0, before, jnp.where(place < Z, own, after))
        block = jnp.where(mask > 0.0, mask * seen[view] / model, 0.0)
        ratio[view] = block
        pack_sides(block, near, far, view)
        near[view, 64:] = marks[view]
        far[view, 64:] = marks[view]


def ratio_back(
    table, band_t, backward_z, ratio, low, high, out_low, out_mid, out_high, planes
):
    @pl.loop(0, V)
    def _(view):
        block = ring(ratio[view].reshape(C * C, Z), low[view, :64], high[view, :64])
        back = dot(block, backward_z[view]).reshape(C, C, Z)
        taps = [table[view, t] for t in range(K)]
        for half in range(2):
            source = [back[i, 8 * half : 8 * half + 8, :] for i in range(C)]
            for a in range(1, W - 1):
                total = None
                for i in range(C):
                    t = a - i - 1
                    if 0 <= t < K:
                        term = taps[t] * source[i]
                        total = term if total is None else total + term
                planes[a, pl.ds(pl.multiple_of(view * C + 8 * half, 8), 8), :] = total

    planes[0] = jnp.zeros((V * C, Z), F32)
    planes[W - 1] = jnp.zeros((V * C, Z), F32)
    for pair in range(W // 2):
        both = jnp.concatenate([planes[2 * pair], planes[2 * pair + 1]], axis=1)
        both = dot(band_t[...], both)
        for part in range(2):
            piece = both[:, part * Z : (part + 1) * Z]
            out_low[2 * pair + part] = piece[:C]
            out_mid[2 * pair + part] = piece[C : 2 * C]
            out_high[2 * pair + part] = piece[2 * C :]


def add_rows(mid, from_low, from_high, out_low, out_mid, out_high):
    has_low, has_high = edges("by")
    total = (
        mid[...]
        + jnp.where(has_low, from_low[...], 0.0)
        + jnp.where(has_high, from_high[...], 0.0)
    )
    out_low[...] = total[:C]
    out_mid[...] = total[C : 2 * C]
    out_high[...] = total[2 * C :]


def part(tap, cell, count, which):
    before = jnp.where(tap > cell + R, 1.0, 0.0)
    after = jnp.where(tap < cell + R + 1 - count, 1.0, 0.0)
    return jnp.where(which == 0, before, jnp.where(which == 2, after, 1.0 - before - after))


def weigh(norm, marks, near_marks, far_marks, weights):
    has_low, has_high = edges("bz")
    tap = lax.broadcasted_iota(jnp.int32, (Z, Z), 0)
    cell = lax.broadcasted_iota(jnp.int32, (Z, Z), 1)
    part_x = [dot(norm[0], part(tap, cell, C, p), HIGHEST) for p in range(3)]
    part_z = [dot(norm[2], part(tap, cell, Z, r), HIGHEST) for r in range(3)]
    part_y = [dot(norm[1], part(tap, cell, C, q), HIGHEST) for q in range(3)]
    part_y = [jnp.concatenate([y] * C, axis=0).T for y in part_y]
    sums = [jnp.zeros((C, Z), F32) for _ in range(C)]
    for view in range(V):
        low = jnp.where(even(), far_marks[view, 0:1], near_marks[view, 0:1])
        high = jnp.where(even(), near_marks[view, 0:1], far_marks[view, 0:1])
        near = [
            jnp.where(has_low, low, 0.0),
            marks[view, 0:1],
            jnp.where(has_high, high, 0.0),
        ]
        share = [
            jnp.broadcast_to(part_y[q][:C, view : view + 1], (C, Z)) for q in range(3)
        ]
        for p in range(3):
            term = None
            for r in range(3):
                level = None
                for q in range(3):
                    at = 3 * q + p
                    cell = jnp.broadcast_to(near[r][:, at : at + 1], (C, Z)) * share[q]
                    level = cell if level is None else level + cell
                level = level * part_z[r][view : view + 1, :]
                term = level if term is None else term + level
            for i in range(C):
                scale = jnp.broadcast_to(part_x[p][view : view + 1, i : i + 1], (C, Z))
                sums[i] = sums[i] + scale * term
    for i in range(C):
        weights[i] = sums[i]


def finish(estimate, mid, from_low, from_high, weights, out):
    has_low, has_high = edges("bx")
    total = (
        mid[...]
        + jnp.where(has_low, from_low[...], 0.0)
        + jnp.where(has_high, from_high[...], 0.0)
    )
    out[...] = estimate[...] * total / weights[...]


def on_device(estimate, raw, psf, offsets, coverage):
    cover = coverage.reshape(V)
    offsets = offsets.T
    full = (V, C, C, Z)

    left = shift(estimate, "bx", 1)
    right = shift(estimate, "bx", -1)
    up, down = call(
        pack_planes,
        [(V, OFF + 1, C, Z)] * 2,
        [HBM, VM],
        [pltpu.SMEM((V,), jnp.int32), pltpu.SemaphoreType.DMA],
        moved=3 << 19,
    )(cover, raw)
    raw_low = shift(up, "bx", 1)
    raw_high = shift(down, "bx", -1)
    (wide,) = call(
        join_planes,
        [(W, C, Z)],
        [VM, HBM, VM],
        [pltpu.SemaphoreType.DMA],
        moved=1 << 18,
    )(left, estimate, right)
    norm, table, band_y, band_t, forward_z, backward_z = call(
        build,
        [
            (3, 8, Z),
            (V, K, 8, Z),
            (V * C, Z),
            (W, V * C),
            (V, 2 * Z, Z),
            (V, 2 * Z, Z),
        ],
        [SM, VM, ANY],
        moved=1 << 23,
    )(offsets, psf, wide)
    low = shift(wide, "by", 1)
    high = shift(wide, "by", -1)

    shifted, up, down, tiles = call(
        shift_planes,
        [
            (V, C, 2 * C, Z),
            (V, C + 1, OFF, Z),
            (V, C + 1, OFF, Z),
            (V, 8, Z),
        ],
        [SM, SM, VM, VM, VM, ANY],
        [pltpu.VMEM((V, 2 * C, C, Z), F32)],
        moved=1 << 26,
    )(offsets, cover, raw, raw_low, raw_high, norm)
    raw_low = shift(up, "by", 1)
    raw_high = shift(down, "by", -1)

    blurred, near, far = call(
        forward,
        [full, (V, 72, Z), (V, 72, Z)],
        [VM] * 5 + [SM, ANY],
        [pltpu.VMEM((W, V * C, Z), F32)],
        flops=1 << 34,
        moved=1 << 26,
    )(table, band_y, wide, low, high, cover, tiles)
    near, far = swap(near, 0), swap(far, 1)

    seen, marks, _ = call(
        shift_rows,
        [full, (V, 8, Z), (V, C, 2 * C, Z)],
        [SM] + [VM] * 4 + [ANY],
        alias={1: 2},
        moved=1 << 26,
    )(offsets, shifted, raw_low, raw_high, tiles, blurred)

    ratio, near, far = call(
        divide,
        [full, (V, 72, Z), (V, 72, Z)],
        [SM, SM] + [VM] * 6,
        flops=1 << 34,
        moved=1 << 26,
    )(offsets, cover, forward_z, blurred, near, far, seen, marks)
    near, far = swap(near, 0), swap(far, 1)

    out_low, out_mid, out_high = call(
        ratio_back,
        [(W, C, Z)] * 3,
        [VM] * 6,
        [pltpu.VMEM((W, V * C, Z), F32)],
        flops=1 << 34,
        moved=8 << 20,
    )(table, band_t, backward_z, ratio, near, far)
    sum_low = shift(out_high, "by", 1)
    sum_high = shift(out_low, "by", -1)
    last = pl.BlockSpec((V, 8, Z), lambda i: (0, 8, 0))
    (weights,) = call(
        weigh, [(C, C, Z)], [VM, VM, last, last], grid=(1,), moved=1 << 19
    )(norm, marks, near, far)
    out_low, out_mid, out_high = call(
        add_rows, [(C, C, Z)] * 3, [VM] * 3, moved=3 << 19
    )(out_mid, sum_low, sum_high)
    sum_low = shift(out_high, "bx", 1)
    sum_high = shift(out_low, "bx", -1)
    (out,) = call(finish, [(C, C, Z)], [VM] * 5, moved=3 << 18)(
        estimate, out_mid, sum_low, sum_high, weights
    )
    return out


def solution(mesh):
    return jax.shard_map(
        on_device,
        mesh=mesh,
        in_specs=(
            P("bx", "by", "bz"),
            P(None, "bx", "by", "bz"),
            P(),
            P(),
            P(None, "bx", "by", "bz"),
        ),
        out_specs=P("bx", "by", "bz"),
        check_vma=False,
    )
```

time: 89.7 us -> 78.3 us (0.87)
  the two profiles are of different devices: /device:TPU:38 before, /device:TPU:6 now
where the time goes in v1:
time: 78.3 us; the launch traced here: 78.1 us
  starting transfers between devices  31.4 us (40%)
  waiting for transfers between devices  27.4 us (35%)
  Pallas kernels  15.8 us (20%)
  local copies, waits for them, and re-layouts  3.42 us (4%)
    ppermute x12, starting transfers between devices, shift(): lax.ppermute(block, axis, [(i, (i + step) % count) for i in range(count)])  24.5 us
    ppermute x12, waiting for transfers between devices, shift(): lax.ppermute(block, axis, [(i, (i + step) % count) for i in range(count)])  18 us
    ppermute x4, waiting for transfers between devices, swap(): return lax.ppermute(block, 'bz', pairs)  9.46 us
    ppermute x4, starting transfers between devices, swap(): return lax.ppermute(block, 'bz', pairs)  6.93 us
    pallas_call x1, Pallas kernels, on_device(): call(ratio_back, [(W, C, Z)] * 3, [VM] * 6, [pltpu.VMEM((W, V * C, Z), F3...  4.06 us
    pallas_call x1, Pallas kernels, on_device(): call(forward, [full, (V, 72, Z), (V, 72, Z)], [VM] * 5 + [SM, ANY], [pltp...  3.94 us
    unnamed x16, local copies, waits for them, and re-layouts  3.42 us
    pallas_call x1, Pallas kernels, on_device(): call(build, [(3, 8, Z), (V, K, 8, Z), (V * C, Z), (W, V * C), (V, 2 * Z,...  1.83 us
  transfers between devices with their start and end apart: 16, of which 7 were waited for; matrix products, arithmetic and copies ran while one was open for 0% of the time, Pallas kernels for 12%

profile of v1, /device:TPU:6, one launch (start us, length us, event | category | flops | bytes accessed | tf_op | source)
XLA Modules:
  0.0 78.1 jit_solution(14169624828459045780)
XLA Ops:
  0.0 0.0 copy-start.7
  0.0 0.8 %collective-permute-start.1 = (f32[16,16,128]{2,1,0:T(8,128)}, f32[16,16,128]{2,1,0:T(8,128)S(1)}, u32[]{:S(2)}, u32[]{:S(2)}) collective-permute-start(f32[16,16,128]{2,1,0:T(8,128)} %estimate.1), channel_id=1, source_target_pairs={{0,224},{32,0},{64,32},{96,64},{128,96},{160,128},{192,160},{224,1... | collective-permute-start | bytes 393224 | tf_op jit(solution)/shard_map/ppermute | solution.py:55
  0.8 3.3 %collective-permute-start = (f32[16,16,128]{2,1,0:T(8,128)}, f32[16,16,128]{2,1,0:T(8,128)S(1)}, u32[]{:S(2)}, u32[]{:S(2)}) collective-permute-start(f32[16,16,128]{2,1,0:T(8,128)} %estimate.1), channel_id=1, source_target_pairs={{0,32},{32,64},{64,96},{96,128},{128,160},{160,192},{192,224},{224... | collective-permute-start | bytes 393224 | tf_op jit(solution)/shard_map/ppermute | solution.py:55
  4.1 0.0 copy-start
  4.1 1.1 %copy-done = f32[6,16,16,128]{3,2,1,0:T(8,128)S(1)} copy-done((f32[6,16,16,128]{3,2,1,0:T(8,128)S(1)}, f32[6,16,16,128]{3,2,1,0:T(8,128)}, u32[]{:S(2)}) %copy-start) | copy-done | bytes 786456
  5.3 0.0 copy-start.6
  5.3 0.7 copy-done.6
  5.9 0.0 copy-start.4
  5.9 0.0 copy-start.1
  5.9 0.6 shard_map.57
  6.5 0.1 collective-permute-start.4
  6.6 2.0 %collective-permute-start.5 = (f32[6,9,16,128]{3,2,1,0:T(8,128)S(1)}, f32[6,9,16,128]{3,2,1,0:T(8,128)S(1)}, u32[]{:S(2)}, u32[]{:S(2)}) collective-permute-start(f32[6,9,16,128]{3,2,1,0:T(8,128)S(1)} %get-tuple-element.37), channel_id=1, source_target_pairs={{0,224},{32,0},{64,32},{96,64},{128,96},{160,128},{192,160},{224,1... | collective-permute-start | bytes 1327112 | tf_op jit(solution)/shard_map/ppermute | solution.py:55
  8.6 0.0 collective-permute-done.1.high
  8.6 0.0 collective-permute-done.low
  8.6 0.0 copy-start.2
  8.6 0.9 %copy-done.2 = f32[16,16,128]{2,1,0:T(8,128)S(1)} copy-done((f32[16,16,128]{2,1,0:T(8,128)S(1)}, f32[16,16,128]{2,1,0:T(8,128)}, u32[]{:S(2)}) %copy-start.2) | copy-done | bytes 131096
  9.5 0.2 shard_map.55.after.own
  9.7 5.9 %collective-permute-start.3 = (f32[48,16,128]{2,1,0:T(8,128)S(1)}, f32[48,16,128]{2,1,0:T(8,128)S(1)}, u32[]{:S(2)}, u32[]{:S(2)}) collective-permute-start(f32[48,16,128]{2,1,0:T(8,128)S(1)} %shard_map.55.after.own), channel_id=1, source_target_pairs={{0,28},{4,0},{8,4},{12,8},{16,12},{20,16},{24,20},{28,24},{1,29},{... | collective-permute-start | bytes 1179656 | tf_op jit(solution)/shard_map/ppermute | solution.py:55
  15.6 0.0 collective-permute-start.2
  15.7 0.0 copy-done.4
  15.7 0.0 copy-start.5
  15.7 0.7 copy-done.5
  16.4 1.8 %shard_map.56 = (f32[3,8,128]{2,1,0:T(8,128)S(1)}, f32[6,31,8,128]{3,2,1,0:T(8,128)S(1)}, f32[96,128]{1,0:T(8,128)S(1)}, f32[48,96]{1,0:T(8,128)S(1)}, f32[6,256...) custom-call(s32[3,6]{1,0:T(4,128)S(1)} %bitcast.2, f32[6,3,31]{2,1,0:T(4,128)S(1)} %copy-done.5, ...), custom_call_target="tpu_custom_call" | custom-call | bytes 8388608 | tf_op jit(solution)/shard_map/pallas_call | solution.py:379
  18.2 0.0 collective-permute-done.4.low
  18.2 1.9 %collective-permute-done.5.high = f32[6,9,16,128]{3,2,1,0:T(8,128)S(1)} collective-permute-done((f32[6,9,16,128]{3,2,1,0:T(8,128)S(1)}, f32[6,9,16,128]{3,2,1,0:T(8,128)S(1)}, u32[]{:S(2)}, u32[]{:S(2)}) %collective-permute-start.5) | collective-permute-done | bytes 442400 | tf_op jit(solution)/shard_map/ppermute | solution.py:55
  20.1 0.0 copy-done.7
  20.1 0.0 copy-done.1
  20.1 0.8 %shard_map.58 = (f32[6,16,32,128]{3,2,1,0:T(8,128)S(1)}, f32[6,17,8,128]{3,2,1,0:T(8,128)S(1)}, f32[6,17,8,128]{3,2,1,0:T(8,128)S(1)}, f32[6,8,128]{2,1,0:T(8,128)S(1)}) custom-call(s32[3,6]{1,0:T(4,128)S(1)} %bitcast.3, s32[6]{0:T(128)S(1)} %bitcast.7, f32[6,16,16,128]{3,2,1,0:T(8,128)S(1)} %copy-done.1, f32[6,9,16,128]{3,2,1,0:T(8,128)S(1)} %collective-permute-done.4.low, ...), custom_call_target="tpu_custom_call" | custom-call | bytes 67108864 | tf_op jit(solution)/shard_map/pallas_call | solution.py:395
  20.9 2.0 %collective-permute-start.8 = (f32[6,17,8,128]{3,2,1,0:T(8,128)S(1)}, f32[6,17,8,128]{3,2,1,0:T(8,128)S(1)}, u32[]{:S(2)}, u32[]{:S(2)}) collective-permute-start(f32[6,17,8,128]{3,2,1,0:T(8,128)S(1)} %get-tuple-element.44), channel_id=1, source_target_pairs={{0,4},{4,8},{8,12},{12,16},{16,20},{20,24},{24,28},{28,0},{1,5},{5... | collective-permute-start | bytes 1253384 | tf_op jit(solution)/shard_map/ppermute | solution.py:55
  22.9 4.0 %collective-permute-start.9 = (f32[6,17,8,128]{3,2,1,0:T(8,128)S(1)}, f32[6,17,8,128]{3,2,1,0:T(8,128)S(1)}, u32[]{:S(2)}, u32[]{:S(2)}) collective-permute-start(f32[6,17,8,128]{3,2,1,0:T(8,128)S(1)} %get-tuple-element.45), channel_id=1, source_target_pairs={{0,28},{4,0},{8,4},{12,8},{16,12},{20,16},{24,20},{28,24},{1,29},{... | collective-permute-start | bytes 1253384 | tf_op jit(solution)/shard_map/ppermute | solution.py:55
  26.9 0.0 collective-permute-done.3.high
  27.0 0.0 collective-permute-done.2.low
  27.0 3.9 %shard_map.59 = (f32[6,16,16,128]{3,2,1,0:T(8,128)S(1)}, f32[6,72,128]{2,1,0:T(8,128)S(1)}, f32[6,72,128]{2,1,0:T(8,128)S(1)}) custom-call(f32[6,31,8,128]{3,2,1,0:T(8,128)S(1)} %get-tuple-element.31.table, f32[96,128]{1,0:T(8,128)S(1)} %get-tuple-element.35.band_y, f32[48,16,128]{2,1,0:T(8,128)S(1)} %shard_map.55.after.own, ...), custom_call_target="tpu_custom_call" | custom-call | flops 17179869184 | bytes 67108864 | tf_op jit(solution)/shard_map/pallas_call | solution.py:410
  30.9 0.1 collective-permute-start.6
  31.0 3.3 %collective-permute-start.7 = (f32[6,72,128]{2,1,0:T(8,128)S(1)}, f32[6,72,128]{2,1,0:T(8,128)S(1)}, u32[]{:S(2)}, u32[]{:S(2)}) collective-permute-start(f32[6,72,128]{2,1,0:T(8,128)S(1)} %get-tuple-element.42), channel_id=1, source_target_pairs={{1,2},{2,1},{3,0},{0,3},{5,6},{6,5},{7,4},{4,7},{9,10},{10,9},{11,... | collective-permute-start | bytes 663560 | tf_op jit(solution)/shard_map/ppermute | solution.py:64
  34.3 1.0 %collective-permute-done.8.low = f32[6,17,8,128]{3,2,1,0:T(8,128)S(1)} collective-permute-done((f32[6,17,8,128]{3,2,1,0:T(8,128)S(1)}, f32[6,17,8,128]{3,2,1,0:T(8,128)S(1)}, u32[]{:S(2)}, u32[]{:S(2)}) %collective-permute-start.8) | collective-permute-done | bytes 417824 | tf_op jit(solution)/shard_map/ppermute | solution.py:55
  35.3 0.0 collective-permute-done.9.high
  35.3 0.8 %shard_map.60 = (f32[6,16,16,128]{3,2,1,0:T(8,128)S(1)}, f32[6,8,128]{2,1,0:T(8,128)S(1)}, f32[6,16,32,128]{3,2,1,0:T(8,128)S(1)}) custom-call(s32[3,6]{1,0:T(4,128)S(1)} %bitcast.4, f32[6,16,32,128]{3,2,1,0:T(8,128)S(1)} %get-tuple-element.43.held, f32[6,17,8,128]{3,2,1,0:T(8,128)S(1)} %collective-permute-done.8.low, ...), custom_call_target="tpu_custom_call", output_to_operand_aliasing={{2}: (1, {})} | custom-call | bytes 67108864 | tf_op jit(solution)/shard_map/pallas_call | solution.py:420
  36.1 0.0 collective-permute-done.6.low
  36.1 3.7 %collective-permute-done.7.high = f32[6,72,128]{2,1,0:T(8,128)S(1)} collective-permute-done((f32[6,72,128]{2,1,0:T(8,128)S(1)}, f32[6,72,128]{2,1,0:T(8,128)S(1)}, u32[]{:S(2)}, u32[]{:S(2)}) %collective-permute-start.7) | collective-permute-done | bytes 221216 | tf_op jit(solution)/shard_map/ppermute | solution.py:64
  39.8 1.6 %shard_map.61 = (f32[6,16,16,128]{3,2,1,0:T(8,128)S(1)}, f32[6,72,128]{2,1,0:T(8,128)S(1)}, f32[6,72,128]{2,1,0:T(8,128)S(1)}) custom-call(s32[3,6]{1,0:T(4,128)S(1)} %bitcast.5, s32[6]{0:T(128)S(1)} %bitcast.9, f32[6,256,128]{2,1,0:T(8,128)S(1)} %get-tuple-element.34.forward_z, f32[6,16,16,128]{3,2,1,0:T(8,128)S(1)} %get-tuple-element.40.after.blurred, ...), custom_call_target="tpu_custom_call" | custom-call | flops 17179869184 | bytes 67108864 | tf_op jit(solution)/shard_map/pallas_call | solution.py:428
  41.4 0.5 collective-permute-start.10
  41.9 3.1 %collective-permute-start.11 = (f32[6,72,128]{2,1,0:T(8,128)S(1)}, f32[6,72,128]{2,1,0:T(8,128)S(1)}, u32[]{:S(2)}, u32[]{:S(2)}) collective-permute-start(f32[6,72,128]{2,1,0:T(8,128)S(1)} %get-tuple-element.50), channel_id=1, source_target_pairs={{1,2},{2,1},{3,0},{0,3},{5,6},{6,5},{7,4},{4,7},{9,10},{10,9},{11,... | collective-permute-start | bytes 663560 | tf_op jit(solution)/shard_map/ppermute | solution.py:64
  44.9 0.0 collective-permute-done.10.low.near_marks
  44.9 5.8 %collective-permute-done.11.high.far_marks = f32[6,72,128]{2,1,0:T(8,128)S(1)} collective-permute-done((f32[6,72,128]{2,1,0:T(8,128)S(1)}, f32[6,72,128]{2,1,0:T(8,128)S(1)}, u32[]{:S(2)}, u32[]{:S(2)}) %collective-permute-start.11) | collective-permute-done | bytes 221216 | tf_op jit(solution)/shard_map/ppermute | solution.py:64
  50.7 4.1 %shard_map.62 = (f32[48,16,128]{2,1,0:T(8,128)S(1)}, f32[48,16,128]{2,1,0:T(8,128)S(1)}, f32[48,16,128]{2,1,0:T(8,128)S(1)}) custom-call(f32[6,31,8,128]{3,2,1,0:T(8,128)S(1)} %get-tuple-element.31.table, f32[48,96]{1,0:T(8,128)S(1)} %get-tuple-element.32.band_t, f32[6,256,128]{2,1,0:T(8,128)S(1)} %get-tuple-element.33.backward_z, ...), custom_call_target="tpu_custom_call" | custom-call | flops 17179869184 | bytes 8388608 | tf_op jit(solution)/shard_map/pallas_call | solution.py:437
  54.8 0.0 copy-start.3
  54.8 0.1 collective-permute-start.12
  54.9 3.2 %collective-permute-start.13 = (f32[48,16,128]{2,1,0:T(8,128)S(1)}, f32[48,16,128]{2,1,0:T(8,128)S(1)}, u32[]{:S(2)}, u32[]{:S(2)}) collective-permute-start(f32[48,16,128]{2,1,0:T(8,128)S(1)} %get-tuple-element.53), channel_id=1, source_target_pairs={{0,28},{4,0},{8,4},{12,8},{16,12},{20,16},{24,20},{28,24},{1,29},{... | collective-permute-start | bytes 1179656 | tf_op jit(solution)/shard_map/ppermute | solution.py:55
  58.1 9.2 %collective-permute-done.12.from_low = f32[48,16,128]{2,1,0:T(8,128)S(1)} collective-permute-done((f32[48,16,128]{2,1,0:T(8,128)S(1)}, f32[48,16,128]{2,1,0:T(8,128)S(1)}, u32[]{:S(2)}, u32[]{:S(2)}) %collective-permute-start.12) | collective-permute-done | bytes 393248 | tf_op jit(solution)/shard_map/ppermute | solution.py:55
  67.3 0.0 collective-permute-done.13.from_high
  67.3 0.1 shard_map.63
  67.4 3.0 %collective-permute-start.14 = (f32[16,16,128]{2,1,0:T(8,128)S(1)}, f32[16,16,128]{2,1,0:T(8,128)S(1)}, u32[]{:S(2)}, u32[]{:S(2)}) collective-permute-start(f32[16,16,128]{2,1,0:T(8,128)S(1)} %get-tuple-element.55), channel_id=1, source_target_pairs={{0,32},{32,64},{64,96},{96,128},{128,160},{160,192},{192,224},{224... | collective-permute-start | bytes 393224 | tf_op jit(solution)/shard_map/ppermute | solution.py:55
  70.4 0.0 collective-permute-start.15
  70.4 1.2 %shard_map.64.weights = f32[16,16,128]{2,1,0:T(8,128)S(1)} custom-call(f32[3,8,128]{2,1,0:T(8,128)S(1)} %get-tuple-element.38.after.norm, f32[6,8,128]{2,1,0:T(8,128)S(1)} %get-tuple-element.47.marks, f32[6,72,128]{2,1,0:T(8,128)S(1)} %collective-permute-done.10.low.near_marks, f32[6,72,128]{2,1,0:T(8,128)S(1)} %collective-permute-done.11.high.far_marks), custom_call_target="tpu_custom_call" | custom-call | bytes 524288 | tf_op jit(solution)/shard_map/pallas_call | solution.py:448
  71.6 1.3 %collective-permute-done.14.from_low = f32[16,16,128]{2,1,0:T(8,128)S(1)} collective-permute-done((f32[16,16,128]{2,1,0:T(8,128)S(1)}, f32[16,16,128]{2,1,0:T(8,128)S(1)}, u32[]{:S(2)}, u32[]{:S(2)}) %collective-permute-start.14) | collective-permute-done | bytes 131104 | tf_op jit(solution)/shard_map/ppermute | solution.py:55
  72.9 4.6 %collective-permute-done.15.from_high = f32[16,16,128]{2,1,0:T(8,128)S(1)} collective-permute-done((f32[16,16,128]{2,1,0:T(8,128)S(1)}, f32[16,16,128]{2,1,0:T(8,128)S(1)}, u32[]{:S(2)}, u32[]{:S(2)}) %collective-permute-start.15) | collective-permute-done | bytes 131104 | tf_op jit(solution)/shard_map/ppermute | solution.py:55
  77.4 0.0 copy-done.3
  77.4 0.7 shard_map.65
Async XLA Ops:
  0.0 20.1 %copy-start.7 = (s32[6,1,1,1]{0,3,2,1:T(1,128)S(1)}, s32[6,1,1,1]{0,3,2,1:T(1,128)}, u32[]{:S(2)}) copy-start(s32[6,1,1,1]{0,3,2,1:T(1,128)} %param.9) | copy-start | bytes 76
  0.0 8.6 %collective-permute-start.1 = (f32[16,16,128]{2,1,0:T(8,128)}, f32[16,16,128]{2,1,0:T(8,128)S(1)}, u32[]{:S(2)}, u32[]{:S(2)}) collective-permute-start(f32[16,16,128]{2,1,0:T(8,128)} %estimate.1), channel_id=1, source_target_pairs={{0,224},{32,0},{64,32},{96,64},{128,96},{160,128},{192,160},{224,1... | collective-permute-start | bytes 393224 | tf_op jit(solution)/shard_map/ppermute | solution.py:55
  0.8 7.8 %collective-permute-start = (f32[16,16,128]{2,1,0:T(8,128)}, f32[16,16,128]{2,1,0:T(8,128)S(1)}, u32[]{:S(2)}, u32[]{:S(2)}) collective-permute-start(f32[16,16,128]{2,1,0:T(8,128)} %estimate.1), channel_id=1, source_target_pairs={{0,32},{32,64},{64,96},{96,128},{128,160},{160,192},{192,224},{224... | collective-permute-start | bytes 393224 | tf_op jit(solution)/shard_map/ppermute | solution.py:55
  4.1 1.1 %copy-start = (f32[6,16,16,128]{3,2,1,0:T(8,128)S(1)}, f32[6,16,16,128]{3,2,1,0:T(8,128)}, u32[]{:S(2)}) copy-start(f32[6,16,16,128]{3,2,1,0:T(8,128)} %raw.3) | copy-start | bytes 2359300
  5.3 0.7 copy-start.6
  5.9 9.7 %copy-start.4 = (s32[6,3]{0,1:T(4,128)S(1)}, s32[6,3]{0,1:T(4,128)}, u32[]{:S(2)}) copy-start(s32[6,3]{0,1:T(4,128)} %param.8) | copy-start | bytes 220
  5.9 14.2 %copy-start.1 = (f32[6,16,16,128]{3,2,1,0:T(8,128)S(1)}, f32[6,16,16,128]{3,2,1,0:T(8,128)}, u32[]{:S(2)}) copy-start(f32[6,16,16,128]{3,2,1,0:T(8,128)} %raw.3) | copy-start | bytes 2359300
  6.5 11.7 %collective-permute-start.4 = (f32[6,9,16,128]{3,2,1,0:T(8,128)S(1)}, f32[6,9,16,128]{3,2,1,0:T(8,128)S(1)}, u32[]{:S(2)}, u32[]{:S(2)}) collective-permute-start(f32[6,9,16,128]{3,2,1,0:T(8,128)S(1)} %get-tuple-element.36), channel_id=1, source_target_pairs={{0,32},{32,64},{64,96},{96,128},{128,160},{160,192},{192,224},{224... | collective-permute-start | bytes 1327112 | tf_op jit(solution)/shard_map/ppermute | solution.py:55
  6.6 13.5 %collective-permute-start.5 = (f32[6,9,16,128]{3,2,1,0:T(8,128)S(1)}, f32[6,9,16,128]{3,2,1,0:T(8,128)S(1)}, u32[]{:S(2)}, u32[]{:S(2)}) collective-permute-start(f32[6,9,16,128]{3,2,1,0:T(8,128)S(1)} %get-tuple-element.37), channel_id=1, source_target_pairs={{0,224},{32,0},{64,32},{96,64},{128,96},{160,128},{192,160},{224,1... | collective-permute-start | bytes 1327112 | tf_op jit(solution)/shard_map/ppermute | solution.py:55
  8.6 0.9 %copy-start.2 = (f32[16,16,128]{2,1,0:T(8,128)S(1)}, f32[16,16,128]{2,1,0:T(8,128)}, u32[]{:S(2)}) copy-start(f32[16,16,128]{2,1,0:T(8,128)} %estimate.1) | copy-start | bytes 393220
  9.7 17.2 %collective-permute-start.3 = (f32[48,16,128]{2,1,0:T(8,128)S(1)}, f32[48,16,128]{2,1,0:T(8,128)S(1)}, u32[]{:S(2)}, u32[]{:S(2)}) collective-permute-start(f32[48,16,128]{2,1,0:T(8,128)S(1)} %shard_map.55.after.own), channel_id=1, source_target_pairs={{0,28},{4,0},{8,4},{12,8},{16,12},{20,16},{24,20},{28,24},{1,29},{... | collective-permute-start | bytes 1179656 | tf_op jit(solution)/shard_map/ppermute | solution.py:55
  15.6 11.3 %collective-permute-start.2 = (f32[48,16,128]{2,1,0:T(8,128)S(1)}, f32[48,16,128]{2,1,0:T(8,128)S(1)}, u32[]{:S(2)}, u32[]{:S(2)}) collective-permute-start(f32[48,16,128]{2,1,0:T(8,128)S(1)} %shard_map.55.after.own), channel_id=1, source_target_pairs={{0,4},{4,8},{8,12},{12,16},{16,20},{20,24},{24,28},{28,0},{1,5},{5... | collective-permute-start | bytes 1179656 | tf_op jit(solution)/shard_map/ppermute | solution.py:55
  15.7 0.7 copy-start.5
  20.9 14.3 %collective-permute-start.8 = (f32[6,17,8,128]{3,2,1,0:T(8,128)S(1)}, f32[6,17,8,128]{3,2,1,0:T(8,128)S(1)}, u32[]{:S(2)}, u32[]{:S(2)}) collective-permute-start(f32[6,17,8,128]{3,2,1,0:T(8,128)S(1)} %get-tuple-element.44), channel_id=1, source_target_pairs={{0,4},{4,8},{8,12},{12,16},{16,20},{20,24},{24,28},{28,0},{1,5},{5... | collective-permute-start | bytes 1253384 | tf_op jit(solution)/shard_map/ppermute | solution.py:55
  22.9 12.3 %collective-permute-start.9 = (f32[6,17,8,128]{3,2,1,0:T(8,128)S(1)}, f32[6,17,8,128]{3,2,1,0:T(8,128)S(1)}, u32[]{:S(2)}, u32[]{:S(2)}) collective-permute-start(f32[6,17,8,128]{3,2,1,0:T(8,128)S(1)} %get-tuple-element.45), channel_id=1, source_target_pairs={{0,28},{4,0},{8,4},{12,8},{16,12},{20,16},{24,20},{28,24},{1,29},{... | collective-permute-start | bytes 1253384 | tf_op jit(solution)/shard_map/ppermute | solution.py:55
  30.9 5.2 %collective-permute-start.6 = (f32[6,72,128]{2,1,0:T(8,128)S(1)}, f32[6,72,128]{2,1,0:T(8,128)S(1)}, u32[]{:S(2)}, u32[]{:S(2)}) collective-permute-start(f32[6,72,128]{2,1,0:T(8,128)S(1)} %get-tuple-element.41), channel_id=1, source_target_pairs={{0,1},{1,0},{2,3},{3,2},{4,5},{5,4},{6,7},{7,6},{8,9},{9,8},{10,11... | collective-permute-start | bytes 663560 | tf_op jit(solution)/shard_map/ppermute | solution.py:64
  31.0 8.8 %collective-permute-start.7 = (f32[6,72,128]{2,1,0:T(8,128)S(1)}, f32[6,72,128]{2,1,0:T(8,128)S(1)}, u32[]{:S(2)}, u32[]{:S(2)}) collective-permute-start(f32[6,72,128]{2,1,0:T(8,128)S(1)} %get-tuple-element.42), channel_id=1, source_target_pairs={{1,2},{2,1},{3,0},{0,3},{5,6},{6,5},{7,4},{4,7},{9,10},{10,9},{11,... | collective-permute-start | bytes 663560 | tf_op jit(solution)/shard_map/ppermute | solution.py:64
  41.4 3.5 %collective-permute-start.10 = (f32[6,72,128]{2,1,0:T(8,128)S(1)}, f32[6,72,128]{2,1,0:T(8,128)S(1)}, u32[]{:S(2)}, u32[]{:S(2)}) collective-permute-start(f32[6,72,128]{2,1,0:T(8,128)S(1)} %get-tuple-element.49), channel_id=1, source_target_pairs={{0,1},{1,0},{2,3},{3,2},{4,5},{5,4},{6,7},{7,6},{8,9},{9,8},{10,11... | collective-permute-start | bytes 663560 | tf_op jit(solution)/shard_map/ppermute | solution.py:64
  41.9 8.8 %collective-permute-start.11 = (f32[6,72,128]{2,1,0:T(8,128)S(1)}, f32[6,72,128]{2,1,0:T(8,128)S(1)}, u32[]{:S(2)}, u32[]{:S(2)}) collective-permute-start(f32[6,72,128]{2,1,0:T(8,128)S(1)} %get-tuple-element.50), channel_id=1, source_target_pairs={{1,2},{2,1},{3,0},{0,3},{5,6},{6,5},{7,4},{4,7},{9,10},{10,9},{11,... | collective-permute-start | bytes 663560 | tf_op jit(solution)/shard_map/ppermute | solution.py:64
  54.8 22.6 %copy-start.3 = (f32[16,16,128]{2,1,0:T(8,128)S(1)}, f32[16,16,128]{2,1,0:T(8,128)}, u32[]{:S(2)}) copy-start(f32[16,16,128]{2,1,0:T(8,128)} %estimate.1) | copy-start | bytes 393220
  54.8 12.5 %collective-permute-start.12 = (f32[48,16,128]{2,1,0:T(8,128)S(1)}, f32[48,16,128]{2,1,0:T(8,128)S(1)}, u32[]{:S(2)}, u32[]{:S(2)}) collective-permute-start(f32[48,16,128]{2,1,0:T(8,128)S(1)} %get-tuple-element.52), channel_id=1, source_target_pairs={{0,4},{4,8},{8,12},{12,16},{16,20},{20,24},{24,28},{28,0},{1,5},{5... | collective-permute-start | bytes 1179656 | tf_op jit(solution)/shard_map/ppermute | solution.py:55
  54.9 12.4 %collective-permute-start.13 = (f32[48,16,128]{2,1,0:T(8,128)S(1)}, f32[48,16,128]{2,1,0:T(8,128)S(1)}, u32[]{:S(2)}, u32[]{:S(2)}) collective-permute-start(f32[48,16,128]{2,1,0:T(8,128)S(1)} %get-tuple-element.53), channel_id=1, source_target_pairs={{0,28},{4,0},{8,4},{12,8},{16,12},{20,16},{24,20},{28,24},{1,29},{... | collective-permute-start | bytes 1179656 | tf_op jit(solution)/shard_map/ppermute | solution.py:55
  67.4 5.5 %collective-permute-start.14 = (f32[16,16,128]{2,1,0:T(8,128)S(1)}, f32[16,16,128]{2,1,0:T(8,128)S(1)}, u32[]{:S(2)}, u32[]{:S(2)}) collective-permute-start(f32[16,16,128]{2,1,0:T(8,128)S(1)} %get-tuple-element.55), channel_id=1, source_target_pairs={{0,32},{32,64},{64,96},{96,128},{128,160},{160,192},{192,224},{224... | collective-permute-start | bytes 393224 | tf_op jit(solution)/shard_map/ppermute | solution.py:55
  70.4 7.1 %collective-permute-start.15 = (f32[16,16,128]{2,1,0:T(8,128)S(1)}, f32[16,16,128]{2,1,0:T(8,128)S(1)}, u32[]{:S(2)}, u32[]{:S(2)}) collective-permute-start(f32[16,16,128]{2,1,0:T(8,128)S(1)} %get-tuple-element.56), channel_id=1, source_target_pairs={{0,224},{32,0},{64,32},{96,64},{128,96},{160,128},{192,160},{224,1... | collective-permute-start | bytes 393224 | tf_op jit(solution)/shard_map/ppermute | solution.py:55

commit v2 on v1

--- a/solution.py
+++ b/solution.py
@@ -15,6 +15,7 @@
 HIGH = lax.Precision.HIGH
 HIGHEST = lax.Precision.HIGHEST
 F32 = jnp.float32
+BF16 = jnp.bfloat16
 
 VM = pl.BlockSpec(memory_space=pltpu.VMEM)
 SM = pl.BlockSpec(memory_space=pltpu.SMEM)
@@ -29,7 +30,9 @@
     return pl.pallas_call(
         body,
         grid=grid,
-        out_shape=[jax.ShapeDtypeStruct(s, F32) for s in outs],
+        out_shape=[
+            s if hasattr(s, "dtype") else jax.ShapeDtypeStruct(s, F32) for s in outs
+        ],
         in_specs=specs,
         out_specs=out_specs or [VM] * len(outs),
         scratch_shapes=list(scratch),
@@ -72,6 +75,11 @@
     return jnp.dot(a, b, precision=precision, preferred_element_type=F32)
 
 
+def split(block):
+    high = block.astype(BF16)
+    return high, (block - high.astype(F32)).astype(BF16)
+
+
 def pack_planes(cover, raw, up, down, flags, sem):
     tag = pltpu.make_async_copy(cover, flags, sem)
     tag.start()
@@ -85,7 +93,8 @@
 
 
 def build(
-    offsets, psf, after, norm, table, band_y, band_t, forward_z, backward_z
+    offsets, psf, after, norm, table, fan_in, fan_out, fan_pair,
+    forward_z, backward_z,
 ):
     norm[...] = jnp.zeros((3, 8, Z), F32)
     for view in range(V):
@@ -94,14 +103,13 @@
             norm[axis, view : view + 1, 0:K] = line / jnp.sum(
                 line, axis=1, keepdims=True
             )
+    bands = []
     for view in range(V):
         line = norm[0, view : view + 1, :]
         for t in range(K):
             table[view, t] = jnp.broadcast_to(line[:, t : t + 1], (8, Z))
         row = jnp.broadcast_to(norm[1, view : view + 1, :], (C, Z))
-        band_y[view * C : (view + 1) * C, :] = pltpu.roll(
-            row, 1, 1, stride=1, stride_axis=0
-        )
+        bands.append(pltpu.roll(row, 1, 1, stride=1, stride_axis=0))
         row = norm[2, view : view + 1, :]
         row = jnp.concatenate([row, jnp.zeros((1, Z), F32)], axis=1)
         row = jnp.broadcast_to(row, (2 * Z, 2 * Z))
@@ -109,7 +117,23 @@
         band = pltpu.roll(band, lax.rem(2 * Z - offsets[2, view], 2 * Z), 1)
         backward_z[view] = band[:, :Z]
         forward_z[view] = band[:Z, :].T
-    band_t[...] = band_y[...].T[:W, :]
+    def side_by_side(*parts):
+        total = None
+        for turn, block in parts:
+            block = block.astype(F32)
+            block = jnp.concatenate([block, jnp.zeros_like(block)], axis=1)
+            block = pltpu.roll(block, turn, 1) if turn else block
+            total = block if total is None else total + block
+        return total.astype(BF16)
+
+    high, low = split(jnp.concatenate(bands, axis=0))
+    fan_in[...] = side_by_side((0, high), (W, high), (2 * W, low))
+    for out, order in ((fan_out, range(V)), (fan_pair, (0, 2, 4, 1, 3, 5))):
+        rows = [bands[v] for v in order]
+        rows += [jnp.zeros((Z - V * C, Z), F32)]
+        high, low = split(jnp.concatenate(rows, axis=0).T[:W, :])
+        out[0:W] = side_by_side((0, high), (V * C, high))
+        out[W:] = side_by_side((0, low), (V * C, low))
 
 
 def join_planes(low, own, high, wide, sem):
@@ -140,9 +164,9 @@
     far[view, :64] = jnp.where(even(), down, up)
 
 
-def forward(table, band_y, own, low, high, cover, after, blurred, near, far, planes):
+def forward(table, fan_in, own, low, high, cover, after, blurred, near, far, planes):
     has_low, has_high = edges("by")
-    band = band_y[:, :W]
+    fan = fan_in[:, : 3 * W]
     for pair in range(W // 2):
         sides = []
         for a in (2 * pair, 2 * pair + 1):
@@ -156,7 +180,8 @@
                     axis=0,
                 )
             )
-        both = dot(band, jnp.concatenate(sides, axis=1))
+        top, rest = split(jnp.concatenate(sides, axis=1))
+        both = dot(fan, jnp.concatenate([top, rest, top], axis=0), None)
         planes[2 * pair] = both[:, :Z]
         planes[2 * pair + 1] = both[:, Z:]
 
@@ -182,19 +207,19 @@
         far[view, 64:] = tile
 
 
-def ring(block, near, far):
+def sides(near, far):
     has_low, has_high = edges("bz")
     lane = lanes(64)
     low = jnp.where(even(), far, near)
     high = jnp.where(even(), near, far)
-    sides = []
+    parts = []
     for group in range(4):
         before = pltpu.roll(low, 96 - 32 * group, 1) if group < 3 else low
         after = pltpu.roll(high, (Z - 32 * group) % Z, 1) if group else high
         before = jnp.where(jnp.logical_and(lane >= 96, has_low), before, 0.0)
         after = jnp.where(jnp.logical_and(lane < 32, has_high), after, 0.0)
-        sides.append(before + after)
-    return jnp.concatenate([block, jnp.concatenate(sides, axis=0)], axis=1)
+        parts.append(before + after)
+    return jnp.concatenate(parts, axis=0)
 
 
 def shift_planes(
@@ -234,14 +259,13 @@
 
 
 def divide(
-    offsets, cover, forward_z, blurred, low, high, seen, marks, ratio, near, far
+    offsets, cover, forward_z, blurred, high, low, seen, marks, ratio, near, far
 ):
     has_low, has_high = edges("bz")
     lane = lanes(1)
     for view in range(V):
-        block = ring(
-            blurred[view].reshape(C * C, Z), low[view, :64], high[view, :64]
-        )
+        block = blurred[view].reshape(C * C, Z)
+        block = jnp.concatenate([block, sides(low[view, :64], high[view, :64])], axis=1)
         model = dot(block, forward_z[view]).reshape(C, C, Z)
         before = jnp.where(even(), high[view, 64:65], low[view, 64:65])
         after = jnp.where(even(), low[view, 64:65], high[view, 64:65])
@@ -257,30 +281,37 @@
         far[view, 64:] = marks[view]
 
 
-def ratio_back(
-    table, band_t, backward_z, ratio, low, high, out_low, out_mid, out_high, planes
+def spread(source, taps, planes, row):
+    for a in range(1, W - 1):
+        total = None
+        for i in range(C):
+            t = a - i - 1
+            if 0 <= t < K:
+                term = taps[t] * source[i]
+                total = term if total is None else total + term
+        planes[a, pl.ds(pl.multiple_of(row, 8), 8), :] = total
+
+
+def back_own(
+    table, fan_out, backward_z, ratio, out_low, out_mid, out_high, planes
 ):
     @pl.loop(0, V)
     def _(view):
-        block = ring(ratio[view].reshape(C * C, Z), low[view, :64], high[view, :64])
-        back = dot(block, backward_z[view]).reshape(C, C, Z)
+        back = dot(ratio[view].reshape(C * C, Z), backward_z[view, :Z])
+        back = back.reshape(C, C, Z)
         taps = [table[view, t] for t in range(K)]
         for half in range(2):
             source = [back[i, 8 * half : 8 * half + 8, :] for i in range(C)]
-            for a in range(1, W - 1):
-                total = None
-                for i in range(C):
-                    t = a - i - 1
-                    if 0 <= t < K:
-                        term = taps[t] * source[i]
-                        total = term if total is None else total + term
-                planes[a, pl.ds(pl.multiple_of(view * C + 8 * half, 8), 8), :] = total
+            spread(source, taps, planes, view * C + 8 * half)
 
     planes[0] = jnp.zeros((V * C, Z), F32)
     planes[W - 1] = jnp.zeros((V * C, Z), F32)
     for pair in range(W // 2):
         both = jnp.concatenate([planes[2 * pair], planes[2 * pair + 1]], axis=1)
-        both = dot(band_t[...], both)
+        both = dot(
+            fan_out[:, : 2 * V * C], jnp.concatenate(split(both), axis=0), None
+        )
+        both = both[:W] + both[W:]
         for part in range(2):
             piece = both[:, part * Z : (part + 1) * Z]
             out_low[2 * pair + part] = piece[:C]
@@ -288,16 +319,79 @@
             out_high[2 * pair + part] = piece[2 * C :]
 
 
-def add_rows(mid, from_low, from_high, out_low, out_mid, out_high):
+def back_rest(
+    table, fan_pair, backward_z, far, near, after, out_low, out_mid, out_high, planes
+):
+    lane = lanes(8)
+    half = lanes(W) < 64
+
+    @pl.loop(0, V // 2)
+    def _(pair):
+        parts = []
+        for odd in range(2):
+            view = 2 * pair + odd
+            block = sides(near[view, :64], far[view, :64])
+            block = dot(block, backward_z[view, Z:])
+            parts.append(pltpu.roll(block, 32 + 64 * odd, 1).reshape(C, C, Z))
+        taps = [
+            jnp.where(lane < 64, table[2 * pair, t], table[2 * pair + 1, t])
+            for t in range(K)
+        ]
+        for half in range(2):
+            rows = slice(8 * half, 8 * half + 8)
+            source = [
+                jnp.where(lane < 64, parts[0][i, rows], parts[1][i, rows])
+                for i in range(C)
+            ]
+            spread(source, taps, planes, pair * C + 8 * half)
+
+    planes[0] = jnp.zeros((W, Z), F32)
+    planes[W - 1] = jnp.zeros((W, Z), F32)
+    def fold(a):
+        first, second = planes[a], planes[a + 1]
+        turned, other = pltpu.roll(first, 64, 1), pltpu.roll(second, 64, 1)
+        even_rows = jnp.where(half, first, other)
+        odd_rows = jnp.where(half, turned, second)
+        return jnp.concatenate([even_rows, odd_rows], axis=0)
+
+    for quad in range(W // 4):
+        both = jnp.concatenate([fold(4 * quad), fold(4 * quad + 2)], axis=1)
+        both = dot(
+            fan_pair[:, : 2 * V * C], jnp.concatenate(split(both), axis=0), None
+        )
+        both = both[:W] + both[W:]
+        for part in range(2):
+            piece = both[:, part * Z : (part + 1) * Z]
+            out_low[2 * quad + part] = piece[:C]
+            out_mid[2 * quad + part] = piece[C : 2 * C]
+            out_high[2 * quad + part] = piece[2 * C :]
+
+
+def add_rows(
+    mid, from_low, from_high, rest, rest_low, rest_high, out_low, out_mid, out_high
+):
     has_low, has_high = edges("by")
-    total = (
-        mid[...]
-        + jnp.where(has_low, from_low[...], 0.0)
-        + jnp.where(has_high, from_high[...], 0.0)
-    )
-    out_low[...] = total[:C]
-    out_mid[...] = total[C : 2 * C]
-    out_high[...] = total[2 * C :]
+    lane = lanes(C)
+    ends = jnp.logical_or(lane < 32, lane >= 96)
+    for a in range(W):
+        total = (
+            mid[a]
+            + jnp.where(has_low, from_low[a], 0.0)
+            + jnp.where(has_high, from_high[a], 0.0)
+        )
+        more = (
+            rest[a // 2]
+            + jnp.where(has_low, rest_low[a // 2], 0.0)
+            + jnp.where(has_high, rest_high[a // 2], 0.0)
+        )
+        more = pltpu.roll(more, 32 if a % 2 else 96, 1)
+        total = total + jnp.where(ends, more, 0.0)
+        if a < C:
+            out_low[a] = total
+        elif a < 2 * C:
+            out_mid[a - C] = total
+        else:
+            out_high[a - 2 * C] = total
 
 
 def part(tap, cell, count, which):
@@ -376,13 +470,14 @@
         [pltpu.SemaphoreType.DMA],
         moved=1 << 18,
     )(left, estimate, right)
-    norm, table, band_y, band_t, forward_z, backward_z = call(
+    norm, table, fan_in, fan_out, fan_pair, forward_z, backward_z = call(
         build,
         [
             (3, 8, Z),
             (V, K, 8, Z),
-            (V * C, Z),
-            (W, V * C),
+            jax.ShapeDtypeStruct((V * C, 2 * Z), BF16),
+            jax.ShapeDtypeStruct((2 * W, 2 * Z), BF16),
+            jax.ShapeDtypeStruct((2 * W, 2 * Z), BF16),
             (V, 2 * Z, Z),
             (V, 2 * Z, Z),
         ],
@@ -414,8 +509,8 @@
         [pltpu.VMEM((W, V * C, Z), F32)],
         flops=1 << 34,
         moved=1 << 26,
-    )(table, band_y, wide, low, high, cover, tiles)
-    near, far = swap(near, 0), swap(far, 1)
+    )(table, fan_in, wide, low, high, cover, tiles)
+    far, near = swap(far, 1), swap(near, 0)
 
     seen, marks, _ = call(
         shift_rows,
@@ -431,26 +526,36 @@
         [SM, SM] + [VM] * 6,
         flops=1 << 34,
         moved=1 << 26,
-    )(offsets, cover, forward_z, blurred, near, far, seen, marks)
-    near, far = swap(near, 0), swap(far, 1)
+    )(offsets, cover, forward_z, blurred, far, near, seen, marks)
+    far, near = swap(far, 1), swap(near, 0)
 
     out_low, out_mid, out_high = call(
-        ratio_back,
+        back_own,
         [(W, C, Z)] * 3,
-        [VM] * 6,
+        [VM] * 4,
         [pltpu.VMEM((W, V * C, Z), F32)],
         flops=1 << 34,
-        moved=8 << 20,
-    )(table, band_t, backward_z, ratio, near, far)
+        moved=1 << 26,
+    )(table, fan_out, backward_z, ratio)
     sum_low = shift(out_high, "by", 1)
     sum_high = shift(out_low, "by", -1)
+    rest_low, rest_mid, rest_high = call(
+        back_rest,
+        [(W // 2, C, Z)] * 3,
+        [VM] * 5 + [ANY],
+        [pltpu.VMEM((W, W, Z), F32)],
+        flops=1 << 34,
+        moved=1 << 26,
+    )(table, fan_pair, backward_z, far, near, out_mid)
+    more_low = shift(rest_high, "by", 1)
+    more_high = shift(rest_low, "by", -1)
     last = pl.BlockSpec((V, 8, Z), lambda i: (0, 8, 0))
     (weights,) = call(
         weigh, [(C, C, Z)], [VM, VM, last, last], grid=(1,), moved=1 << 19
     )(norm, marks, near, far)
     out_low, out_mid, out_high = call(
-        add_rows, [(C, C, Z)] * 3, [VM] * 3, moved=3 << 19
-    )(out_mid, sum_low, sum_high)
+        add_rows, [(C, C, Z)] * 3, [VM] * 6, moved=3 << 19
+    )(out_mid, sum_low, sum_high, rest_mid, more_low, more_high)
     sum_low = shift(out_high, "bx", 1)
     sum_high = shift(out_low, "bx", -1)
     (out,) = call(finish, [(C, C, Z)], [VM] * 5, moved=3 << 18)(

time: 78.3 us -> 73.1 us (0.934)
  the two profiles are of different devices: /device:TPU:6 before, /device:TPU:14 now
where the time goes in v2:
time: 73.1 us; the launch traced here: 73 us
  starting transfers between devices  31.7 us (43%)
  waiting for transfers between devices  20.2 us (28%)
  Pallas kernels  17.5 us (24%)
  local copies, waits for them, and re-layouts  3.41 us (5%)
    ppermute x14, starting transfers between devices, shift(): lax.ppermute(block, axis, [(i, (i + step) % count) for i in range(count)])  27.8 us
    ppermute x14, waiting for transfers between devices, shift(): lax.ppermute(block, axis, [(i, (i + step) % count) for i in range(count)])  16.5 us
    ppermute x4, starting transfers between devices, swap(): return lax.ppermute(block, 'bz', pairs)  3.91 us
    ppermute x4, waiting for transfers between devices, swap(): return lax.ppermute(block, 'bz', pairs)  3.74 us
    unnamed x16, local copies, waits for them, and re-layouts  3.41 us
    pallas_call x1, Pallas kernels, on_device(): call(back_own, [(W, C, Z)] * 3, [VM] * 4, [pltpu.VMEM((W, V * C, Z), F32)...  3.4 us
    pallas_call x1, Pallas kernels, on_device(): call(forward, [full, (V, 72, Z), (V, 72, Z)], [VM] * 5 + [SM, ANY], [pltp...  3.36 us
    pallas_call x1, Pallas kernels, on_device(): call(back_rest, [(W // 2, C, Z)] * 3, [VM] * 5 + [ANY], [pltpu.VMEM((W, W...  2.73 us
  transfers between devices with their start and end apart: 18, of which 8 were waited for; matrix products, arithmetic and copies ran while one was open for 0% of the time, Pallas kernels for 21%

profile of v2, /device:TPU:14, one launch (start us, length us, event | category | flops | bytes accessed | tf_op | source)
XLA Modules:
  0.0 73.0 jit_solution(15837408979777099769)
XLA Ops:
  0.0 0.0 copy-start.7
  0.0 0.8 %collective-permute-start.1 = (f32[16,16,128]{2,1,0:T(8,128)}, f32[16,16,128]{2,1,0:T(8,128)S(1)}, u32[]{:S(2)}, u32[]{:S(2)}) collective-permute-start(f32[16,16,128]{2,1,0:T(8,128)} %estimate.1), channel_id=1, source_target_pairs={{0,224},{32,0},{64,32},{96,64},{128,96},{160,128},{192,160},{224,1... | collective-permute-start | bytes 393224 | tf_op jit(solution)/shard_map/ppermute | solution.py:58
  0.8 3.3 %collective-permute-start = (f32[16,16,128]{2,1,0:T(8,128)}, f32[16,16,128]{2,1,0:T(8,128)S(1)}, u32[]{:S(2)}, u32[]{:S(2)}) collective-permute-start(f32[16,16,128]{2,1,0:T(8,128)} %estimate.1), channel_id=1, source_target_pairs={{0,32},{32,64},{64,96},{96,128},{128,160},{160,192},{192,224},{224... | collective-permute-start | bytes 393224 | tf_op jit(solution)/shard_map/ppermute | solution.py:58
  4.1 0.0 copy-start
  4.1 1.1 %copy-done = f32[6,16,16,128]{3,2,1,0:T(8,128)S(1)} copy-done((f32[6,16,16,128]{3,2,1,0:T(8,128)S(1)}, f32[6,16,16,128]{3,2,1,0:T(8,128)}, u32[]{:S(2)}) %copy-start) | copy-done | bytes 786456
  5.3 0.0 copy-start.6
  5.3 0.7 copy-done.6
  5.9 0.0 copy-start.4
  5.9 0.0 copy-start.1
  5.9 0.6 shard_map.57
  6.5 0.1 collective-permute-start.4
  6.6 2.0 %collective-permute-start.5 = (f32[6,9,16,128]{3,2,1,0:T(8,128)S(1)}, f32[6,9,16,128]{3,2,1,0:T(8,128)S(1)}, u32[]{:S(2)}, u32[]{:S(2)}) collective-permute-start(f32[6,9,16,128]{3,2,1,0:T(8,128)S(1)} %get-tuple-element.41), channel_id=1, source_target_pairs={{0,224},{32,0},{64,32},{96,64},{128,96},{160,128},{192,160},{224,1... | collective-permute-start | bytes 1327112 | tf_op jit(solution)/shard_map/ppermute | solution.py:58
  8.6 0.0 collective-permute-done.1.high
  8.6 0.0 collective-permute-done.low
  8.6 0.0 copy-start.2
  8.6 0.9 %copy-done.2 = f32[16,16,128]{2,1,0:T(8,128)S(1)} copy-done((f32[16,16,128]{2,1,0:T(8,128)S(1)}, f32[16,16,128]{2,1,0:T(8,128)}, u32[]{:S(2)}) %copy-start.2) | copy-done | bytes 131096
  9.5 0.2 shard_map.55.after.own
  9.7 5.9 %collective-permute-start.3 = (f32[48,16,128]{2,1,0:T(8,128)S(1)}, f32[48,16,128]{2,1,0:T(8,128)S(1)}, u32[]{:S(2)}, u32[]{:S(2)}) collective-permute-start(f32[48,16,128]{2,1,0:T(8,128)S(1)} %shard_map.55.after.own), channel_id=1, source_target_pairs={{0,28},{4,0},{8,4},{12,8},{16,12},{20,16},{24,20},{28,24},{1,29},{... | collective-permute-start | bytes 1179656 | tf_op jit(solution)/shard_map/ppermute | solution.py:58
  15.6 0.0 collective-permute-start.2
  15.7 0.0 copy-done.4
  15.7 0.0 copy-start.5
  15.7 0.7 copy-done.5
  16.4 1.9 %shard_map.56 = (f32[3,8,128]{2,1,0:T(8,128)S(1)}, f32[6,31,8,128]{3,2,1,0:T(8,128)S(1)}, bf16[96,256]{1,0:T(8,128)(2,1)S(1)}, bf16[96,256]{1,0:T(8,128)(2,1)S(1...) custom-call(s32[3,6]{1,0:T(4,128)S(1)} %bitcast.2, ...), custom_call_target="tpu_custom_call" | custom-call | bytes 8388608 | tf_op jit(solution)/shard_map/pallas_call | solution.py:473
  18.3 0.0 collective-permute-done.4.low
  18.3 1.8 %collective-permute-done.5.high = f32[6,9,16,128]{3,2,1,0:T(8,128)S(1)} collective-permute-done((f32[6,9,16,128]{3,2,1,0:T(8,128)S(1)}, f32[6,9,16,128]{3,2,1,0:T(8,128)S(1)}, u32[]{:S(2)}, u32[]{:S(2)}) %collective-permute-start.5) | collective-permute-done | bytes 442400 | tf_op jit(solution)/shard_map/ppermute | solution.py:58
  20.1 0.0 copy-done.7
  20.1 0.0 copy-done.1
  20.1 0.8 %shard_map.58 = (f32[6,16,32,128]{3,2,1,0:T(8,128)S(1)}, f32[6,17,8,128]{3,2,1,0:T(8,128)S(1)}, f32[6,17,8,128]{3,2,1,0:T(8,128)S(1)}, f32[6,8,128]{2,1,0:T(8,128)S(1)}) custom-call(s32[3,6]{1,0:T(4,128)S(1)} %bitcast.3, s32[6]{0:T(128)S(1)} %bitcast.7, f32[6,16,16,128]{3,2,1,0:T(8,128)S(1)} %copy-done.1, f32[6,9,16,128]{3,2,1,0:T(8,128)S(1)} %collective-permute-done.4.low, ...), custom_call_target="tpu_custom_call" | custom-call | bytes 67108864 | tf_op jit(solution)/shard_map/pallas_call | solution.py:490
  20.9 2.0 %collective-permute-start.8 = (f32[6,17,8,128]{3,2,1,0:T(8,128)S(1)}, f32[6,17,8,128]{3,2,1,0:T(8,128)S(1)}, u32[]{:S(2)}, u32[]{:S(2)}) collective-permute-start(f32[6,17,8,128]{3,2,1,0:T(8,128)S(1)} %get-tuple-element.48), channel_id=1, source_target_pairs={{0,4},{4,8},{8,12},{12,16},{16,20},{20,24},{24,28},{28,0},{1,5},{5... | collective-permute-start | bytes 1253384 | tf_op jit(solution)/shard_map/ppermute | solution.py:58
  22.9 4.0 %collective-permute-start.9 = (f32[6,17,8,128]{3,2,1,0:T(8,128)S(1)}, f32[6,17,8,128]{3,2,1,0:T(8,128)S(1)}, u32[]{:S(2)}, u32[]{:S(2)}) collective-permute-start(f32[6,17,8,128]{3,2,1,0:T(8,128)S(1)} %get-tuple-element.49), channel_id=1, source_target_pairs={{0,28},{4,0},{8,4},{12,8},{16,12},{20,16},{24,20},{28,24},{1,29},{... | collective-permute-start | bytes 1253384 | tf_op jit(solution)/shard_map/ppermute | solution.py:58
  26.9 0.0 collective-permute-done.3.high
  27.0 0.0 collective-permute-done.2.low
  27.0 3.4 %shard_map.59 = (f32[6,16,16,128]{3,2,1,0:T(8,128)S(1)}, f32[6,72,128]{2,1,0:T(8,128)S(1)}, f32[6,72,128]{2,1,0:T(8,128)S(1)}) custom-call(f32[6,31,8,128]{3,2,1,0:T(8,128)S(1)} %get-tuple-element.35.table, bf16[96,256]{1,0:T(8,128)(2,1)S(1)} %get-tuple-element.39.fan_in, f32[48,16,128]{2,1,0:T(8,128)S(1)} %shard_map.55.after.own, ...), custom_call_target="tpu_custom_call" | custom-call | flops 17179869184 | bytes 67108864 | tf_op jit(solution)/shard_map/pallas_call | solution.py:505
  30.3 0.1 collective-permute-start.6
  30.4 2.4 %collective-permute-start.7 = (f32[6,72,128]{2,1,0:T(8,128)S(1)}, f32[6,72,128]{2,1,0:T(8,128)S(1)}, u32[]{:S(2)}, u32[]{:S(2)}) collective-permute-start(f32[6,72,128]{2,1,0:T(8,128)S(1)} %get-tuple-element.46), channel_id=1, source_target_pairs={{0,1},{1,0},{2,3},{3,2},{4,5},{5,4},{6,7},{7,6},{8,9},{9,8},{10,11... | collective-permute-start | bytes 663560 | tf_op jit(solution)/shard_map/ppermute | solution.py:67
  32.8 2.5 %collective-permute-done.8.low = f32[6,17,8,128]{3,2,1,0:T(8,128)S(1)} collective-permute-done((f32[6,17,8,128]{3,2,1,0:T(8,128)S(1)}, f32[6,17,8,128]{3,2,1,0:T(8,128)S(1)}, u32[]{:S(2)}, u32[]{:S(2)}) %collective-permute-start.8) | collective-permute-done | bytes 417824 | tf_op jit(solution)/shard_map/ppermute | solution.py:58
  35.3 0.0 collective-permute-done.9.high
  35.3 0.8 %shard_map.60 = (f32[6,16,16,128]{3,2,1,0:T(8,128)S(1)}, f32[6,8,128]{2,1,0:T(8,128)S(1)}, f32[6,16,32,128]{3,2,1,0:T(8,128)S(1)}) custom-call(s32[3,6]{1,0:T(4,128)S(1)} %bitcast.4, f32[6,16,32,128]{3,2,1,0:T(8,128)S(1)} %get-tuple-element.47.held, f32[6,17,8,128]{3,2,1,0:T(8,128)S(1)} %collective-permute-done.8.low, ...), custom_call_target="tpu_custom_call", output_to_operand_aliasing={{2}: (1, {})} | custom-call | bytes 67108864 | tf_op jit(solution)/shard_map/pallas_call | solution.py:515
  36.1 2.9 %collective-permute-done.6.high = f32[6,72,128]{2,1,0:T(8,128)S(1)} collective-permute-done((f32[6,72,128]{2,1,0:T(8,128)S(1)}, f32[6,72,128]{2,1,0:T(8,128)S(1)}, u32[]{:S(2)}, u32[]{:S(2)}) %collective-permute-start.6) | collective-permute-done | bytes 221216 | tf_op jit(solution)/shard_map/ppermute | solution.py:67
  39.0 0.0 collective-permute-done.7.low
  39.0 1.6 %shard_map.61 = (f32[6,16,16,128]{3,2,1,0:T(8,128)S(1)}, f32[6,72,128]{2,1,0:T(8,128)S(1)}, f32[6,72,128]{2,1,0:T(8,128)S(1)}) custom-call(s32[3,6]{1,0:T(4,128)S(1)} %bitcast.5, s32[6]{0:T(128)S(1)} %bitcast.9, f32[6,256,128]{2,1,0:T(8,128)S(1)} %get-tuple-element.38.forward_z, f32[6,16,16,128]{3,2,1,0:T(8,128)S(1)} %get-tuple-element.44.after.blurred, ...), custom_call_target="tpu_custom_call" | custom-call | flops 17179869184 | bytes 67108864 | tf_op jit(solution)/shard_map/pallas_call | solution.py:523
  40.6 0.1 collective-permute-start.12
  40.7 1.3 %collective-permute-start.13 = (f32[6,72,128]{2,1,0:T(8,128)S(1)}, f32[6,72,128]{2,1,0:T(8,128)S(1)}, u32[]{:S(2)}, u32[]{:S(2)}) collective-permute-start(f32[6,72,128]{2,1,0:T(8,128)S(1)} %get-tuple-element.58), channel_id=1, source_target_pairs={{0,1},{1,0},{2,3},{3,2},{4,5},{5,4},{6,7},{7,6},{8,9},{9,8},{10,11... | collective-permute-start | bytes 663560 | tf_op jit(solution)/shard_map/ppermute | solution.py:67
  42.1 3.4 %shard_map.62 = (f32[48,16,128]{2,1,0:T(8,128)S(1)}, f32[48,16,128]{2,1,0:T(8,128)S(1)}, f32[48,16,128]{2,1,0:T(8,128)S(1)}) custom-call(f32[6,31,8,128]{3,2,1,0:T(8,128)S(1)} %get-tuple-element.35.table, bf16[96,256]{1,0:T(8,128)(2,1)S(1)} %get-tuple-element.36.fan_out, f32[6,256,128]{2,1,0:T(8,128)S(1)} %get-tuple-element.37.backward_z, ...), custom_call_target="tpu_custom_call" | custom-call | flops 17179869184 | bytes 67108864 | tf_op jit(solution)/shard_map/pallas_call | solution.py:532
  45.5 0.1 collective-permute-start.10
  45.6 3.2 %collective-permute-start.11 = (f32[48,16,128]{2,1,0:T(8,128)S(1)}, f32[48,16,128]{2,1,0:T(8,128)S(1)}, u32[]{:S(2)}, u32[]{:S(2)}) collective-permute-start(f32[48,16,128]{2,1,0:T(8,128)S(1)} %get-tuple-element.55), channel_id=1, source_target_pairs={{0,28},{4,0},{8,4},{12,8},{16,12},{20,16},{24,20},{28,24},{1,29},{... | collective-permute-start | bytes 1179656 | tf_op jit(solution)/shard_map/ppermute | solution.py:58
  48.8 0.8 %collective-permute-done.12.far.far_marks = f32[6,72,128]{2,1,0:T(8,128)S(1)} collective-permute-done((f32[6,72,128]{2,1,0:T(8,128)S(1)}, f32[6,72,128]{2,1,0:T(8,128)S(1)}, u32[]{:S(2)}, u32[]{:S(2)}) %collective-permute-start.12) | collective-permute-done | bytes 221216 | tf_op jit(solution)/shard_map/ppermute | solution.py:67
  49.6 0.0 collective-permute-done.13.near.near_marks
  49.6 2.7 %shard_map.63 = (f32[24,16,128]{2,1,0:T(8,128)S(1)}, f32[24,16,128]{2,1,0:T(8,128)S(1)}, f32[24,16,128]{2,1,0:T(8,128)S(1)}) custom-call(f32[6,31,8,128]{3,2,1,0:T(8,128)S(1)} %get-tuple-element.35.table, bf16[96,256]{1,0:T(8,128)(2,1)S(1)} %get-tuple-element.56.fan_pair, f32[6,256,128]{2,1,0:T(8,128)S(1)} %get-tuple-element.37.backward_z, ...), custom_call_target="tpu_custom_call" | custom-call | flops 17179869184 | bytes 67108864 | tf_op jit(solution)/shard_map/pallas_call | solution.py:542
  52.4 0.0 copy-start.3
  52.4 0.1 collective-permute-start.14
  52.5 3.2 %collective-permute-start.15 = (f32[24,16,128]{2,1,0:T(8,128)S(1)}, f32[24,16,128]{2,1,0:T(8,128)S(1)}, u32[]{:S(2)}, u32[]{:S(2)}) collective-permute-start(f32[24,16,128]{2,1,0:T(8,128)S(1)} %get-tuple-element.61), channel_id=1, source_target_pairs={{0,28},{4,0},{8,4},{12,8},{16,12},{20,16},{24,20},{28,24},{1,29},{... | collective-permute-start | bytes 589832 | tf_op jit(solution)/shard_map/ppermute | solution.py:58
  55.7 3.1 %collective-permute-done.10.from_low = f32[48,16,128]{2,1,0:T(8,128)S(1)} collective-permute-done((f32[48,16,128]{2,1,0:T(8,128)S(1)}, f32[48,16,128]{2,1,0:T(8,128)S(1)}, u32[]{:S(2)}, u32[]{:S(2)}) %collective-permute-start.10) | collective-permute-done | bytes 393248 | tf_op jit(solution)/shard_map/ppermute | solution.py:58
  58.8 0.0 collective-permute-done.11.from_high
  58.8 3.2 %collective-permute-done.14.rest_low = f32[24,16,128]{2,1,0:T(8,128)S(1)} collective-permute-done((f32[24,16,128]{2,1,0:T(8,128)S(1)}, f32[24,16,128]{2,1,0:T(8,128)S(1)}, u32[]{:S(2)}, u32[]{:S(2)}) %collective-permute-start.14) | collective-permute-done | bytes 196640 | tf_op jit(solution)/shard_map/ppermute | solution.py:58
  62.0 0.0 collective-permute-done.15.rest_high
  62.0 0.2 shard_map.64
  62.2 3.0 %collective-permute-start.16 = (f32[16,16,128]{2,1,0:T(8,128)S(1)}, f32[16,16,128]{2,1,0:T(8,128)S(1)}, u32[]{:S(2)}, u32[]{:S(2)}) collective-permute-start(f32[16,16,128]{2,1,0:T(8,128)S(1)} %get-tuple-element.63), channel_id=1, source_target_pairs={{0,32},{32,64},{64,96},{96,128},{128,160},{160,192},{192,224},{224... | collective-permute-start | bytes 393224 | tf_op jit(solution)/shard_map/ppermute | solution.py:58
  65.2 0.0 collective-permute-start.17
  65.2 1.2 %shard_map.65.weights = f32[16,16,128]{2,1,0:T(8,128)S(1)} custom-call(f32[3,8,128]{2,1,0:T(8,128)S(1)} %get-tuple-element.42.after.norm, f32[6,8,128]{2,1,0:T(8,128)S(1)} %get-tuple-element.51.marks, f32[6,72,128]{2,1,0:T(8,128)S(1)} %collective-permute-done.13.near.near_marks, f32[6,72,128]{2,1,0:T(8,128)S(1)} %collective-permute-done.12.far.far_marks), custom_call_target="tpu_custom_call" | custom-call | bytes 524288 | tf_op jit(solution)/shard_map/pallas_call | solution.py:553
  66.4 1.3 %collective-permute-done.16.from_low = f32[16,16,128]{2,1,0:T(8,128)S(1)} collective-permute-done((f32[16,16,128]{2,1,0:T(8,128)S(1)}, f32[16,16,128]{2,1,0:T(8,128)S(1)}, u32[]{:S(2)}, u32[]{:S(2)}) %collective-permute-start.16) | collective-permute-done | bytes 131104 | tf_op jit(solution)/shard_map/ppermute | solution.py:58
  67.7 4.6 %collective-permute-done.17.from_high = f32[16,16,128]{2,1,0:T(8,128)S(1)} collective-permute-done((f32[16,16,128]{2,1,0:T(8,128)S(1)}, f32[16,16,128]{2,1,0:T(8,128)S(1)}, u32[]{:S(2)}, u32[]{:S(2)}) %collective-permute-start.17) | collective-permute-done | bytes 131104 | tf_op jit(solution)/shard_map/ppermute | solution.py:58
  72.3 0.0 copy-done.3
  72.3 0.7 shard_map.66
Async XLA Ops:
  0.0 20.1 %copy-start.7 = (s32[6,1,1,1]{0,3,2,1:T(1,128)S(1)}, s32[6,1,1,1]{0,3,2,1:T(1,128)}, u32[]{:S(2)}) copy-start(s32[6,1,1,1]{0,3,2,1:T(1,128)} %param.9) | copy-start | bytes 76
  0.0 8.6 %collective-permute-start.1 = (f32[16,16,128]{2,1,0:T(8,128)}, f32[16,16,128]{2,1,0:T(8,128)S(1)}, u32[]{:S(2)}, u32[]{:S(2)}) collective-permute-start(f32[16,16,128]{2,1,0:T(8,128)} %estimate.1), channel_id=1, source_target_pairs={{0,224},{32,0},{64,32},{96,64},{128,96},{160,128},{192,160},{224,1... | collective-permute-start | bytes 393224 | tf_op jit(solution)/shard_map/ppermute | solution.py:58
  0.8 7.8 %collective-permute-start = (f32[16,16,128]{2,1,0:T(8,128)}, f32[16,16,128]{2,1,0:T(8,128)S(1)}, u32[]{:S(2)}, u32[]{:S(2)}) collective-permute-start(f32[16,16,128]{2,1,0:T(8,128)} %estimate.1), channel_id=1, source_target_pairs={{0,32},{32,64},{64,96},{96,128},{128,160},{160,192},{192,224},{224... | collective-permute-start | bytes 393224 | tf_op jit(solution)/shard_map/ppermute | solution.py:58
  4.1 1.1 %copy-start = (f32[6,16,16,128]{3,2,1,0:T(8,128)S(1)}, f32[6,16,16,128]{3,2,1,0:T(8,128)}, u32[]{:S(2)}) copy-start(f32[6,16,16,128]{3,2,1,0:T(8,128)} %raw.3) | copy-start | bytes 2359300
  5.3 0.7 copy-start.6
  5.9 9.7 %copy-start.4 = (s32[6,3]{0,1:T(4,128)S(1)}, s32[6,3]{0,1:T(4,128)}, u32[]{:S(2)}) copy-start(s32[6,3]{0,1:T(4,128)} %param.8) | copy-start | bytes 220
  5.9 14.2 %copy-start.1 = (f32[6,16,16,128]{3,2,1,0:T(8,128)S(1)}, f32[6,16,16,128]{3,2,1,0:T(8,128)}, u32[]{:S(2)}) copy-start(f32[6,16,16,128]{3,2,1,0:T(8,128)} %raw.3) | copy-start | bytes 2359300
  6.5 11.8 %collective-permute-start.4 = (f32[6,9,16,128]{3,2,1,0:T(8,128)S(1)}, f32[6,9,16,128]{3,2,1,0:T(8,128)S(1)}, u32[]{:S(2)}, u32[]{:S(2)}) collective-permute-start(f32[6,9,16,128]{3,2,1,0:T(8,128)S(1)} %get-tuple-element.40), channel_id=1, source_target_pairs={{0,32},{32,64},{64,96},{96,128},{128,160},{160,192},{192,224},{224... | collective-permute-start | bytes 1327112 | tf_op jit(solution)/shard_map/ppermute | solution.py:58
  6.6 13.5 %collective-permute-start.5 = (f32[6,9,16,128]{3,2,1,0:T(8,128)S(1)}, f32[6,9,16,128]{3,2,1,0:T(8,128)S(1)}, u32[]{:S(2)}, u32[]{:S(2)}) collective-permute-start(f32[6,9,16,128]{3,2,1,0:T(8,128)S(1)} %get-tuple-element.41), channel_id=1, source_target_pairs={{0,224},{32,0},{64,32},{96,64},{128,96},{160,128},{192,160},{224,1... | collective-permute-start | bytes 1327112 | tf_op jit(solution)/shard_map/ppermute | solution.py:58
  8.6 0.9 %copy-start.2 = (f32[16,16,128]{2,1,0:T(8,128)S(1)}, f32[16,16,128]{2,1,0:T(8,128)}, u32[]{:S(2)}) copy-start(f32[16,16,128]{2,1,0:T(8,128)} %estimate.1) | copy-start | bytes 393220
  9.7 17.2 %collective-permute-start.3 = (f32[48,16,128]{2,1,0:T(8,128)S(1)}, f32[48,16,128]{2,1,0:T(8,128)S(1)}, u32[]{:S(2)}, u32[]{:S(2)}) collective-permute-start(f32[48,16,128]{2,1,0:T(8,128)S(1)} %shard_map.55.after.own), channel_id=1, source_target_pairs={{0,28},{4,0},{8,4},{12,8},{16,12},{20,16},{24,20},{28,24},{1,29},{... | collective-permute-start | bytes 1179656 | tf_op jit(solution)/shard_map/ppermute | solution.py:58
  15.6 11.3 %collective-permute-start.2 = (f32[48,16,128]{2,1,0:T(8,128)S(1)}, f32[48,16,128]{2,1,0:T(8,128)S(1)}, u32[]{:S(2)}, u32[]{:S(2)}) collective-permute-start(f32[48,16,128]{2,1,0:T(8,128)S(1)} %shard_map.55.after.own), channel_id=1, source_target_pairs={{0,4},{4,8},{8,12},{12,16},{16,20},{20,24},{24,28},{28,0},{1,5},{5... | collective-permute-start | bytes 1179656 | tf_op jit(solution)/shard_map/ppermute | solution.py:58
  15.7 0.7 copy-start.5
  20.9 14.3 %collective-permute-start.8 = (f32[6,17,8,128]{3,2,1,0:T(8,128)S(1)}, f32[6,17,8,128]{3,2,1,0:T(8,128)S(1)}, u32[]{:S(2)}, u32[]{:S(2)}) collective-permute-start(f32[6,17,8,128]{3,2,1,0:T(8,128)S(1)} %get-tuple-element.48), channel_id=1, source_target_pairs={{0,4},{4,8},{8,12},{12,16},{16,20},{20,24},{24,28},{28,0},{1,5},{5... | collective-permute-start | bytes 1253384 | tf_op jit(solution)/shard_map/ppermute | solution.py:58
  22.9 12.3 %collective-permute-start.9 = (f32[6,17,8,128]{3,2,1,0:T(8,128)S(1)}, f32[6,17,8,128]{3,2,1,0:T(8,128)S(1)}, u32[]{:S(2)}, u32[]{:S(2)}) collective-permute-start(f32[6,17,8,128]{3,2,1,0:T(8,128)S(1)} %get-tuple-element.49), channel_id=1, source_target_pairs={{0,28},{4,0},{8,4},{12,8},{16,12},{20,16},{24,20},{28,24},{1,29},{... | collective-permute-start | bytes 1253384 | tf_op jit(solution)/shard_map/ppermute | solution.py:58
  30.3 8.7 %collective-permute-start.6 = (f32[6,72,128]{2,1,0:T(8,128)S(1)}, f32[6,72,128]{2,1,0:T(8,128)S(1)}, u32[]{:S(2)}, u32[]{:S(2)}) collective-permute-start(f32[6,72,128]{2,1,0:T(8,128)S(1)} %get-tuple-element.45), channel_id=1, source_target_pairs={{1,2},{2,1},{3,0},{0,3},{5,6},{6,5},{7,4},{4,7},{9,10},{10,9},{11,... | collective-permute-start | bytes 663560 | tf_op jit(solution)/shard_map/ppermute | solution.py:67
  30.4 8.6 %collective-permute-start.7 = (f32[6,72,128]{2,1,0:T(8,128)S(1)}, f32[6,72,128]{2,1,0:T(8,128)S(1)}, u32[]{:S(2)}, u32[]{:S(2)}) collective-permute-start(f32[6,72,128]{2,1,0:T(8,128)S(1)} %get-tuple-element.46), channel_id=1, source_target_pairs={{0,1},{1,0},{2,3},{3,2},{4,5},{5,4},{6,7},{7,6},{8,9},{9,8},{10,11... | collective-permute-start | bytes 663560 | tf_op jit(solution)/shard_map/ppermute | solution.py:67
  40.6 9.0 %collective-permute-start.12 = (f32[6,72,128]{2,1,0:T(8,128)S(1)}, f32[6,72,128]{2,1,0:T(8,128)S(1)}, u32[]{:S(2)}, u32[]{:S(2)}) collective-permute-start(f32[6,72,128]{2,1,0:T(8,128)S(1)} %get-tuple-element.57), channel_id=1, source_target_pairs={{1,2},{2,1},{3,0},{0,3},{5,6},{6,5},{7,4},{4,7},{9,10},{10,9},{11,... | collective-permute-start | bytes 663560 | tf_op jit(solution)/shard_map/ppermute | solution.py:67
  40.7 8.9 %collective-permute-start.13 = (f32[6,72,128]{2,1,0:T(8,128)S(1)}, f32[6,72,128]{2,1,0:T(8,128)S(1)}, u32[]{:S(2)}, u32[]{:S(2)}) collective-permute-start(f32[6,72,128]{2,1,0:T(8,128)S(1)} %get-tuple-element.58), channel_id=1, source_target_pairs={{0,1},{1,0},{2,3},{3,2},{4,5},{5,4},{6,7},{7,6},{8,9},{9,8},{10,11... | collective-permute-start | bytes 663560 | tf_op jit(solution)/shard_map/ppermute | solution.py:67
  45.5 13.3 %collective-permute-start.10 = (f32[48,16,128]{2,1,0:T(8,128)S(1)}, f32[48,16,128]{2,1,0:T(8,128)S(1)}, u32[]{:S(2)}, u32[]{:S(2)}) collective-permute-start(f32[48,16,128]{2,1,0:T(8,128)S(1)} %get-tuple-element.54), channel_id=1, source_target_pairs={{0,4},{4,8},{8,12},{12,16},{16,20},{20,24},{24,28},{28,0},{1,5},{5... | collective-permute-start | bytes 1179656 | tf_op jit(solution)/shard_map/ppermute | solution.py:58
  45.6 13.2 %collective-permute-start.11 = (f32[48,16,128]{2,1,0:T(8,128)S(1)}, f32[48,16,128]{2,1,0:T(8,128)S(1)}, u32[]{:S(2)}, u32[]{:S(2)}) collective-permute-start(f32[48,16,128]{2,1,0:T(8,128)S(1)} %get-tuple-element.55), channel_id=1, source_target_pairs={{0,28},{4,0},{8,4},{12,8},{16,12},{20,16},{24,20},{28,24},{1,29},{... | collective-permute-start | bytes 1179656 | tf_op jit(solution)/shard_map/ppermute | solution.py:58
  52.4 19.9 %copy-start.3 = (f32[16,16,128]{2,1,0:T(8,128)S(1)}, f32[16,16,128]{2,1,0:T(8,128)}, u32[]{:S(2)}) copy-start(f32[16,16,128]{2,1,0:T(8,128)} %estimate.1) | copy-start | bytes 393220
  52.4 9.6 %collective-permute-start.14 = (f32[24,16,128]{2,1,0:T(8,128)S(1)}, f32[24,16,128]{2,1,0:T(8,128)S(1)}, u32[]{:S(2)}, u32[]{:S(2)}) collective-permute-start(f32[24,16,128]{2,1,0:T(8,128)S(1)} %get-tuple-element.60), channel_id=1, source_target_pairs={{0,4},{4,8},{8,12},{12,16},{16,20},{20,24},{24,28},{28,0},{1,5},{5... | collective-permute-start | bytes 589832 | tf_op jit(solution)/shard_map/ppermute | solution.py:58
  52.5 9.5 %collective-permute-start.15 = (f32[24,16,128]{2,1,0:T(8,128)S(1)}, f32[24,16,128]{2,1,0:T(8,128)S(1)}, u32[]{:S(2)}, u32[]{:S(2)}) collective-permute-start(f32[24,16,128]{2,1,0:T(8,128)S(1)} %get-tuple-element.61), channel_id=1, source_target_pairs={{0,28},{4,0},{8,4},{12,8},{16,12},{20,16},{24,20},{28,24},{1,29},{... | collective-permute-start | bytes 589832 | tf_op jit(solution)/shard_map/ppermute | solution.py:58
  62.2 5.5 %collective-permute-start.16 = (f32[16,16,128]{2,1,0:T(8,128)S(1)}, f32[16,16,128]{2,1,0:T(8,128)S(1)}, u32[]{:S(2)}, u32[]{:S(2)}) collective-permute-start(f32[16,16,128]{2,1,0:T(8,128)S(1)} %get-tuple-element.63), channel_id=1, source_target_pairs={{0,32},{32,64},{64,96},{96,128},{128,160},{160,192},{192,224},{224... | collective-permute-start | bytes 393224 | tf_op jit(solution)/shard_map/ppermute | solution.py:58
  65.2 7.1 %collective-permute-start.17 = (f32[16,16,128]{2,1,0:T(8,128)S(1)}, f32[16,16,128]{2,1,0:T(8,128)S(1)}, u32[]{:S(2)}, u32[]{:S(2)}) collective-permute-start(f32[16,16,128]{2,1,0:T(8,128)S(1)} %get-tuple-element.64), channel_id=1, source_target_pairs={{0,224},{32,0},{64,32},{96,64},{128,96},{160,128},{192,160},{224,1... | collective-permute-start | bytes 393224 | tf_op jit(solution)/shard_map/ppermute | solution.py:58

commit v3 on v2

v3 whole, which is shorter than its diff:
```python
import jax
import jax.numpy as jnp
from jax import lax
from jax.experimental import pallas as pl
from jax.experimental.pallas import tpu as pltpu
from jax.sharding import PartitionSpec as P

V = 6
K = 31
R = 15
OFF = 8
C = 16
Z = 128
W = 3 * C
N = W - 2
HIGH = lax.Precision.HIGH
HIGHEST = lax.Precision.HIGHEST
F32 = jnp.float32
BF16 = jnp.bfloat16

VM = pl.BlockSpec(memory_space=pltpu.VMEM)
SM = pl.BlockSpec(memory_space=pltpu.SMEM)
ANY = pl.BlockSpec(memory_space=pl.ANY)
HBM = pl.BlockSpec(memory_space=pltpu.HBM)


def call(
    body, outs, specs, scratch=(), out_specs=None, grid=(), alias=None,
    flops=0, moved=0, vmem=16,
):
    return pl.pallas_call(
        body,
        grid=grid,
        out_shape=[
            s if hasattr(s, "dtype") else jax.ShapeDtypeStruct(s, F32) for s in outs
        ],
        in_specs=specs,
        out_specs=out_specs or [VM] * len(outs),
        scratch_shapes=list(scratch),
        input_output_aliases=alias or {},
        compiler_params=pltpu.CompilerParams(vmem_limit_bytes=vmem << 20),
        cost_estimate=pl.CostEstimate(
            flops=flops, bytes_accessed=moved, transcendentals=0
        ),
    )


def edges(axis):
    place = lax.axis_index(axis)
    return place > 0, place < lax.axis_size(axis) - 1


def even(axis="bz"):
    return lax.rem(lax.axis_index(axis), 2) == 0


def choose(axis, first, second):
    has_low, has_high = edges(axis)
    low = jnp.where(even(axis), second, first)
    high = jnp.where(even(axis), first, second)
    return jnp.where(has_low, low, 0.0), jnp.where(has_high, high, 0.0)


def trade(block, axis, first):
    count, depth = lax.axis_size(axis), lax.axis_size("bz")
    pairs = []
    for i in range(count):
        j = i + 1 if (i - first) % 2 == 0 else i - 1
        for z in range(depth):
            target = j * depth + z if 0 <= j < count else i * depth + (z ^ 1)
            pairs.append((i * depth + z, target))
    return lax.ppermute(block, (axis, "bz"), pairs)


def swap(block, first):
    count = lax.axis_size("bz")
    pairs = []
    for i in range(first, count, 2):
        a, b = i % count, (i + 1) % count
        pairs += [(a, b), (b, a)]
    return lax.ppermute(block, "bz", pairs)


def lanes(rows):
    return lax.broadcasted_iota(jnp.int32, (rows, Z), 1)


def dot(a, b, precision=HIGH):
    return jnp.dot(a, b, precision=precision, preferred_element_type=F32)


def split(block):
    high = block.astype(BF16)
    return high, (block - high.astype(F32)).astype(BF16)


def pack_planes(cover, own, raw, held, up, down, flags, sem):
    tag = pltpu.make_async_copy(cover, flags, sem)
    tag.start()
    held[C - 1 : 2 * C - 1] = own[...]
    for view in range(V):
        at = slice(view * OFF, (view + 1) * OFF)
        up[at] = jnp.where(even("bx"), raw[view, OFF:], raw[view, :OFF])
        down[at] = jnp.where(even("bx"), raw[view, :OFF], raw[view, OFF:])
    tag.wait()
    for view in range(V):
        tile = jnp.full((1, Z), flags[view].astype(F32))
        up[V * OFF, view : view + 1] = tile
        down[V * OFF, view : view + 1] = tile


def build(
    offsets, psf, after, norm, table, fan_in, fan_out, fan_pair,
    forward_z, backward_z,
):
    norm[...] = jnp.zeros((3, 8, Z), F32)
    for view in range(V):
        for axis in range(3):
            line = psf[view, axis : axis + 1, :]
            norm[axis, view : view + 1, 0:K] = line / jnp.sum(
                line, axis=1, keepdims=True
            )
    bands = []
    for view in range(V):
        line = norm[0, view : view + 1, :]
        for t in range(K):
            table[view, t] = jnp.broadcast_to(line[:, t : t + 1], (8, Z))
        row = jnp.broadcast_to(norm[1, view : view + 1, :], (C, Z))
        bands.append(pltpu.roll(row, 1, 1, stride=1, stride_axis=0))
        row = norm[2, view : view + 1, :]
        row = jnp.concatenate([row, jnp.zeros((1, Z), F32)], axis=1)
        row = jnp.broadcast_to(row, (2 * Z, 2 * Z))
        band = pltpu.roll(row, 2 * Z - R, 1, stride=1, stride_axis=0)
        band = pltpu.roll(band, lax.rem(2 * Z - offsets[2, view], 2 * Z), 1)
        backward_z[view] = band[:, :Z]
        forward_z[view] = band[:Z, :].T
    def side_by_side(*parts):
        total = None
        for turn, block in parts:
            block = block.astype(F32)
            block = jnp.concatenate([block, jnp.zeros_like(block)], axis=1)
            block = pltpu.roll(block, turn, 1) if turn else block
            total = block if total is None else total + block
        return total.astype(BF16)

    high, low = split(jnp.concatenate(bands, axis=0))
    fan_in[...] = side_by_side((0, high), (W, high), (2 * W, low))
    for out, order in ((fan_out, range(V)), (fan_pair, (0, 2, 4, 1, 3, 5))):
        rows = [bands[v] for v in order]
        rows += [jnp.zeros((Z - V * C, Z), F32)]
        high, low = split(jnp.concatenate(rows, axis=0).T[:W, :])
        out[0:W] = side_by_side((0, high), (V * C, high))
        out[W:] = side_by_side((0, low), (V * C, low))


def join_planes(held, low, high, wide):
    low, high = choose("bx", low[...], high[...])
    wide[: C - 1] = low[1:]
    wide[2 * C - 1 :] = high[: C - 1]


def pack_lanes(block, first):
    lane = lanes(64)
    packed = None
    for group in range(4):
        piece = block[4 * group : 4 * group + 4].reshape(64, Z)
        turn = (32 * group - first) % Z
        if turn:
            piece = pltpu.roll(piece, turn, 1)
        packed = piece if packed is None else jnp.where(lane >= 32 * group, piece, packed)
    return packed


def pack_sides(block, near, far, view):
    up = pack_lanes(block, 96)
    down = pack_lanes(block, 0)
    rows = pl.ds(pl.multiple_of(view * 64, 64), 64)
    near[rows, :] = jnp.where(even(), up, down)
    far[rows, :] = jnp.where(even(), down, up)


def forward(table, fan_in, own, low, high, cover, after, blurred, near, far, planes):
    fan = fan_in[:, : 3 * W]
    for pair in range(N // 2):
        sides = []
        for a in (2 * pair, 2 * pair + 1):
            below, above = choose("by", low[a], high[a])
            sides.append(jnp.concatenate([below, own[a], above], axis=0))
        top, rest = split(jnp.concatenate(sides, axis=1))
        both = dot(fan, jnp.concatenate([top, rest, top], axis=0), None)
        planes[2 * pair] = both[:, :Z]
        planes[2 * pair + 1] = both[:, Z:]

    @pl.loop(0, V)
    def _(view):
        taps = [table[view, t] for t in range(K)]
        for half in range(2):
            sums = [None] * C
            for a in range(N):
                plane = planes[a, pl.ds(pl.multiple_of(view * C + 8 * half, 8), 8), :]
                for i in range(C):
                    t = a - i
                    if 0 <= t < K:
                        term = taps[t] * plane
                        sums[i] = term if sums[i] is None else sums[i] + term
            for i in range(C):
                blurred[view, i, 8 * half : 8 * half + 8, :] = sums[i]
        pack_sides(blurred[view], near, far, view)

    for view in range(V):
        tile = jnp.full((1, Z), cover[view].astype(F32))
        near[64 * V + view : 64 * V + view + 1] = tile
        far[64 * V + view : 64 * V + view + 1] = tile


def sides(near, far, view):
    has_low, has_high = edges("bz")
    lane = lanes(64)
    rows = pl.ds(pl.multiple_of(view * 64, 64), 64)
    near, far = near[rows, :], far[rows, :]
    low = jnp.where(even(), far, near)
    high = jnp.where(even(), near, far)
    parts = []
    for group in range(4):
        before = pltpu.roll(low, 96 - 32 * group, 1) if group < 3 else low
        after = pltpu.roll(high, (Z - 32 * group) % Z, 1) if group else high
        before = jnp.where(jnp.logical_and(lane >= 96, has_low), before, 0.0)
        after = jnp.where(jnp.logical_and(lane < 32, has_high), after, 0.0)
        parts.append(before + after)
    return jnp.concatenate(parts, axis=0)


def shift_planes(
    offsets, cover, raw, low, high, after, shifted, up, down, tiles, wide
):
    lane = lanes(8)
    row = lax.broadcasted_iota(jnp.int32, (8, Z), 0)
    own = jnp.zeros((8, Z), F32)
    for view in range(V):
        at = slice(view * OFF, (view + 1) * OFF)
        below, above = choose("bx", low[at], high[at])
        wide[view, 0:OFF] = below
        wide[view, OFF : OFF + C] = raw[view]
        wide[view, OFF + C :] = above
        block = wide[view, pl.ds(OFF + offsets[0, view], C)]
        shifted[view, :, OFF : OFF + C] = block
        at = slice(view * C, (view + 1) * C)
        up[at] = jnp.where(even("by"), block[:, OFF:], block[:, :OFF])
        down[at] = jnp.where(even("by"), block[:, :OFF], block[:, OFF:])
        own = jnp.where(row == view, cover[view].astype(F32), own)
    below, above = choose("bx", low[V * OFF, 0:8], high[V * OFF, 0:8])
    tile = jnp.where(lane == 0, below, jnp.where(lane == 1, own, above))
    tiles[...] = tile
    up[V * C] = tile
    down[V * C] = tile


def shift_rows(offsets, held, low, high, tiles, after, out, marks, main):
    lane = lanes(8)
    for view in range(V):
        at = slice(view * C, (view + 1) * C)
        below, above = choose("by", low[at], high[at])
        main[view, :, 0:OFF] = below
        main[view, :, OFF + C :] = above
        out[view] = main[view, :, pl.ds(OFF + offsets[1, view], C)]
    below, above = choose("by", low[V * C], high[V * C])
    middle = pltpu.roll(tiles[...], 3, 1)
    above = pltpu.roll(above, 6, 1)
    marks[...] = jnp.where(lane < 3, below, jnp.where(lane < 6, middle, above))


def model_own(forward_z, blurred, after, out):
    for view in range(V):
        block = dot(blurred[view].reshape(C * C, Z), forward_z[view, :Z])
        out[view] = block.reshape(C, C, Z)


def divide(
    offsets, cover, forward_z, model, high, low, seen, marks, ratio, near, far
):
    has_low, has_high = edges("bz")
    lane = lanes(1)
    for view in range(V):
        block = dot(sides(low, high, view), forward_z[view, Z:])
        block = model[view] + block.reshape(C, C, Z)
        at = slice(64 * V + view, 64 * V + view + 1)
        before = jnp.where(even(), high[at], low[at])
        after = jnp.where(even(), low[at], high[at])
        before = jnp.where(has_low, before, 0.0)
        after = jnp.where(has_high, after, 0.0)
        own = jnp.full((1, Z), cover[view].astype(F32))
        place = lane - offsets[2, view]
        mask = jnp.where(place < 0, before, jnp.where(place < Z, own, after))
        block = jnp.where(mask > 0.0, mask * seen[view] / block, 0.0)
        ratio[view] = block
        pack_sides(block, near, far, view)
    near[64 * V :] = marks[...]
    far[64 * V :] = marks[...]


def spread(source, taps, planes, row):
    for a in range(N):
        total = None
        for i in range(C):
            t = a - i
            if 0 <= t < K:
                term = taps[t] * source[i]
                total = term if total is None else total + term
        planes[a, pl.ds(pl.multiple_of(row, 8), 8), :] = total


def put(at, piece, first, mid, second):
    mid[at] = piece[C : 2 * C]
    first[at] = jnp.where(even("by"), piece[2 * C :], piece[:C])
    second[at] = jnp.where(even("by"), piece[:C], piece[2 * C :])


def back_own(
    table, fan_out, backward_z, ratio, first, out_mid, second, planes
):
    @pl.loop(0, V)
    def _(view):
        back = dot(ratio[view].reshape(C * C, Z), backward_z[view, :Z])
        back = back.reshape(C, C, Z)
        taps = [table[view, t] for t in range(K)]
        for half in range(2):
            source = [back[i, 8 * half : 8 * half + 8, :] for i in range(C)]
            spread(source, taps, planes, view * C + 8 * half)

    for pair in range(N // 2):
        both = jnp.concatenate([planes[2 * pair], planes[2 * pair + 1]], axis=1)
        both = dot(
            fan_out[:, : 2 * V * C], jnp.concatenate(split(both), axis=0), None
        )
        both = both[:W] + both[W:]
        for part in range(2):
            piece = both[:, part * Z : (part + 1) * Z]
            put(2 * pair + part, piece, first, out_mid, second)


def back_rest(
    table, fan_pair, backward_z, far, near, after, out_first, out_mid, out_second, planes
):
    lane = lanes(8)
    half = lanes(W) < 64

    @pl.loop(0, V // 2)
    def _(pair):
        parts = []
        for odd in range(2):
            view = 2 * pair + odd
            block = sides(near, far, view)
            block = dot(block, backward_z[view, Z:])
            parts.append(pltpu.roll(block, 32 + 64 * odd, 1).reshape(C, C, Z))
        taps = [
            jnp.where(lane < 64, table[2 * pair, t], table[2 * pair + 1, t])
            for t in range(K)
        ]
        for half in range(2):
            rows = slice(8 * half, 8 * half + 8)
            source = [
                jnp.where(lane < 64, parts[0][i, rows], parts[1][i, rows])
                for i in range(C)
            ]
            spread(source, taps, planes, pair * C + 8 * half)

    planes[N] = jnp.zeros((W, Z), F32)
    planes[N + 1] = jnp.zeros((W, Z), F32)

    def fold(a):
        first, second = planes[a], planes[a + 1]
        turned, other = pltpu.roll(first, 64, 1), pltpu.roll(second, 64, 1)
        even_rows = jnp.where(half, first, other)
        odd_rows = jnp.where(half, turned, second)
        return jnp.concatenate([even_rows, odd_rows], axis=0)

    for quad in range(W // 4):
        both = jnp.concatenate([fold(4 * quad), fold(4 * quad + 2)], axis=1)
        both = dot(
            fan_pair[:, : 2 * V * C], jnp.concatenate(split(both), axis=0), None
        )
        both = both[:W] + both[W:]
        for part in range(min(2, N // 2 - 2 * quad)):
            piece = both[:, part * Z : (part + 1) * Z]
            put(2 * quad + part, piece, out_first, out_mid, out_second)


def add_rows(
    mid, from_low, from_high, rest, rest_low, rest_high, out_mid, first, second,
    out_low, out_high,
):
    lane = lanes(C)
    ends = jnp.logical_or(lane < 32, lane >= 96)
    out_low[0] = jnp.zeros((C, Z), F32)
    out_high[C - 1] = jnp.zeros((C, Z), F32)
    for a in range(N):
        below, above = choose("by", from_low[a], from_high[a])
        total = mid[a] + below + above
        below, above = choose("by", rest_low[a // 2], rest_high[a // 2])
        more = rest[a // 2] + below + above
        more = pltpu.roll(more, 32 if a % 2 else 96, 1)
        total = total + jnp.where(ends, more, 0.0)
        out = (out_low, out_mid, out_high)[(a + 1) // C]
        out[(a + 1) % C] = total
    first[...] = jnp.where(even("bx"), out_high[...], out_low[...])
    second[...] = jnp.where(even("bx"), out_low[...], out_high[...])


def part(tap, cell, count, which):
    before = jnp.where(tap > cell + R, 1.0, 0.0)
    after = jnp.where(tap < cell + R + 1 - count, 1.0, 0.0)
    return jnp.where(which == 0, before, jnp.where(which == 2, after, 1.0 - before - after))


def weigh(norm, estimate, marks, near_marks, far_marks, scale):
    has_low, has_high = edges("bz")
    tap = lax.broadcasted_iota(jnp.int32, (Z, Z), 0)
    cell = lax.broadcasted_iota(jnp.int32, (Z, Z), 1)
    part_x = [dot(norm[0], part(tap, cell, C, p), HIGHEST) for p in range(3)]
    part_z = [dot(norm[2], part(tap, cell, Z, r), HIGHEST) for r in range(3)]
    part_y = [dot(norm[1], part(tap, cell, C, q), HIGHEST) for q in range(3)]
    part_y = [jnp.concatenate([y] * C, axis=0).T for y in part_y]
    sums = [jnp.zeros((C, Z), F32) for _ in range(C)]
    for view in range(V):
        at = slice(view, view + 1)
        low = jnp.where(even(), far_marks[at], near_marks[at])
        high = jnp.where(even(), near_marks[at], far_marks[at])
        near = [
            jnp.where(has_low, low, 0.0),
            marks[at],
            jnp.where(has_high, high, 0.0),
        ]
        share = [
            jnp.broadcast_to(part_y[q][:C, view : view + 1], (C, Z)) for q in range(3)
        ]
        for p in range(3):
            term = None
            for r in range(3):
                level = None
                for q in range(3):
                    at = 3 * q + p
                    cell = jnp.broadcast_to(near[r][:, at : at + 1], (C, Z)) * share[q]
                    level = cell if level is None else level + cell
                level = level * part_z[r][view : view + 1, :]
                term = level if term is None else term + level
            for i in range(C):
                factor = jnp.broadcast_to(part_x[p][view : view + 1, i : i + 1], (C, Z))
                sums[i] = sums[i] + factor * term
    for i in range(C):
        scale[i] = estimate[i] / sums[i]


def finish(scale, mid, from_low, from_high, out):
    low, high = choose("bx", from_low[...], from_high[...])
    total = mid[...] + low + high
    out[...] = scale[...] * total


def on_device(estimate, raw, psf, offsets, coverage):
    cover = coverage.reshape(V)
    offsets = offsets.T
    full = (V, C, C, Z)

    left = trade(estimate, "bx", 0)
    right = trade(estimate, "bx", 1)
    held, up, down = call(
        pack_planes,
        [(N, C, Z)] + [(V * OFF + 1, C, Z)] * 2,
        [HBM, VM, VM],
        [pltpu.SMEM((V,), jnp.int32), pltpu.SemaphoreType.DMA],
        moved=3 << 19,
    )(cover, estimate, raw)
    raw_low = trade(up, "bx", 0)
    raw_high = trade(down, "bx", 1)
    (wide,) = call(join_planes, [(N, C, Z)], [VM] * 3, alias={0: 0}, moved=1 << 18)(
        held, left, right
    )
    norm, table, fan_in, fan_out, fan_pair, forward_z, backward_z = call(
        build,
        [
            (3, 8, Z),
            (V, K, 8, Z),
            jax.ShapeDtypeStruct((V * C, 2 * Z), BF16),
            jax.ShapeDtypeStruct((2 * W, 2 * Z), BF16),
            jax.ShapeDtypeStruct((2 * W, 2 * Z), BF16),
            (V, 2 * Z, Z),
            (V, 2 * Z, Z),
        ],
        [SM, VM, ANY],
        moved=1 << 23,
    )(offsets, psf, wide)
    low = trade(wide, "by", 0)
    high = trade(wide, "by", 1)

    shifted, up, down, tiles = call(
        shift_planes,
        [
            (V, C, 2 * C, Z),
            (V * C + 1, OFF, Z),
            (V * C + 1, OFF, Z),
            (8, Z),
        ],
        [SM, SM, VM, VM, VM, ANY],
        [pltpu.VMEM((V, 2 * C, C, Z), F32)],
        moved=1 << 26,
    )(offsets, cover, raw, raw_low, raw_high, norm)
    raw_low = trade(up, "by", 0)
    raw_high = trade(down, "by", 1)

    blurred, near, far = call(
        forward,
        [full, (64 * V + 8, Z), (64 * V + 8, Z)],
        [VM] * 5 + [SM, ANY],
        [pltpu.VMEM((N, V * C, Z), F32)],
        flops=1 << 34,
        moved=1 << 26,
    )(table, fan_in, wide, low, high, cover, tiles)
    far, near = swap(far, 1), swap(near, 0)

    seen, marks, _ = call(
        shift_rows,
        [full, (8, Z), (V, C, 2 * C, Z)],
        [SM] + [VM] * 4 + [ANY],
        alias={1: 2},
        moved=1 << 26,
    )(offsets, shifted, raw_low, raw_high, tiles, blurred)

    (model,) = call(
        model_own, [full], [VM, VM, ANY], flops=1 << 30, moved=3 << 20
    )(forward_z, blurred, seen)
    ratio, near, far = call(
        divide,
        [full, (64 * V + 8, Z), (64 * V + 8, Z)],
        [SM, SM] + [VM] * 6,
        flops=1 << 34,
        moved=1 << 26,
    )(offsets, cover, forward_z, model, far, near, seen, marks)
    far, near = swap(far, 1), swap(near, 0)

    first, out_mid, second = call(
        back_own,
        [(N, C, Z)] * 3,
        [VM] * 4,
        [pltpu.VMEM((N, V * C, Z), F32)],
        flops=1 << 34,
        moved=1 << 26,
    )(table, fan_out, backward_z, ratio)
    sum_low = trade(first, "by", 0)
    sum_high = trade(second, "by", 1)
    rest_first, rest_mid, rest_second = call(
        back_rest,
        [(N // 2, C, Z)] * 3,
        [VM] * 5 + [ANY],
        [pltpu.VMEM((W, W, Z), F32)],
        flops=1 << 34,
        moved=1 << 26,
    )(table, fan_pair, backward_z, far, near, out_mid)
    more_low = trade(rest_first, "by", 0)
    more_high = trade(rest_second, "by", 1)
    last = pl.BlockSpec((8, Z), lambda i: (8 * V, 0))
    (scale,) = call(
        weigh, [(C, C, Z)], [VM, VM, VM, last, last], grid=(1,), moved=1 << 19
    )(norm, estimate, marks, near, far)
    out_mid, first, second = call(
        add_rows,
        [(C, C, Z)] * 3,
        [VM] * 6,
        [pltpu.VMEM((C, C, Z), F32)] * 2,
        moved=3 << 19,
    )(out_mid, sum_low, sum_high, rest_mid, more_low, more_high)
    sum_low = trade(first, "bx", 0)
    sum_high = trade(second, "bx", 1)
    (out,) = call(finish, [(C, C, Z)], [VM] * 4, moved=3 << 18)(
        scale, out_mid, sum_low, sum_high
    )
    return out


def solution(mesh):
    return jax.shard_map(
        on_device,
        mesh=mesh,
        in_specs=(
            P("bx", "by", "bz"),
            P(None, "bx", "by", "bz"),
            P(),
            P(),
            P(None, "bx", "by", "bz"),
        ),
        out_specs=P("bx", "by", "bz"),
        check_vma=False,
    )
```

time: 73.1 us -> 67.9 us (0.929)
  the two profiles are of different devices: /device:TPU:14 before, /device:TPU:38 now
where the time goes in v3:
time: 67.9 us; the launch traced here: 67.2 us
  starting transfers between devices  26.2 us (39%)
  waiting for transfers between devices  20.4 us (30%)
  Pallas kernels  17.7 us (26%)
  local copies, waits for them, and re-layouts  2.71 us (4%)
    ppermute x14, starting transfers between devices, trade(): return lax.ppermute(block, (axis, 'bz'), pairs)  22 us
    ppermute x14, waiting for transfers between devices, trade(): return lax.ppermute(block, (axis, 'bz'), pairs)  16.9 us
    ppermute x4, starting transfers between devices, swap(): return lax.ppermute(block, 'bz', pairs)  4.23 us
    ppermute x4, waiting for transfers between devices, swap(): return lax.ppermute(block, 'bz', pairs)  3.54 us
    pallas_call x1, Pallas kernels, on_device(): call(back_own, [(N, C, Z)] * 3, [VM] * 4, [pltpu.VMEM((N, V * C, Z), F32)...  3.41 us
    pallas_call x1, Pallas kernels, on_device(): call(forward, [full, (64 * V + 8, Z), (64 * V + 8, Z)], [VM] * 5 + [SM, A...  3.38 us
    pallas_call x1, Pallas kernels, on_device(): call(back_rest, [(N // 2, C, Z)] * 3, [VM] * 5 + [ANY], [pltpu.VMEM((W, W...  2.74 us
    unnamed x16, local copies, waits for them, and re-layouts  2.71 us
  transfers between devices with their start and end apart: 18, of which 10 were waited for; matrix products, arithmetic and copies ran while one was open for 0% of the time, Pallas kernels for 23%

profile of v3, /device:TPU:38, one launch (start us, length us, event | category | flops | bytes accessed | tf_op | source)
XLA Modules:
  0.0 67.2 jit_solution(13094838201184079706)
XLA Ops:
  0.0 0.8 %collective-permute-start = (f32[16,16,128]{2,1,0:T(8,128)}, f32[16,16,128]{2,1,0:T(8,128)S(1)}, u32[]{:S(2)}, u32[]{:S(2)}) collective-permute-start(f32[16,16,128]{2,1,0:T(8,128)} %estimate.1), channel_id=1, source_target_pairs={{0,32},{1,33},{2,34},{3,35},{32,0},{33,1},{34,2},{35,3},{64,96},{6... | collective-permute-start | bytes 393224 | tf_op jit(solution)/shard_map/ppermute | solution.py:72
  0.8 2.2 %collective-permute-start.1 = (f32[16,16,128]{2,1,0:T(8,128)}, f32[16,16,128]{2,1,0:T(8,128)S(1)}, u32[]{:S(2)}, u32[]{:S(2)}) collective-permute-start(f32[16,16,128]{2,1,0:T(8,128)} %estimate.1), channel_id=1, source_target_pairs={{0,1},{1,0},{2,3},{3,2},{32,64},{33,65},{34,66},{35,67},{64,32},{6... | collective-permute-start | bytes 393224 | tf_op jit(solution)/shard_map/ppermute | solution.py:72
  3.0 0.0 copy-start
  3.0 1.1 %copy-done = f32[6,16,16,128]{3,2,1,0:T(8,128)S(1)} copy-done((f32[6,16,16,128]{3,2,1,0:T(8,128)S(1)}, f32[6,16,16,128]{3,2,1,0:T(8,128)}, u32[]{:S(2)}) %copy-start) | copy-done | bytes 786456
  4.1 0.0 copy-start.2
  4.1 0.9 %copy-done.2 = f32[16,16,128]{2,1,0:T(8,128)S(1)} copy-done((f32[16,16,128]{2,1,0:T(8,128)S(1)}, f32[16,16,128]{2,1,0:T(8,128)}, u32[]{:S(2)}) %copy-start.2) | copy-done | bytes 131096
  5.0 0.0 copy-start.6
  5.0 0.7 copy-done.6
  5.7 0.0 copy-start.4
  5.7 0.0 copy-start.5
  5.7 0.0 copy-start.1
  5.7 0.6 shard_map.55
  6.2 0.1 collective-permute-start.2
  6.3 2.7 %collective-permute-start.3 = (f32[49,16,128]{2,1,0:T(8,128)S(1)}, f32[49,16,128]{2,1,0:T(8,128)S(1)}, u32[]{:S(2)}, u32[]{:S(2)}) collective-permute-start(f32[49,16,128]{2,1,0:T(8,128)S(1)} %get-tuple-element.39), channel_id=1, source_target_pairs={{0,1},{1,0},{2,3},{3,2},{32,64},{33,65},{34,66},{35,67},{64,32},{6... | collective-permute-start | bytes 1204232 | tf_op jit(solution)/shard_map/ppermute | solution.py:72
  9.0 0.0 collective-permute-done.low
  9.0 0.0 collective-permute-done.1.high
  9.1 2.0 %collective-permute-start.7 = (f32[46,16,128]{2,1,0:T(8,128)S(1)}, f32[46,16,128]{2,1,0:T(8,128)S(1)}, u32[]{:S(2)}, u32[]{:S(2)}) collective-permute-start(f32[46,16,128]{2,1,0:T(8,128)S(1)} %shard_map.56.after.own), channel_id=1, source_target_pairs={{0,1},{1,0},{2,3},{3,2},{4,8},{5,9},{6,10},{7,11},{8,4},{9,5},{10,... | collective-permute-start | bytes 1130504 | tf_op jit(solution)/shard_map/ppermute | solution.py:72
  11.1 0.0 collective-permute-start.6
  11.1 0.0 copy-done.4
  11.1 0.0 copy-done.5
  11.1 1.9 %shard_map.57 = (f32[3,8,128]{2,1,0:T(8,128)S(1)}, f32[6,31,8,128]{3,2,1,0:T(8,128)S(1)}, bf16[96,256]{1,0:T(8,128)(2,1)S(1)}, bf16[96,256]{1,0:T(8,128)(2,1)S(1...) custom-call(s32[3,6]{1,0:T(4,128)S(1)} %bitcast.2, ...), custom_call_target="tpu_custom_call" | custom-call | bytes 8388608 | tf_op jit(solution)/shard_map/pallas_call | solution.py:478
  13.0 3.8 %collective-permute-done.2.low = f32[49,16,128]{2,1,0:T(8,128)S(1)} collective-permute-done((f32[49,16,128]{2,1,0:T(8,128)S(1)}, f32[49,16,128]{2,1,0:T(8,128)S(1)}, u32[]{:S(2)}, u32[]{:S(2)}) %collective-permute-start.2) | collective-permute-done | bytes 401440 | tf_op jit(solution)/shard_map/ppermute | solution.py:72
  16.8 2.2 %collective-permute-done.3.high = f32[49,16,128]{2,1,0:T(8,128)S(1)} collective-permute-done((f32[49,16,128]{2,1,0:T(8,128)S(1)}, f32[49,16,128]{2,1,0:T(8,128)S(1)}, u32[]{:S(2)}, u32[]{:S(2)}) %collective-permute-start.3) | collective-permute-done | bytes 401440 | tf_op jit(solution)/shard_map/ppermute | solution.py:72
  19.0 0.0 copy-done.1
  19.0 0.8 %shard_map.58 = (f32[6,16,32,128]{3,2,1,0:T(8,128)S(1)}, f32[97,8,128]{2,1,0:T(8,128)S(1)}, f32[97,8,128]{2,1,0:T(8,128)S(1)}, f32[8,128]{1,0:T(8,128)S(1)}) custom-call(s32[3,6]{1,0:T(4,128)S(1)} %bitcast.3, s32[6]{0:T(128)S(1)} %bitcast.7, f32[6,16,16,128]{3,2,1,0:T(8,128)S(1)} %copy-done.1, f32[49,16,128]{2,1,0:T(8,128)S(1)} %collective-permute-done.2.low, ...), custom_call_target="tpu_custom_call" | custom-call | bytes 67108864 | tf_op jit(solution)/shard_map/pallas_call | solution.py:495
  19.8 0.2 collective-permute-start.4
  20.0 3.7 %collective-permute-start.5 = (f32[97,8,128]{2,1,0:T(8,128)S(1)}, f32[97,8,128]{2,1,0:T(8,128)S(1)}, u32[]{:S(2)}, u32[]{:S(2)}) collective-permute-start(f32[97,8,128]{2,1,0:T(8,128)S(1)} %get-tuple-element.42), channel_id=1, source_target_pairs={{0,1},{1,0},{2,3},{3,2},{4,8},{5,9},{6,10},{7,11},{8,4},{9,5},{10,... | collective-permute-start | bytes 1191944 | tf_op jit(solution)/shard_map/ppermute | solution.py:72
  23.8 0.0 collective-permute-done.7.high
  23.8 0.0 collective-permute-done.6.low
  23.8 3.4 %shard_map.59 = (f32[6,16,16,128]{3,2,1,0:T(8,128)S(1)}, f32[392,128]{1,0:T(8,128)S(1)}, f32[392,128]{1,0:T(8,128)S(1)}) custom-call(f32[6,31,8,128]{3,2,1,0:T(8,128)S(1)} %get-tuple-element.44.table, bf16[96,256]{1,0:T(8,128)(2,1)S(1)} %get-tuple-element.45.fan_in, f32[46,16,128]{2,1,0:T(8,128)S(1)} %shard_map.56.after.own, ...), custom_call_target="tpu_custom_call" | custom-call | flops 17179869184 | bytes 67108864 | tf_op jit(solution)/shard_map/pallas_call | solution.py:510
  27.1 0.4 collective-permute-start.8
  27.5 2.7 %collective-permute-start.9 = (f32[392,128]{1,0:T(8,128)S(1)}, f32[392,128]{1,0:T(8,128)S(1)}, u32[]{:S(2)}, u32[]{:S(2)}) collective-permute-start(f32[392,128]{1,0:T(8,128)S(1)} %get-tuple-element.51), channel_id=1, source_target_pairs={{0,1},{1,0},{2,3},{3,2},{4,5},{5,4},{6,7},{7,6},{8,9},{9,8},{10,11... | collective-permute-start | bytes 602120 | tf_op jit(solution)/shard_map/ppermute | solution.py:81
  30.2 0.0 collective-permute-done.4.low
  30.2 1.0 %collective-permute-done.5.high = f32[97,8,128]{2,1,0:T(8,128)S(1)} collective-permute-done((f32[97,8,128]{2,1,0:T(8,128)S(1)}, f32[97,8,128]{2,1,0:T(8,128)S(1)}, u32[]{:S(2)}, u32[]{:S(2)}) %collective-permute-start.5) | collective-permute-done | bytes 397344 | tf_op jit(solution)/shard_map/ppermute | solution.py:72
  31.2 0.7 %shard_map.60 = (f32[6,16,16,128]{3,2,1,0:T(8,128)S(1)}, f32[8,128]{1,0:T(8,128)S(1)}, f32[6,16,32,128]{3,2,1,0:T(8,128)S(1)}) custom-call(s32[3,6]{1,0:T(4,128)S(1)} %bitcast.4, f32[6,16,32,128]{3,2,1,0:T(8,128)S(1)} %get-tuple-element.40.held, f32[97,8,128]{2,1,0:T(8,128)S(1)} %collective-permute-done.4.low, ...), custom_call_target="tpu_custom_call", output_to_operand_aliasing={{2}: (1, {})} | custom-call | bytes 67108864 | tf_op jit(solution)/shard_map/pallas_call | solution.py:520
  31.9 0.0 copy-start.7
  32.0 0.5 shard_map.61.model
  32.4 3.5 %collective-permute-done.8.high = f32[392,128]{1,0:T(8,128)S(1)} collective-permute-done((f32[392,128]{1,0:T(8,128)S(1)}, f32[392,128]{1,0:T(8,128)S(1)}, u32[]{:S(2)}, u32[]{:S(2)}) %collective-permute-start.8) | collective-permute-done | bytes 200736 | tf_op jit(solution)/shard_map/ppermute | solution.py:81
  36.0 0.0 collective-permute-done.9.low
  36.0 0.0 copy-done.7
  36.0 1.5 %shard_map.62 = (f32[6,16,16,128]{3,2,1,0:T(8,128)S(1)}, f32[392,128]{1,0:T(8,128)S(1)}, f32[392,128]{1,0:T(8,128)S(1)}) custom-call(s32[3,6]{1,0:T(4,128)S(1)} %bitcast.5, s32[6]{0:T(128)S(1)} %bitcast.9, f32[6,256,128]{2,1,0:T(8,128)S(1)} %get-tuple-element.48.forward_z, f32[6,16,16,128]{3,2,1,0:T(8,128)S(1)} %shard_map.61.model, ...), custom_call_target="tpu_custom_call" | custom-call | flops 17179869184 | bytes 67108864 | tf_op jit(solution)/shard_map/pallas_call | solution.py:531
  37.5 0.1 collective-permute-start.10
  37.7 1.0 %collective-permute-start.11 = (f32[392,128]{1,0:T(8,128)S(1)}, f32[392,128]{1,0:T(8,128)S(1)}, u32[]{:S(2)}, u32[]{:S(2)}) collective-permute-start(f32[392,128]{1,0:T(8,128)S(1)} %get-tuple-element.53), channel_id=1, source_target_pairs={{1,2},{2,1},{3,0},{0,3},{5,6},{6,5},{7,4},{4,7},{9,10},{10,9},{11,... | collective-permute-start | bytes 602120 | tf_op jit(solution)/shard_map/ppermute | solution.py:81
  38.7 3.4 %shard_map.64 = (f32[46,16,128]{2,1,0:T(8,128)S(1)}, f32[46,16,128]{2,1,0:T(8,128)S(1)}, f32[46,16,128]{2,1,0:T(8,128)S(1)}) custom-call(f32[6,31,8,128]{3,2,1,0:T(8,128)S(1)} %get-tuple-element.44.table, bf16[96,256]{1,0:T(8,128)(2,1)S(1)} %get-tuple-element.54.fan_out, f32[6,256,128]{2,1,0:T(8,128)S(1)} %get-tuple-element.55.backward_z, ...), custom_call_target="tpu_custom_call" | custom-call | flops 17179869184 | bytes 67108864 | tf_op jit(solution)/shard_map/pallas_call | solution.py:540
  42.1 0.1 collective-permute-start.12
  42.2 4.1 %collective-permute-start.13 = (f32[46,16,128]{2,1,0:T(8,128)S(1)}, f32[46,16,128]{2,1,0:T(8,128)S(1)}, u32[]{:S(2)}, u32[]{:S(2)}) collective-permute-start(f32[46,16,128]{2,1,0:T(8,128)S(1)} %get-tuple-element.59), channel_id=1, source_target_pairs={{0,1},{1,0},{2,3},{3,2},{4,8},{5,9},{6,10},{7,11},{8,4},{9,5},{10,... | collective-permute-start | bytes 1130504 | tf_op jit(solution)/shard_map/ppermute | solution.py:72
  46.3 0.0 collective-permute-done.10.near_marks.near
  46.3 0.0 collective-permute-done.11.far_marks.far
  46.3 2.7 %shard_map.65 = (f32[23,16,128]{2,1,0:T(8,128)S(1)}, f32[23,16,128]{2,1,0:T(8,128)S(1)}, f32[23,16,128]{2,1,0:T(8,128)S(1)}) custom-call(f32[6,31,8,128]{3,2,1,0:T(8,128)S(1)} %get-tuple-element.44.table, bf16[96,256]{1,0:T(8,128)(2,1)S(1)} %get-tuple-element.60.fan_pair, f32[6,256,128]{2,1,0:T(8,128)S(1)} %get-tuple-element.55.backward_z, ...), custom_call_target="tpu_custom_call" | custom-call | flops 17179869184 | bytes 67108864 | tf_op jit(solution)/shard_map/pallas_call | solution.py:550
  49.1 0.0 copy-start.3
  49.1 0.1 collective-permute-start.14
  49.2 3.8 %collective-permute-start.15 = (f32[23,16,128]{2,1,0:T(8,128)S(1)}, f32[23,16,128]{2,1,0:T(8,128)S(1)}, u32[]{:S(2)}, u32[]{:S(2)}) collective-permute-start(f32[23,16,128]{2,1,0:T(8,128)S(1)} %get-tuple-element.63), channel_id=1, source_target_pairs={{0,1},{1,0},{2,3},{3,2},{4,8},{5,9},{6,10},{7,11},{8,4},{9,5},{10,... | collective-permute-start | bytes 565256 | tf_op jit(solution)/shard_map/ppermute | solution.py:72
  53.0 0.8 %collective-permute-done.12.from_low = f32[46,16,128]{2,1,0:T(8,128)S(1)} collective-permute-done((f32[46,16,128]{2,1,0:T(8,128)S(1)}, f32[46,16,128]{2,1,0:T(8,128)S(1)}, u32[]{:S(2)}, u32[]{:S(2)}) %collective-permute-start.12) | collective-permute-done | bytes 376864 | tf_op jit(solution)/shard_map/ppermute | solution.py:72
  53.8 2.1 %collective-permute-done.13.from_high = f32[46,16,128]{2,1,0:T(8,128)S(1)} collective-permute-done((f32[46,16,128]{2,1,0:T(8,128)S(1)}, f32[46,16,128]{2,1,0:T(8,128)S(1)}, u32[]{:S(2)}, u32[]{:S(2)}) %collective-permute-start.13) | collective-permute-done | bytes 376864 | tf_op jit(solution)/shard_map/ppermute | solution.py:72
  55.9 1.1 %collective-permute-done.14.rest_low = f32[23,16,128]{2,1,0:T(8,128)S(1)} collective-permute-done((f32[23,16,128]{2,1,0:T(8,128)S(1)}, f32[23,16,128]{2,1,0:T(8,128)S(1)}, u32[]{:S(2)}, u32[]{:S(2)}) %collective-permute-start.14) | collective-permute-done | bytes 188448 | tf_op jit(solution)/shard_map/ppermute | solution.py:72
  57.0 2.1 %collective-permute-done.15.rest_high = f32[23,16,128]{2,1,0:T(8,128)S(1)} collective-permute-done((f32[23,16,128]{2,1,0:T(8,128)S(1)}, f32[23,16,128]{2,1,0:T(8,128)S(1)}, u32[]{:S(2)}, u32[]{:S(2)}) %collective-permute-start.15) | collective-permute-done | bytes 188448 | tf_op jit(solution)/shard_map/ppermute | solution.py:72
  59.1 0.2 shard_map.66
  59.3 0.1 collective-permute-start.16
  59.4 2.1 %collective-permute-start.17 = (f32[16,16,128]{2,1,0:T(8,128)S(1)}, f32[16,16,128]{2,1,0:T(8,128)S(1)}, u32[]{:S(2)}, u32[]{:S(2)}) collective-permute-start(f32[16,16,128]{2,1,0:T(8,128)S(1)} %get-tuple-element.66), channel_id=1, source_target_pairs={{0,1},{1,0},{2,3},{3,2},{32,64},{33,65},{34,66},{35,67},{64,32},{6... | collective-permute-start | bytes 393224 | tf_op jit(solution)/shard_map/ppermute | solution.py:72
  61.5 0.0 copy-done.3
  61.5 1.2 %shard_map.63.scale = f32[16,16,128]{2,1,0:T(8,128)S(1)} custom-call(f32[3,8,128]{2,1,0:T(8,128)S(1)} %get-tuple-element.37.after.norm, f32[16,16,128]{2,1,0:T(8,128)S(1)} %copy-done.3, f32[8,128]{1,0:T(8,128)S(1)} %get-tuple-element.47.marks, f32[392,128]{1,0:T(8,128)S(1)} %collective-permute-done.10.near_marks.near, ...), custom_call_target="tpu_custom_call" | custom-call | bytes 524288 | tf_op jit(solution)/shard_map/pallas_call | solution.py:561
  62.7 1.6 %collective-permute-done.16.from_low = f32[16,16,128]{2,1,0:T(8,128)S(1)} collective-permute-done((f32[16,16,128]{2,1,0:T(8,128)S(1)}, f32[16,16,128]{2,1,0:T(8,128)S(1)}, u32[]{:S(2)}, u32[]{:S(2)}) %collective-permute-start.16) | collective-permute-done | bytes 131104 | tf_op jit(solution)/shard_map/ppermute | solution.py:72
  64.3 2.2 %collective-permute-done.17.from_high = f32[16,16,128]{2,1,0:T(8,128)S(1)} collective-permute-done((f32[16,16,128]{2,1,0:T(8,128)S(1)}, f32[16,16,128]{2,1,0:T(8,128)S(1)}, u32[]{:S(2)}, u32[]{:S(2)}) %collective-permute-start.17) | collective-permute-done | bytes 131104 | tf_op jit(solution)/shard_map/ppermute | solution.py:72
  66.5 0.7 %shard_map.67 = f32[16,16,128]{2,1,0:T(8,128)} custom-call(f32[16,16,128]{2,1,0:T(8,128)S(1)} %shard_map.63.scale, f32[16,16,128]{2,1,0:T(8,128)S(1)} %get-tuple-element.64.mid, f32[16,16,128]{2,1,0:T(8,128)S(1)} %collective-permute-done.16.from_low, f32[16,16,128]{2,1,0:T(8,128)S(1)} %collective-permute-done.17.from_high), custom_call_target="tpu_custom_call" | custom-call | bytes 786432 | tf_op jit(solution)/shard_map/pallas_call | solution.py:573
  (1 shorter events, 0.0 us)
Async XLA Ops:
  0.0 9.0 %collective-permute-start = (f32[16,16,128]{2,1,0:T(8,128)}, f32[16,16,128]{2,1,0:T(8,128)S(1)}, u32[]{:S(2)}, u32[]{:S(2)}) collective-permute-start(f32[16,16,128]{2,1,0:T(8,128)} %estimate.1), channel_id=1, source_target_pairs={{0,32},{1,33},{2,34},{3,35},{32,0},{33,1},{34,2},{35,3},{64,96},{6... | collective-permute-start | bytes 393224 | tf_op jit(solution)/shard_map/ppermute | solution.py:72
  0.8 8.2 %collective-permute-start.1 = (f32[16,16,128]{2,1,0:T(8,128)}, f32[16,16,128]{2,1,0:T(8,128)S(1)}, u32[]{:S(2)}, u32[]{:S(2)}) collective-permute-start(f32[16,16,128]{2,1,0:T(8,128)} %estimate.1), channel_id=1, source_target_pairs={{0,1},{1,0},{2,3},{3,2},{32,64},{33,65},{34,66},{35,67},{64,32},{6... | collective-permute-start | bytes 393224 | tf_op jit(solution)/shard_map/ppermute | solution.py:72
  3.0 1.1 %copy-start = (f32[6,16,16,128]{3,2,1,0:T(8,128)S(1)}, f32[6,16,16,128]{3,2,1,0:T(8,128)}, u32[]{:S(2)}) copy-start(f32[6,16,16,128]{3,2,1,0:T(8,128)} %raw.3) | copy-start | bytes 2359300
  4.1 0.9 %copy-start.2 = (f32[16,16,128]{2,1,0:T(8,128)S(1)}, f32[16,16,128]{2,1,0:T(8,128)}, u32[]{:S(2)}) copy-start(f32[16,16,128]{2,1,0:T(8,128)} %estimate.1) | copy-start | bytes 393220
  5.0 0.7 copy-start.6
  5.7 5.4 %copy-start.4 = (s32[6,3]{0,1:T(4,128)S(1)}, s32[6,3]{0,1:T(4,128)}, u32[]{:S(2)}) copy-start(s32[6,3]{0,1:T(4,128)} %param.8) | copy-start | bytes 220
  5.7 5.4 %copy-start.5 = (f32[6,3,31]{2,1,0:T(4,128)S(1)}, f32[6,3,31]{2,1,0:T(4,128)}, u32[]{:S(2)}) copy-start(f32[6,3,31]{2,1,0:T(4,128)} %psf.1) | copy-start | bytes 6700
  5.7 13.3 %copy-start.1 = (f32[6,16,16,128]{3,2,1,0:T(8,128)S(1)}, f32[6,16,16,128]{3,2,1,0:T(8,128)}, u32[]{:S(2)}) copy-start(f32[6,16,16,128]{3,2,1,0:T(8,128)} %raw.3) | copy-start | bytes 2359300
  6.2 10.6 %collective-permute-start.2 = (f32[49,16,128]{2,1,0:T(8,128)S(1)}, f32[49,16,128]{2,1,0:T(8,128)S(1)}, u32[]{:S(2)}, u32[]{:S(2)}) collective-permute-start(f32[49,16,128]{2,1,0:T(8,128)S(1)} %get-tuple-element.38), channel_id=1, source_target_pairs={{0,32},{1,33},{2,34},{3,35},{32,0},{33,1},{34,2},{35,3},{64,96},{6... | collective-permute-start | bytes 1204232 | tf_op jit(solution)/shard_map/ppermute | solution.py:72
  6.3 12.7 %collective-permute-start.3 = (f32[49,16,128]{2,1,0:T(8,128)S(1)}, f32[49,16,128]{2,1,0:T(8,128)S(1)}, u32[]{:S(2)}, u32[]{:S(2)}) collective-permute-start(f32[49,16,128]{2,1,0:T(8,128)S(1)} %get-tuple-element.39), channel_id=1, source_target_pairs={{0,1},{1,0},{2,3},{3,2},{32,64},{33,65},{34,66},{35,67},{64,32},{6... | collective-permute-start | bytes 1204232 | tf_op jit(solution)/shard_map/ppermute | solution.py:72
  9.1 14.7 %collective-permute-start.7 = (f32[46,16,128]{2,1,0:T(8,128)S(1)}, f32[46,16,128]{2,1,0:T(8,128)S(1)}, u32[]{:S(2)}, u32[]{:S(2)}) collective-permute-start(f32[46,16,128]{2,1,0:T(8,128)S(1)} %shard_map.56.after.own), channel_id=1, source_target_pairs={{0,1},{1,0},{2,3},{3,2},{4,8},{5,9},{6,10},{7,11},{8,4},{9,5},{10,... | collective-permute-start | bytes 1130504 | tf_op jit(solution)/shard_map/ppermute | solution.py:72
  11.1 12.7 %collective-permute-start.6 = (f32[46,16,128]{2,1,0:T(8,128)S(1)}, f32[46,16,128]{2,1,0:T(8,128)S(1)}, u32[]{:S(2)}, u32[]{:S(2)}) collective-permute-start(f32[46,16,128]{2,1,0:T(8,128)S(1)} %shard_map.56.after.own), channel_id=1, source_target_pairs={{0,4},{1,5},{2,6},{3,7},{4,0},{5,1},{6,2},{7,3},{8,12},{9,13},{10,... | collective-permute-start | bytes 1130504 | tf_op jit(solution)/shard_map/ppermute | solution.py:72
  19.8 10.4 %collective-permute-start.4 = (f32[97,8,128]{2,1,0:T(8,128)S(1)}, f32[97,8,128]{2,1,0:T(8,128)S(1)}, u32[]{:S(2)}, u32[]{:S(2)}) collective-permute-start(f32[97,8,128]{2,1,0:T(8,128)S(1)} %get-tuple-element.41), channel_id=1, source_target_pairs={{0,4},{1,5},{2,6},{3,7},{4,0},{5,1},{6,2},{7,3},{8,12},{9,13},{10,... | collective-permute-start | bytes 1191944 | tf_op jit(solution)/shard_map/ppermute | solution.py:72
  20.0 11.2 %collective-permute-start.5 = (f32[97,8,128]{2,1,0:T(8,128)S(1)}, f32[97,8,128]{2,1,0:T(8,128)S(1)}, u32[]{:S(2)}, u32[]{:S(2)}) collective-permute-start(f32[97,8,128]{2,1,0:T(8,128)S(1)} %get-tuple-element.42), channel_id=1, source_target_pairs={{0,1},{1,0},{2,3},{3,2},{4,8},{5,9},{6,10},{7,11},{8,4},{9,5},{10,... | collective-permute-start | bytes 1191944 | tf_op jit(solution)/shard_map/ppermute | solution.py:72
  27.1 8.8 %collective-permute-start.8 = (f32[392,128]{1,0:T(8,128)S(1)}, f32[392,128]{1,0:T(8,128)S(1)}, u32[]{:S(2)}, u32[]{:S(2)}) collective-permute-start(f32[392,128]{1,0:T(8,128)S(1)} %get-tuple-element.50), channel_id=1, source_target_pairs={{1,2},{2,1},{3,0},{0,3},{5,6},{6,5},{7,4},{4,7},{9,10},{10,9},{11,... | collective-permute-start | bytes 602120 | tf_op jit(solution)/shard_map/ppermute | solution.py:81
  27.5 8.4 %collective-permute-start.9 = (f32[392,128]{1,0:T(8,128)S(1)}, f32[392,128]{1,0:T(8,128)S(1)}, u32[]{:S(2)}, u32[]{:S(2)}) collective-permute-start(f32[392,128]{1,0:T(8,128)S(1)} %get-tuple-element.51), channel_id=1, source_target_pairs={{0,1},{1,0},{2,3},{3,2},{4,5},{5,4},{6,7},{7,6},{8,9},{9,8},{10,11... | collective-permute-start | bytes 602120 | tf_op jit(solution)/shard_map/ppermute | solution.py:81
  31.9 4.0 %copy-start.7 = (s32[6,1,1,1]{0,3,2,1:T(1,128)S(1)}, s32[6,1,1,1]{0,3,2,1:T(1,128)}, u32[]{:S(2)}) copy-start(s32[6,1,1,1]{0,3,2,1:T(1,128)} %param.9) | copy-start | bytes 76
  37.5 8.8 %collective-permute-start.10 = (f32[392,128]{1,0:T(8,128)S(1)}, f32[392,128]{1,0:T(8,128)S(1)}, u32[]{:S(2)}, u32[]{:S(2)}) collective-permute-start(f32[392,128]{1,0:T(8,128)S(1)} %get-tuple-element.52), channel_id=1, source_target_pairs={{0,1},{1,0},{2,3},{3,2},{4,5},{5,4},{6,7},{7,6},{8,9},{9,8},{10,11... | collective-permute-start | bytes 602120 | tf_op jit(solution)/shard_map/ppermute | solution.py:81
  37.7 8.6 %collective-permute-start.11 = (f32[392,128]{1,0:T(8,128)S(1)}, f32[392,128]{1,0:T(8,128)S(1)}, u32[]{:S(2)}, u32[]{:S(2)}) collective-permute-start(f32[392,128]{1,0:T(8,128)S(1)} %get-tuple-element.53), channel_id=1, source_target_pairs={{1,2},{2,1},{3,0},{0,3},{5,6},{6,5},{7,4},{4,7},{9,10},{10,9},{11,... | collective-permute-start | bytes 602120 | tf_op jit(solution)/shard_map/ppermute | solution.py:81
  42.1 11.7 %collective-permute-start.12 = (f32[46,16,128]{2,1,0:T(8,128)S(1)}, f32[46,16,128]{2,1,0:T(8,128)S(1)}, u32[]{:S(2)}, u32[]{:S(2)}) collective-permute-start(f32[46,16,128]{2,1,0:T(8,128)S(1)} %get-tuple-element.58), channel_id=1, source_target_pairs={{0,4},{1,5},{2,6},{3,7},{4,0},{5,1},{6,2},{7,3},{8,12},{9,13},{10,... | collective-permute-start | bytes 1130504 | tf_op jit(solution)/shard_map/ppermute | solution.py:72
  42.2 13.7 %collective-permute-start.13 = (f32[46,16,128]{2,1,0:T(8,128)S(1)}, f32[46,16,128]{2,1,0:T(8,128)S(1)}, u32[]{:S(2)}, u32[]{:S(2)}) collective-permute-start(f32[46,16,128]{2,1,0:T(8,128)S(1)} %get-tuple-element.59), channel_id=1, source_target_pairs={{0,1},{1,0},{2,3},{3,2},{4,8},{5,9},{6,10},{7,11},{8,4},{9,5},{10,... | collective-permute-start | bytes 1130504 | tf_op jit(solution)/shard_map/ppermute | solution.py:72
  49.1 12.4 %copy-start.3 = (f32[16,16,128]{2,1,0:T(8,128)S(1)}, f32[16,16,128]{2,1,0:T(8,128)}, u32[]{:S(2)}) copy-start(f32[16,16,128]{2,1,0:T(8,128)} %estimate.1) | copy-start | bytes 393220
  49.1 7.9 %collective-permute-start.14 = (f32[23,16,128]{2,1,0:T(8,128)S(1)}, f32[23,16,128]{2,1,0:T(8,128)S(1)}, u32[]{:S(2)}, u32[]{:S(2)}) collective-permute-start(f32[23,16,128]{2,1,0:T(8,128)S(1)} %get-tuple-element.62), channel_id=1, source_target_pairs={{0,4},{1,5},{2,6},{3,7},{4,0},{5,1},{6,2},{7,3},{8,12},{9,13},{10,... | collective-permute-start | bytes 565256 | tf_op jit(solution)/shard_map/ppermute | solution.py:72
  49.2 9.9 %collective-permute-start.15 = (f32[23,16,128]{2,1,0:T(8,128)S(1)}, f32[23,16,128]{2,1,0:T(8,128)S(1)}, u32[]{:S(2)}, u32[]{:S(2)}) collective-permute-start(f32[23,16,128]{2,1,0:T(8,128)S(1)} %get-tuple-element.63), channel_id=1, source_target_pairs={{0,1},{1,0},{2,3},{3,2},{4,8},{5,9},{6,10},{7,11},{8,4},{9,5},{10,... | collective-permute-start | bytes 565256 | tf_op jit(solution)/shard_map/ppermute | solution.py:72
  59.3 5.1 %collective-permute-start.16 = (f32[16,16,128]{2,1,0:T(8,128)S(1)}, f32[16,16,128]{2,1,0:T(8,128)S(1)}, u32[]{:S(2)}, u32[]{:S(2)}) collective-permute-start(f32[16,16,128]{2,1,0:T(8,128)S(1)} %get-tuple-element.65), channel_id=1, source_target_pairs={{0,32},{1,33},{2,34},{3,35},{32,0},{33,1},{34,2},{35,3},{64,96},{6... | collective-permute-start | bytes 393224 | tf_op jit(solution)/shard_map/ppermute | solution.py:72
  59.4 7.2 %collective-permute-start.17 = (f32[16,16,128]{2,1,0:T(8,128)S(1)}, f32[16,16,128]{2,1,0:T(8,128)S(1)}, u32[]{:S(2)}, u32[]{:S(2)}) collective-permute-start(f32[16,16,128]{2,1,0:T(8,128)S(1)} %get-tuple-element.66), channel_id=1, source_target_pairs={{0,1},{1,0},{2,3},{3,2},{32,64},{33,65},{34,66},{35,67},{64,32},{6... | collective-permute-start | bytes 393224 | tf_op jit(solution)/shard_map/ppermute | solution.py:72

commit v4 on v3

--- a/solution.py
+++ b/solution.py
@@ -94,10 +94,9 @@
     return high, (block - high.astype(F32)).astype(BF16)
 
 
-def pack_planes(cover, own, raw, held, up, down, flags, sem):
+def pack_planes(cover, raw, up, down, flags, sem):
     tag = pltpu.make_async_copy(cover, flags, sem)
     tag.start()
-    held[C - 1 : 2 * C - 1] = own[...]
     for view in range(V):
         at = slice(view * OFF, (view + 1) * OFF)
         up[at] = jnp.where(even("bx"), raw[view, OFF:], raw[view, :OFF])
@@ -111,7 +110,7 @@
 
 def build(
     offsets, psf, after, norm, table, fan_in, fan_out, fan_pair,
-    forward_z, backward_z,
+    forward_z, backward_z, rest_z,
 ):
     norm[...] = jnp.zeros((3, 8, Z), F32)
     for view in range(V):
@@ -132,7 +131,8 @@
         row = jnp.broadcast_to(row, (2 * Z, 2 * Z))
         band = pltpu.roll(row, 2 * Z - R, 1, stride=1, stride_axis=0)
         band = pltpu.roll(band, lax.rem(2 * Z - offsets[2, view], 2 * Z), 1)
-        backward_z[view] = band[:, :Z]
+        backward_z[view] = band[:Z, :Z]
+        rest_z[view] = pltpu.roll(band[Z:, :Z], 32 + 64 * (view % 2), 1)
         forward_z[view] = band[:Z, :].T
     def side_by_side(*parts):
         total = None
@@ -153,10 +153,13 @@
         out[W:] = side_by_side((0, low), (V * C, low))
 
 
-def join_planes(held, low, high, wide):
+def join_planes(own, low, high, wide, sem):
+    copy = pltpu.make_async_copy(own, wide.at[pl.ds(C - 1, C)], sem)
+    copy.start()
     low, high = choose("bx", low[...], high[...])
     wide[: C - 1] = low[1:]
     wide[2 * C - 1 :] = high[: C - 1]
+    copy.wait()
 
 
 def pack_lanes(block, first):
@@ -191,8 +194,7 @@
         planes[2 * pair] = both[:, :Z]
         planes[2 * pair + 1] = both[:, Z:]
 
-    @pl.loop(0, V)
-    def _(view):
+    for view in range(V):
         taps = [table[view, t] for t in range(K)]
         for half in range(2):
             sums = [None] * C
@@ -318,9 +320,8 @@
 def back_own(
     table, fan_out, backward_z, ratio, first, out_mid, second, planes
 ):
-    @pl.loop(0, V)
-    def _(view):
-        back = dot(ratio[view].reshape(C * C, Z), backward_z[view, :Z])
+    for view in range(V):
+        back = dot(ratio[view].reshape(C * C, Z), backward_z[view])
         back = back.reshape(C, C, Z)
         taps = [table[view, t] for t in range(K)]
         for half in range(2):
@@ -339,29 +340,23 @@
 
 
 def back_rest(
-    table, fan_pair, backward_z, far, near, after, out_first, out_mid, out_second, planes
+    table, fan_pair, rest_z, far, near, after, out_first, out_mid, out_second, planes
 ):
     lane = lanes(8)
-    half = lanes(W) < 64
-
-    @pl.loop(0, V // 2)
-    def _(pair):
-        parts = []
-        for odd in range(2):
-            view = 2 * pair + odd
-            block = sides(near, far, view)
-            block = dot(block, backward_z[view, Z:])
-            parts.append(pltpu.roll(block, 32 + 64 * odd, 1).reshape(C, C, Z))
+    front = lanes(W) < 64
+
+    for pair in range(V // 2):
+        block = [sides(near, far, 2 * pair + odd) for odd in range(2)]
+        bands = [rest_z[2 * pair + odd] for odd in range(2)]
+        back = dot(jnp.concatenate(block, axis=1), jnp.concatenate(bands, axis=0))
+        back = back.reshape(C, C, Z)
         taps = [
             jnp.where(lane < 64, table[2 * pair, t], table[2 * pair + 1, t])
             for t in range(K)
         ]
         for half in range(2):
             rows = slice(8 * half, 8 * half + 8)
-            source = [
-                jnp.where(lane < 64, parts[0][i, rows], parts[1][i, rows])
-                for i in range(C)
-            ]
+            source = [back[i, rows] for i in range(C)]
             spread(source, taps, planes, pair * C + 8 * half)
 
     planes[N] = jnp.zeros((W, Z), F32)
@@ -370,8 +365,8 @@
     def fold(a):
         first, second = planes[a], planes[a + 1]
         turned, other = pltpu.roll(first, 64, 1), pltpu.roll(second, 64, 1)
-        even_rows = jnp.where(half, first, other)
-        odd_rows = jnp.where(half, turned, second)
+        even_rows = jnp.where(front, first, other)
+        odd_rows = jnp.where(front, turned, second)
         return jnp.concatenate([even_rows, odd_rows], axis=0)
 
     for quad in range(W // 4):
@@ -412,7 +407,7 @@
     return jnp.where(which == 0, before, jnp.where(which == 2, after, 1.0 - before - after))
 
 
-def weigh(norm, estimate, marks, near_marks, far_marks, scale):
+def weigh(norm, estimate, marks, far_marks, near_marks, scale):
     has_low, has_high = edges("bz")
     tap = lax.broadcasted_iota(jnp.int32, (Z, Z), 0)
     cell = lax.broadcasted_iota(jnp.int32, (Z, Z), 1)
@@ -463,19 +458,23 @@
 
     left = trade(estimate, "bx", 0)
     right = trade(estimate, "bx", 1)
-    held, up, down = call(
+    up, down = call(
         pack_planes,
-        [(N, C, Z)] + [(V * OFF + 1, C, Z)] * 2,
-        [HBM, VM, VM],
+        [(V * OFF + 1, C, Z)] * 2,
+        [HBM, VM],
         [pltpu.SMEM((V,), jnp.int32), pltpu.SemaphoreType.DMA],
         moved=3 << 19,
-    )(cover, estimate, raw)
+    )(cover, raw)
     raw_low = trade(up, "bx", 0)
     raw_high = trade(down, "bx", 1)
-    (wide,) = call(join_planes, [(N, C, Z)], [VM] * 3, alias={0: 0}, moved=1 << 18)(
-        held, left, right
-    )
-    norm, table, fan_in, fan_out, fan_pair, forward_z, backward_z = call(
+    (wide,) = call(
+        join_planes,
+        [(N, C, Z)],
+        [HBM, VM, VM],
+        [pltpu.SemaphoreType.DMA],
+        moved=1 << 18,
+    )(estimate, left, right)
+    norm, table, fan_in, fan_out, fan_pair, forward_z, backward_z, rest_z = call(
         build,
         [
             (3, 8, Z),
@@ -484,7 +483,8 @@
             jax.ShapeDtypeStruct((2 * W, 2 * Z), BF16),
             jax.ShapeDtypeStruct((2 * W, 2 * Z), BF16),
             (V, 2 * Z, Z),
-            (V, 2 * Z, Z),
+            (V, Z, Z),
+            (V, Z, Z),
         ],
         [SM, VM, ANY],
         moved=1 << 23,
@@ -554,13 +554,13 @@
         [pltpu.VMEM((W, W, Z), F32)],
         flops=1 << 34,
         moved=1 << 26,
-    )(table, fan_pair, backward_z, far, near, out_mid)
+    )(table, fan_pair, rest_z, far, near, out_mid)
     more_low = trade(rest_first, "by", 0)
     more_high = trade(rest_second, "by", 1)
     last = pl.BlockSpec((8, Z), lambda i: (8 * V, 0))
     (scale,) = call(
         weigh, [(C, C, Z)], [VM, VM, VM, last, last], grid=(1,), moved=1 << 19
-    )(norm, estimate, marks, near, far)
+    )(norm, estimate, marks, far, near)
     out_mid, first, second = call(
         add_rows,
         [(C, C, Z)] * 3,

time: 67.9 us -> 66.4 us (0.978)
  Pallas kernels: 17.7 us -> 15.5 us
  local copies, waits for them, and re-layouts: 2.71 us -> 4.1 us
  waiting for transfers between devices: 20.4 us -> 19.2 us
  starting transfers between devices: 26.2 us -> 27.2 us
    unnamed x16 -> x18, local copies, waits for them, and re-layouts: 2.71 us -> 4.1 us
    ppermute x14, starting transfers between devices: 22 us -> 23.1 us  [trade(): return lax.ppermute(block, (axis, 'bz'), pairs)]
    pallas_call x1, Pallas kernels: 2.74 us -> 1.61 us  [on_device(): call(back_rest, [(N // 2, C, Z)] * 3, [VM] * 5 + [ANY], [pltpu.VMEM((W, W...]
    ppermute x14, waiting for transfers between devices: 16.9 us -> 15.8 us  [trade(): return lax.ppermute(block, (axis, 'bz'), pairs)]
    pallas_call x1, Pallas kernels: 3.41 us -> 2.42 us  [on_device(): call(back_own, [(N, C, Z)] * 3, [VM] * 4, [pltpu.VMEM((N, V * C, Z), F32)...]
  transfers between devices with their start and end apart: 18 -> 18, of which waited for: 10 -> 9; matrix products, arithmetic and copies ran while one was open for 0% -> 0% of each run, Pallas kernels for 23% -> 20%
where the time goes in v4:
time: 66.4 us; the launch traced here: 66.2 us
  starting transfers between devices  27.2 us (41%)
  waiting for transfers between devices  19.2 us (29%)
  Pallas kernels  15.5 us (23%)
  local copies, waits for them, and re-layouts  4.1 us (6%)
    ppermute x14, starting transfers between devices, trade(): return lax.ppermute(block, (axis, 'bz'), pairs)  23.1 us
    ppermute x14, waiting for transfers between devices, trade(): return lax.ppermute(block, (axis, 'bz'), pairs)  15.8 us
    ppermute x4, starting transfers between devices, swap(): return lax.ppermute(block, 'bz', pairs)  4.1 us
    unnamed x18, local copies, waits for them, and re-layouts  4.1 us
    ppermute x4, waiting for transfers between devices, swap(): return lax.ppermute(block, 'bz', pairs)  3.33 us
    pallas_call x1, Pallas kernels, on_device(): call(forward, [full, (64 * V + 8, Z), (64 * V + 8, Z)], [VM] * 5 + [SM, A...  2.85 us
    pallas_call x1, Pallas kernels, on_device(): call(back_own, [(N, C, Z)] * 3, [VM] * 4, [pltpu.VMEM((N, V * C, Z), F32)...  2.42 us
    pallas_call x1, Pallas kernels, on_device(): call(build, [(3, 8, Z), (V, K, 8, Z), jax.ShapeDtypeStruct((V * C, 2 * Z)...  2.23 us
  transfers between devices with their start and end apart: 18, of which 9 were waited for; matrix products, arithmetic and copies ran while one was open for 0% of the time, Pallas kernels for 20%

profile of v4, /device:TPU:38, one launch (start us, length us, event | category | flops | bytes accessed | tf_op | source)
XLA Modules:
  0.0 66.2 jit_solution(5974911464503220177)
XLA Ops:
  0.0 0.0 copy-start.8
  0.0 1.5 %collective-permute-start.1 = (f32[16,16,128]{2,1,0:T(8,128)}, f32[16,16,128]{2,1,0:T(8,128)S(1)}, u32[]{:S(2)}, u32[]{:S(2)}) collective-permute-start(f32[16,16,128]{2,1,0:T(8,128)} %estimate.1), channel_id=1, source_target_pairs={{0,1},{1,0},{2,3},{3,2},{32,64},{33,65},{34,66},{35,67},{64,32},{6... | collective-permute-start | bytes 393224 | tf_op jit(solution)/shard_map/ppermute | solution.py:72
  1.5 0.0 collective-permute-start
  1.5 0.0 copy-start
  1.5 1.1 %copy-done = f32[6,16,16,128]{3,2,1,0:T(8,128)S(1)} copy-done((f32[6,16,16,128]{3,2,1,0:T(8,128)S(1)}, f32[6,16,16,128]{3,2,1,0:T(8,128)}, u32[]{:S(2)}) %copy-start) | copy-done | bytes 786456
  2.6 0.0 copy-start.7
  2.6 0.7 copy-done.7
  3.3 0.0 copy-start.1
  3.3 0.6 shard_map.57
  3.9 2.1 %collective-permute-start.2 = (f32[49,16,128]{2,1,0:T(8,128)S(1)}, f32[49,16,128]{2,1,0:T(8,128)S(1)}, u32[]{:S(2)}, u32[]{:S(2)}) collective-permute-start(f32[49,16,128]{2,1,0:T(8,128)S(1)} %get-tuple-element.37), channel_id=1, source_target_pairs={{0,32},{1,33},{2,34},{3,35},{32,0},{33,1},{34,2},{35,3},{64,96},{6... | collective-permute-start | bytes 1204232 | tf_op jit(solution)/shard_map/ppermute | solution.py:72
  6.0 2.6 %collective-permute-start.3 = (f32[49,16,128]{2,1,0:T(8,128)S(1)}, f32[49,16,128]{2,1,0:T(8,128)S(1)}, u32[]{:S(2)}, u32[]{:S(2)}) collective-permute-start(f32[49,16,128]{2,1,0:T(8,128)S(1)} %get-tuple-element.38), channel_id=1, source_target_pairs={{0,1},{1,0},{2,3},{3,2},{32,64},{33,65},{34,66},{35,67},{64,32},{6... | collective-permute-start | bytes 1204232 | tf_op jit(solution)/shard_map/ppermute | solution.py:72
  8.6 0.0 collective-permute-done.1.high
  8.6 0.0 collective-permute-done.low
  8.6 0.0 copy-start.2
  8.6 0.9 %copy-done.2 = f32[16,16,128]{2,1,0:T(8,128)S(1)} copy-done((f32[16,16,128]{2,1,0:T(8,128)S(1)}, f32[16,16,128]{2,1,0:T(8,128)}, u32[]{:S(2)}) %copy-start.2) | copy-done | bytes 131096
  9.5 0.2 shard_map.55.after.own
  9.7 2.0 %collective-permute-start.7 = (f32[46,16,128]{2,1,0:T(8,128)S(1)}, f32[46,16,128]{2,1,0:T(8,128)S(1)}, u32[]{:S(2)}, u32[]{:S(2)}) collective-permute-start(f32[46,16,128]{2,1,0:T(8,128)S(1)} %shard_map.55.after.own), channel_id=1, source_target_pairs={{0,1},{1,0},{2,3},{3,2},{4,8},{5,9},{6,10},{7,11},{8,4},{9,5},{10,... | collective-permute-start | bytes 1130504 | tf_op jit(solution)/shard_map/ppermute | solution.py:72
  11.7 0.0 collective-permute-start.6
  11.7 0.7 %copy-done.4 = s32[6,3]{0,1:T(4,128)S(1)} copy-done((s32[6,3]{0,1:T(4,128)S(1)}, s32[6,3]{0,1:T(4,128)}, u32[]{:S(2)}) %copy-start.4) | copy-done | bytes 96
  12.4 0.7 %copy-done.6 = f32[6,3,31]{2,1,0:T(4,128)S(1)} copy-done((f32[6,3,31]{2,1,0:T(4,128)S(1)}, f32[6,3,31]{2,1,0:T(4,128)}, u32[]{:S(2)}) %copy-start.6) | copy-done | bytes 2256
  13.1 2.2 %shard_map.56 = (f32[3,8,128]{2,1,0:T(8,128)S(1)}, f32[6,31,8,128]{3,2,1,0:T(8,128)S(1)}, bf16[96,256]{1,0:T(8,128)(2,1)S(1)}, bf16[96,256]{1,0:T(8,128)(2,1)S(1...) custom-call(s32[3,6]{1,0:T(4,128)S(1)} %bitcast.2, ...), custom_call_target="tpu_custom_call" | custom-call | bytes 8388608 | tf_op jit(solution)/shard_map/pallas_call | solution.py:477
  15.3 0.0 collective-permute-done.2.low
  15.4 2.9 %collective-permute-done.3.high = f32[49,16,128]{2,1,0:T(8,128)S(1)} collective-permute-done((f32[49,16,128]{2,1,0:T(8,128)S(1)}, f32[49,16,128]{2,1,0:T(8,128)S(1)}, u32[]{:S(2)}, u32[]{:S(2)}) %collective-permute-start.3) | collective-permute-done | bytes 401440 | tf_op jit(solution)/shard_map/ppermute | solution.py:72
  18.3 0.0 copy-done.8
  18.3 0.0 copy-done.1
  18.3 0.8 %shard_map.58 = (f32[6,16,32,128]{3,2,1,0:T(8,128)S(1)}, f32[97,8,128]{2,1,0:T(8,128)S(1)}, f32[97,8,128]{2,1,0:T(8,128)S(1)}, f32[8,128]{1,0:T(8,128)S(1)}) custom-call(s32[3,6]{1,0:T(4,128)S(1)} %bitcast.3, s32[6]{0:T(128)S(1)} %bitcast.7, f32[6,16,16,128]{3,2,1,0:T(8,128)S(1)} %copy-done.1, f32[49,16,128]{2,1,0:T(8,128)S(1)} %collective-permute-done.2.low, ...), custom_call_target="tpu_custom_call" | custom-call | bytes 67108864 | tf_op jit(solution)/shard_map/pallas_call | solution.py:495
  19.1 0.2 collective-permute-start.4
  19.3 3.7 %collective-permute-start.5 = (f32[97,8,128]{2,1,0:T(8,128)S(1)}, f32[97,8,128]{2,1,0:T(8,128)S(1)}, u32[]{:S(2)}, u32[]{:S(2)}) collective-permute-start(f32[97,8,128]{2,1,0:T(8,128)S(1)} %get-tuple-element.41), channel_id=1, source_target_pairs={{0,1},{1,0},{2,3},{3,2},{4,8},{5,9},{6,10},{7,11},{8,4},{9,5},{10,... | collective-permute-start | bytes 1191944 | tf_op jit(solution)/shard_map/ppermute | solution.py:72
  23.0 0.0 collective-permute-done.7.high
  23.0 0.0 collective-permute-done.6.low
  23.0 2.8 %shard_map.59 = (f32[6,16,16,128]{3,2,1,0:T(8,128)S(1)}, f32[392,128]{1,0:T(8,128)S(1)}, f32[392,128]{1,0:T(8,128)S(1)}) custom-call(f32[6,31,8,128]{3,2,1,0:T(8,128)S(1)} %get-tuple-element.43.table, bf16[96,256]{1,0:T(8,128)(2,1)S(1)} %get-tuple-element.44.fan_in, f32[46,16,128]{2,1,0:T(8,128)S(1)} %shard_map.55.after.own, ...), custom_call_target="tpu_custom_call" | custom-call | flops 17179869184 | bytes 67108864 | tf_op jit(solution)/shard_map/pallas_call | solution.py:510
  25.9 0.1 collective-permute-start.8
  26.0 3.0 %collective-permute-start.9 = (f32[392,128]{1,0:T(8,128)S(1)}, f32[392,128]{1,0:T(8,128)S(1)}, u32[]{:S(2)}, u32[]{:S(2)}) collective-permute-start(f32[392,128]{1,0:T(8,128)S(1)} %get-tuple-element.50), channel_id=1, source_target_pairs={{0,1},{1,0},{2,3},{3,2},{4,5},{5,4},{6,7},{7,6},{8,9},{9,8},{10,11... | collective-permute-start | bytes 602120 | tf_op jit(solution)/shard_map/ppermute | solution.py:81
  29.0 0.3 collective-permute-done.4.low
  29.3 0.8 %collective-permute-done.5.high = f32[97,8,128]{2,1,0:T(8,128)S(1)} collective-permute-done((f32[97,8,128]{2,1,0:T(8,128)S(1)}, f32[97,8,128]{2,1,0:T(8,128)S(1)}, u32[]{:S(2)}, u32[]{:S(2)}) %collective-permute-start.5) | collective-permute-done | bytes 397344 | tf_op jit(solution)/shard_map/ppermute | solution.py:72
  30.2 0.0 copy-done.5
  30.2 0.7 %shard_map.60 = (f32[6,16,16,128]{3,2,1,0:T(8,128)S(1)}, f32[8,128]{1,0:T(8,128)S(1)}, f32[6,16,32,128]{3,2,1,0:T(8,128)S(1)}) custom-call(s32[3,6]{1,0:T(4,128)S(1)} %bitcast.4, f32[6,16,32,128]{3,2,1,0:T(8,128)S(1)} %get-tuple-element.39.held, f32[97,8,128]{2,1,0:T(8,128)S(1)} %collective-permute-done.4.low, ...), custom_call_target="tpu_custom_call", output_to_operand_aliasing={{2}: (1, {})} | custom-call | bytes 67108864 | tf_op jit(solution)/shard_map/pallas_call | solution.py:520
  30.9 0.5 shard_map.61.model
  31.4 3.3 %collective-permute-done.8.high = f32[392,128]{1,0:T(8,128)S(1)} collective-permute-done((f32[392,128]{1,0:T(8,128)S(1)}, f32[392,128]{1,0:T(8,128)S(1)}, u32[]{:S(2)}, u32[]{:S(2)}) %collective-permute-start.8) | collective-permute-done | bytes 200736 | tf_op jit(solution)/shard_map/ppermute | solution.py:81
  34.7 0.0 collective-permute-done.9.low
  34.7 1.5 %shard_map.62 = (f32[6,16,16,128]{3,2,1,0:T(8,128)S(1)}, f32[392,128]{1,0:T(8,128)S(1)}, f32[392,128]{1,0:T(8,128)S(1)}) custom-call(s32[3,6]{1,0:T(4,128)S(1)} %bitcast.5, s32[6]{0:T(128)S(1)} %bitcast.9, f32[6,256,128]{2,1,0:T(8,128)S(1)} %get-tuple-element.47.forward_z, f32[6,16,16,128]{3,2,1,0:T(8,128)S(1)} %shard_map.61.model, ...), custom_call_target="tpu_custom_call" | custom-call | flops 17179869184 | bytes 67108864 | tf_op jit(solution)/shard_map/pallas_call | solution.py:531
  36.3 0.1 collective-permute-start.10
  36.4 0.9 %collective-permute-start.11 = (f32[392,128]{1,0:T(8,128)S(1)}, f32[392,128]{1,0:T(8,128)S(1)}, u32[]{:S(2)}, u32[]{:S(2)}) collective-permute-start(f32[392,128]{1,0:T(8,128)S(1)} %get-tuple-element.52), channel_id=1, source_target_pairs={{0,1},{1,0},{2,3},{3,2},{4,5},{5,4},{6,7},{7,6},{8,9},{9,8},{10,11... | collective-permute-start | bytes 602120 | tf_op jit(solution)/shard_map/ppermute | solution.py:81
  37.3 2.4 %shard_map.64 = (f32[46,16,128]{2,1,0:T(8,128)S(1)}, f32[46,16,128]{2,1,0:T(8,128)S(1)}, f32[46,16,128]{2,1,0:T(8,128)S(1)}) custom-call(f32[6,31,8,128]{3,2,1,0:T(8,128)S(1)} %get-tuple-element.43.table, bf16[96,256]{1,0:T(8,128)(2,1)S(1)} %get-tuple-element.53.fan_out, f32[6,128,128]{2,1,0:T(8,128)S(1)} %get-tuple-element.54.backward_z, ...), custom_call_target="tpu_custom_call" | custom-call | flops 17179869184 | bytes 67108864 | tf_op jit(solution)/shard_map/pallas_call | solution.py:540
  39.7 1.1 %collective-permute-start.12 = (f32[46,16,128]{2,1,0:T(8,128)S(1)}, f32[46,16,128]{2,1,0:T(8,128)S(1)}, u32[]{:S(2)}, u32[]{:S(2)}) collective-permute-start(f32[46,16,128]{2,1,0:T(8,128)S(1)} %get-tuple-element.57), channel_id=1, source_target_pairs={{0,4},{1,5},{2,6},{3,7},{4,0},{5,1},{6,2},{7,3},{8,12},{9,13},{10,... | collective-permute-start | bytes 1130504 | tf_op jit(solution)/shard_map/ppermute | solution.py:72
  40.8 4.5 %collective-permute-start.13 = (f32[46,16,128]{2,1,0:T(8,128)S(1)}, f32[46,16,128]{2,1,0:T(8,128)S(1)}, u32[]{:S(2)}, u32[]{:S(2)}) collective-permute-start(f32[46,16,128]{2,1,0:T(8,128)S(1)} %get-tuple-element.58), channel_id=1, source_target_pairs={{0,1},{1,0},{2,3},{3,2},{4,8},{5,9},{6,10},{7,11},{8,4},{9,5},{10,... | collective-permute-start | bytes 1130504 | tf_op jit(solution)/shard_map/ppermute | solution.py:72
  45.3 0.0 collective-permute-done.10.far_marks.far
  45.3 0.0 collective-permute-done.11.near_marks.near
  45.3 1.6 %shard_map.65 = (f32[23,16,128]{2,1,0:T(8,128)S(1)}, f32[23,16,128]{2,1,0:T(8,128)S(1)}, f32[23,16,128]{2,1,0:T(8,128)S(1)}) custom-call(f32[6,31,8,128]{3,2,1,0:T(8,128)S(1)} %get-tuple-element.43.table, bf16[96,256]{1,0:T(8,128)(2,1)S(1)} %get-tuple-element.59.fan_pair, f32[6,128,128]{2,1,0:T(8,128)S(1)} %get-tuple-element.60.rest_z, ...), custom_call_target="tpu_custom_call" | custom-call | flops 17179869184 | bytes 67108864 | tf_op jit(solution)/shard_map/pallas_call | solution.py:550
  46.9 0.0 copy-start.3
  47.0 0.1 collective-permute-start.14
  47.1 4.0 %collective-permute-start.15 = (f32[23,16,128]{2,1,0:T(8,128)S(1)}, f32[23,16,128]{2,1,0:T(8,128)S(1)}, u32[]{:S(2)}, u32[]{:S(2)}) collective-permute-start(f32[23,16,128]{2,1,0:T(8,128)S(1)} %get-tuple-element.63), channel_id=1, source_target_pairs={{0,1},{1,0},{2,3},{3,2},{4,8},{5,9},{6,10},{7,11},{8,4},{9,5},{10,... | collective-permute-start | bytes 565256 | tf_op jit(solution)/shard_map/ppermute | solution.py:72
  51.0 0.4 collective-permute-done.12.from_low
  51.4 3.5 %collective-permute-done.13.from_high = f32[46,16,128]{2,1,0:T(8,128)S(1)} collective-permute-done((f32[46,16,128]{2,1,0:T(8,128)S(1)}, f32[46,16,128]{2,1,0:T(8,128)S(1)}, u32[]{:S(2)}, u32[]{:S(2)}) %collective-permute-start.13) | collective-permute-done | bytes 376864 | tf_op jit(solution)/shard_map/ppermute | solution.py:72
  54.9 0.0 collective-permute-done.14.rest_low
  54.9 3.1 %collective-permute-done.15.rest_high = f32[23,16,128]{2,1,0:T(8,128)S(1)} collective-permute-done((f32[23,16,128]{2,1,0:T(8,128)S(1)}, f32[23,16,128]{2,1,0:T(8,128)S(1)}, u32[]{:S(2)}, u32[]{:S(2)}) %collective-permute-start.15) | collective-permute-done | bytes 188448 | tf_op jit(solution)/shard_map/ppermute | solution.py:72
  58.0 0.2 shard_map.66
  58.2 0.1 collective-permute-start.16
  58.3 1.2 %collective-permute-start.17 = (f32[16,16,128]{2,1,0:T(8,128)S(1)}, f32[16,16,128]{2,1,0:T(8,128)S(1)}, u32[]{:S(2)}, u32[]{:S(2)}) collective-permute-start(f32[16,16,128]{2,1,0:T(8,128)S(1)} %get-tuple-element.66), channel_id=1, source_target_pairs={{0,1},{1,0},{2,3},{3,2},{32,64},{33,65},{34,66},{35,67},{64,32},{6... | collective-permute-start | bytes 393224 | tf_op jit(solution)/shard_map/ppermute | solution.py:72
  59.5 0.0 copy-done.3
  59.5 1.2 %shard_map.63.scale = f32[16,16,128]{2,1,0:T(8,128)S(1)} custom-call(f32[3,8,128]{2,1,0:T(8,128)S(1)} %get-tuple-element.36.after.norm, f32[16,16,128]{2,1,0:T(8,128)S(1)} %copy-done.3, f32[8,128]{1,0:T(8,128)S(1)} %get-tuple-element.46.marks, f32[392,128]{1,0:T(8,128)S(1)} %collective-permute-done.10.far_marks.far, ...), custom_call_target="tpu_custom_call" | custom-call | bytes 524288 | tf_op jit(solution)/shard_map/pallas_call | solution.py:561
  60.7 2.5 %collective-permute-done.16.from_low = f32[16,16,128]{2,1,0:T(8,128)S(1)} collective-permute-done((f32[16,16,128]{2,1,0:T(8,128)S(1)}, f32[16,16,128]{2,1,0:T(8,128)S(1)}, u32[]{:S(2)}, u32[]{:S(2)}) %collective-permute-start.16) | collective-permute-done | bytes 131104 | tf_op jit(solution)/shard_map/ppermute | solution.py:72
  63.3 2.2 %collective-permute-done.17.from_high = f32[16,16,128]{2,1,0:T(8,128)S(1)} collective-permute-done((f32[16,16,128]{2,1,0:T(8,128)S(1)}, f32[16,16,128]{2,1,0:T(8,128)S(1)}, u32[]{:S(2)}, u32[]{:S(2)}) %collective-permute-start.17) | collective-permute-done | bytes 131104 | tf_op jit(solution)/shard_map/ppermute | solution.py:72
  65.5 0.7 %shard_map.67 = f32[16,16,128]{2,1,0:T(8,128)} custom-call(f32[16,16,128]{2,1,0:T(8,128)S(1)} %shard_map.63.scale, f32[16,16,128]{2,1,0:T(8,128)S(1)} %get-tuple-element.64.mid, f32[16,16,128]{2,1,0:T(8,128)S(1)} %collective-permute-done.16.from_low, f32[16,16,128]{2,1,0:T(8,128)S(1)} %collective-permute-done.17.from_high), custom_call_target="tpu_custom_call" | custom-call | bytes 786432 | tf_op jit(solution)/shard_map/pallas_call | solution.py:573
  (3 shorter events, 0.0 us)
Async XLA Ops:
  0.0 18.3 %copy-start.8 = (s32[6,1,1,1]{0,3,2,1:T(1,128)S(1)}, s32[6,1,1,1]{0,3,2,1:T(1,128)}, u32[]{:S(2)}) copy-start(s32[6,1,1,1]{0,3,2,1:T(1,128)} %param.9) | copy-start | bytes 76
  0.0 8.6 %collective-permute-start.1 = (f32[16,16,128]{2,1,0:T(8,128)}, f32[16,16,128]{2,1,0:T(8,128)S(1)}, u32[]{:S(2)}, u32[]{:S(2)}) collective-permute-start(f32[16,16,128]{2,1,0:T(8,128)} %estimate.1), channel_id=1, source_target_pairs={{0,1},{1,0},{2,3},{3,2},{32,64},{33,65},{34,66},{35,67},{64,32},{6... | collective-permute-start | bytes 393224 | tf_op jit(solution)/shard_map/ppermute | solution.py:72
  1.5 7.1 %collective-permute-start = (f32[16,16,128]{2,1,0:T(8,128)}, f32[16,16,128]{2,1,0:T(8,128)S(1)}, u32[]{:S(2)}, u32[]{:S(2)}) collective-permute-start(f32[16,16,128]{2,1,0:T(8,128)} %estimate.1), channel_id=1, source_target_pairs={{0,32},{1,33},{2,34},{3,35},{32,0},{33,1},{34,2},{35,3},{64,96},{6... | collective-permute-start | bytes 393224 | tf_op jit(solution)/shard_map/ppermute | solution.py:72
  1.5 1.1 %copy-start = (f32[6,16,16,128]{3,2,1,0:T(8,128)S(1)}, f32[6,16,16,128]{3,2,1,0:T(8,128)}, u32[]{:S(2)}) copy-start(f32[6,16,16,128]{3,2,1,0:T(8,128)} %raw.3) | copy-start | bytes 2359300
  2.6 0.7 copy-start.7
  3.3 15.0 %copy-start.1 = (f32[6,16,16,128]{3,2,1,0:T(8,128)S(1)}, f32[6,16,16,128]{3,2,1,0:T(8,128)}, u32[]{:S(2)}) copy-start(f32[6,16,16,128]{3,2,1,0:T(8,128)} %raw.3) | copy-start | bytes 2359300
  3.9 11.5 %collective-permute-start.2 = (f32[49,16,128]{2,1,0:T(8,128)S(1)}, f32[49,16,128]{2,1,0:T(8,128)S(1)}, u32[]{:S(2)}, u32[]{:S(2)}) collective-permute-start(f32[49,16,128]{2,1,0:T(8,128)S(1)} %get-tuple-element.37), channel_id=1, source_target_pairs={{0,32},{1,33},{2,34},{3,35},{32,0},{33,1},{34,2},{35,3},{64,96},{6... | collective-permute-start | bytes 1204232 | tf_op jit(solution)/shard_map/ppermute | solution.py:72
  6.0 12.3 %collective-permute-start.3 = (f32[49,16,128]{2,1,0:T(8,128)S(1)}, f32[49,16,128]{2,1,0:T(8,128)S(1)}, u32[]{:S(2)}, u32[]{:S(2)}) collective-permute-start(f32[49,16,128]{2,1,0:T(8,128)S(1)} %get-tuple-element.38), channel_id=1, source_target_pairs={{0,1},{1,0},{2,3},{3,2},{32,64},{33,65},{34,66},{35,67},{64,32},{6... | collective-permute-start | bytes 1204232 | tf_op jit(solution)/shard_map/ppermute | solution.py:72
  8.6 0.9 %copy-start.2 = (f32[16,16,128]{2,1,0:T(8,128)S(1)}, f32[16,16,128]{2,1,0:T(8,128)}, u32[]{:S(2)}) copy-start(f32[16,16,128]{2,1,0:T(8,128)} %estimate.1) | copy-start | bytes 393220
  9.7 13.3 %collective-permute-start.7 = (f32[46,16,128]{2,1,0:T(8,128)S(1)}, f32[46,16,128]{2,1,0:T(8,128)S(1)}, u32[]{:S(2)}, u32[]{:S(2)}) collective-permute-start(f32[46,16,128]{2,1,0:T(8,128)S(1)} %shard_map.55.after.own), channel_id=1, source_target_pairs={{0,1},{1,0},{2,3},{3,2},{4,8},{5,9},{6,10},{7,11},{8,4},{9,5},{10,... | collective-permute-start | bytes 1130504 | tf_op jit(solution)/shard_map/ppermute | solution.py:72
  11.7 11.3 %collective-permute-start.6 = (f32[46,16,128]{2,1,0:T(8,128)S(1)}, f32[46,16,128]{2,1,0:T(8,128)S(1)}, u32[]{:S(2)}, u32[]{:S(2)}) collective-permute-start(f32[46,16,128]{2,1,0:T(8,128)S(1)} %shard_map.55.after.own), channel_id=1, source_target_pairs={{0,4},{1,5},{2,6},{3,7},{4,0},{5,1},{6,2},{7,3},{8,12},{9,13},{10,... | collective-permute-start | bytes 1130504 | tf_op jit(solution)/shard_map/ppermute | solution.py:72
  11.7 0.7 %copy-start.4 = (s32[6,3]{0,1:T(4,128)S(1)}, s32[6,3]{0,1:T(4,128)}, u32[]{:S(2)}) copy-start(s32[6,3]{0,1:T(4,128)} %param.8) | copy-start | bytes 220
  12.4 0.7 %copy-start.6 = (f32[6,3,31]{2,1,0:T(4,128)S(1)}, f32[6,3,31]{2,1,0:T(4,128)}, u32[]{:S(2)}) copy-start(f32[6,3,31]{2,1,0:T(4,128)} %psf.1) | copy-start | bytes 6700
  19.1 10.2 %collective-permute-start.4 = (f32[97,8,128]{2,1,0:T(8,128)S(1)}, f32[97,8,128]{2,1,0:T(8,128)S(1)}, u32[]{:S(2)}, u32[]{:S(2)}) collective-permute-start(f32[97,8,128]{2,1,0:T(8,128)S(1)} %get-tuple-element.40), channel_id=1, source_target_pairs={{0,4},{1,5},{2,6},{3,7},{4,0},{5,1},{6,2},{7,3},{8,12},{9,13},{10,... | collective-permute-start | bytes 1191944 | tf_op jit(solution)/shard_map/ppermute | solution.py:72
  19.3 10.9 %collective-permute-start.5 = (f32[97,8,128]{2,1,0:T(8,128)S(1)}, f32[97,8,128]{2,1,0:T(8,128)S(1)}, u32[]{:S(2)}, u32[]{:S(2)}) collective-permute-start(f32[97,8,128]{2,1,0:T(8,128)S(1)} %get-tuple-element.41), channel_id=1, source_target_pairs={{0,1},{1,0},{2,3},{3,2},{4,8},{5,9},{6,10},{7,11},{8,4},{9,5},{10,... | collective-permute-start | bytes 1191944 | tf_op jit(solution)/shard_map/ppermute | solution.py:72
  23.0 7.2 %copy-start.5 = (s32[6,3]{0,1:T(4,128)S(1)}, s32[6,3]{0,1:T(4,128)}, u32[]{:S(2)}) copy-start(s32[6,3]{0,1:T(4,128)} %param.8) | copy-start | bytes 220
  25.9 8.8 %collective-permute-start.8 = (f32[392,128]{1,0:T(8,128)S(1)}, f32[392,128]{1,0:T(8,128)S(1)}, u32[]{:S(2)}, u32[]{:S(2)}) collective-permute-start(f32[392,128]{1,0:T(8,128)S(1)} %get-tuple-element.49), channel_id=1, source_target_pairs={{1,2},{2,1},{3,0},{0,3},{5,6},{6,5},{7,4},{4,7},{9,10},{10,9},{11,... | collective-permute-start | bytes 602120 | tf_op jit(solution)/shard_map/ppermute | solution.py:81
  26.0 8.7 %collective-permute-start.9 = (f32[392,128]{1,0:T(8,128)S(1)}, f32[392,128]{1,0:T(8,128)S(1)}, u32[]{:S(2)}, u32[]{:S(2)}) collective-permute-start(f32[392,128]{1,0:T(8,128)S(1)} %get-tuple-element.50), channel_id=1, source_target_pairs={{0,1},{1,0},{2,3},{3,2},{4,5},{5,4},{6,7},{7,6},{8,9},{9,8},{10,11... | collective-permute-start | bytes 602120 | tf_op jit(solution)/shard_map/ppermute | solution.py:81
  36.3 9.1 %collective-permute-start.10 = (f32[392,128]{1,0:T(8,128)S(1)}, f32[392,128]{1,0:T(8,128)S(1)}, u32[]{:S(2)}, u32[]{:S(2)}) collective-permute-start(f32[392,128]{1,0:T(8,128)S(1)} %get-tuple-element.51), channel_id=1, source_target_pairs={{1,2},{2,1},{3,0},{0,3},{5,6},{6,5},{7,4},{4,7},{9,10},{10,9},{11,... | collective-permute-start | bytes 602120 | tf_op jit(solution)/shard_map/ppermute | solution.py:81
  36.4 9.0 %collective-permute-start.11 = (f32[392,128]{1,0:T(8,128)S(1)}, f32[392,128]{1,0:T(8,128)S(1)}, u32[]{:S(2)}, u32[]{:S(2)}) collective-permute-start(f32[392,128]{1,0:T(8,128)S(1)} %get-tuple-element.52), channel_id=1, source_target_pairs={{0,1},{1,0},{2,3},{3,2},{4,5},{5,4},{6,7},{7,6},{8,9},{9,8},{10,11... | collective-permute-start | bytes 602120 | tf_op jit(solution)/shard_map/ppermute | solution.py:81
  39.7 11.7 %collective-permute-start.12 = (f32[46,16,128]{2,1,0:T(8,128)S(1)}, f32[46,16,128]{2,1,0:T(8,128)S(1)}, u32[]{:S(2)}, u32[]{:S(2)}) collective-permute-start(f32[46,16,128]{2,1,0:T(8,128)S(1)} %get-tuple-element.57), channel_id=1, source_target_pairs={{0,4},{1,5},{2,6},{3,7},{4,0},{5,1},{6,2},{7,3},{8,12},{9,13},{10,... | collective-permute-start | bytes 1130504 | tf_op jit(solution)/shard_map/ppermute | solution.py:72
  40.8 14.1 %collective-permute-start.13 = (f32[46,16,128]{2,1,0:T(8,128)S(1)}, f32[46,16,128]{2,1,0:T(8,128)S(1)}, u32[]{:S(2)}, u32[]{:S(2)}) collective-permute-start(f32[46,16,128]{2,1,0:T(8,128)S(1)} %get-tuple-element.58), channel_id=1, source_target_pairs={{0,1},{1,0},{2,3},{3,2},{4,8},{5,9},{6,10},{7,11},{8,4},{9,5},{10,... | collective-permute-start | bytes 1130504 | tf_op jit(solution)/shard_map/ppermute | solution.py:72
  46.9 12.5 %copy-start.3 = (f32[16,16,128]{2,1,0:T(8,128)S(1)}, f32[16,16,128]{2,1,0:T(8,128)}, u32[]{:S(2)}) copy-start(f32[16,16,128]{2,1,0:T(8,128)} %estimate.1) | copy-start | bytes 393220
  47.0 8.0 %collective-permute-start.14 = (f32[23,16,128]{2,1,0:T(8,128)S(1)}, f32[23,16,128]{2,1,0:T(8,128)S(1)}, u32[]{:S(2)}, u32[]{:S(2)}) collective-permute-start(f32[23,16,128]{2,1,0:T(8,128)S(1)} %get-tuple-element.62), channel_id=1, source_target_pairs={{0,4},{1,5},{2,6},{3,7},{4,0},{5,1},{6,2},{7,3},{8,12},{9,13},{10,... | collective-permute-start | bytes 565256 | tf_op jit(solution)/shard_map/ppermute | solution.py:72
  47.1 11.0 %collective-permute-start.15 = (f32[23,16,128]{2,1,0:T(8,128)S(1)}, f32[23,16,128]{2,1,0:T(8,128)S(1)}, u32[]{:S(2)}, u32[]{:S(2)}) collective-permute-start(f32[23,16,128]{2,1,0:T(8,128)S(1)} %get-tuple-element.63), channel_id=1, source_target_pairs={{0,1},{1,0},{2,3},{3,2},{4,8},{5,9},{6,10},{7,11},{8,4},{9,5},{10,... | collective-permute-start | bytes 565256 | tf_op jit(solution)/shard_map/ppermute | solution.py:72
  58.2 5.1 %collective-permute-start.16 = (f32[16,16,128]{2,1,0:T(8,128)S(1)}, f32[16,16,128]{2,1,0:T(8,128)S(1)}, u32[]{:S(2)}, u32[]{:S(2)}) collective-permute-start(f32[16,16,128]{2,1,0:T(8,128)S(1)} %get-tuple-element.65), channel_id=1, source_target_pairs={{0,32},{1,33},{2,34},{3,35},{32,0},{33,1},{34,2},{35,3},{64,96},{6... | collective-permute-start | bytes 393224 | tf_op jit(solution)/shard_map/ppermute | solution.py:72
  58.3 7.2 %collective-permute-start.17 = (f32[16,16,128]{2,1,0:T(8,128)S(1)}, f32[16,16,128]{2,1,0:T(8,128)S(1)}, u32[]{:S(2)}, u32[]{:S(2)}) collective-permute-start(f32[16,16,128]{2,1,0:T(8,128)S(1)} %get-tuple-element.66), channel_id=1, source_target_pairs={{0,1},{1,0},{2,3},{3,2},{32,64},{33,65},{34,66},{35,67},{64,32},{6... | collective-permute-start | bytes 393224 | tf_op jit(solution)/shard_map/ppermute | solution.py:72

commit v5 on v4

--- a/solution.py
+++ b/solution.py
@@ -73,12 +73,14 @@
 
 
 def swap(block, first):
-    count = lax.axis_size("bz")
+    count, depth = lax.axis_size("by"), lax.axis_size("bz")
     pairs = []
-    for i in range(first, count, 2):
-        a, b = i % count, (i + 1) % count
-        pairs += [(a, b), (b, a)]
-    return lax.ppermute(block, "bz", pairs)
+    for x in range(count):
+        for z in range(depth):
+            to = z + 1 if (z - first) % 2 == 0 else z - 1
+            target = x * depth + to if 0 <= to < depth else (x ^ 1) * depth + z
+            pairs.append((x * depth + z, target))
+    return lax.ppermute(block, ("by", "bz"), pairs)
 
 
 def lanes(rows):
@@ -380,25 +382,24 @@
             put(2 * quad + part, piece, out_first, out_mid, out_second)
 
 
-def add_rows(
-    mid, from_low, from_high, rest, rest_low, rest_high, out_mid, first, second,
-    out_low, out_high,
-):
-    lane = lanes(C)
-    ends = jnp.logical_or(lane < 32, lane >= 96)
+def add_own(mid, from_low, from_high, out_mid, first, second, out_low, out_high):
     out_low[0] = jnp.zeros((C, Z), F32)
     out_high[C - 1] = jnp.zeros((C, Z), F32)
     for a in range(N):
         below, above = choose("by", from_low[a], from_high[a])
-        total = mid[a] + below + above
-        below, above = choose("by", rest_low[a // 2], rest_high[a // 2])
-        more = rest[a // 2] + below + above
-        more = pltpu.roll(more, 32 if a % 2 else 96, 1)
-        total = total + jnp.where(ends, more, 0.0)
         out = (out_low, out_mid, out_high)[(a + 1) // C]
-        out[(a + 1) % C] = total
+        out[(a + 1) % C] = mid[a] + below + above
     first[...] = jnp.where(even("bx"), out_high[...], out_low[...])
     second[...] = jnp.where(even("bx"), out_low[...], out_high[...])
+
+
+def add_rest(rest, from_low, from_high, after, mid, first, second):
+    below, above = choose("by", from_low[...], from_high[...])
+    total = rest[...] + below + above
+    low, high = total[:8], total[15:]
+    mid[...] = total[7:16]
+    first[...] = jnp.where(even("bx"), high, low)
+    second[...] = jnp.where(even("bx"), low, high)
 
 
 def part(tap, cell, count, which):
@@ -445,10 +446,20 @@
         scale[i] = estimate[i] / sums[i]
 
 
-def finish(scale, mid, from_low, from_high, out):
+def finish(scale, mid, from_low, from_high, rest, rest_low, rest_high, out):
     low, high = choose("bx", from_low[...], from_high[...])
-    total = mid[...] + low + high
-    out[...] = scale[...] * total
+    below, above = choose("bx", rest_low[...], rest_high[...])
+    lane = lanes(C)
+    ends = jnp.logical_or(lane < 32, lane >= 96)
+    for x in range(C):
+        n, second = (C - 1 + x) // 2 - 7, (C - 1 + x) % 2
+        more = rest[n]
+        if n < 8:
+            more = more + below[n]
+        if n > 0:
+            more = more + above[n - 1]
+        more = jnp.where(ends, pltpu.roll(more, 32 if second else 96, 1), 0.0)
+        out[x] = scale[x] * (mid[x] + low[x] + high[x] + more)
 
 
 def on_device(estimate, raw, psf, offsets, coverage):
@@ -557,21 +568,30 @@
     )(table, fan_pair, rest_z, far, near, out_mid)
     more_low = trade(rest_first, "by", 0)
     more_high = trade(rest_second, "by", 1)
+    out_mid, first, second = call(
+        add_own,
+        [(C, C, Z)] * 3,
+        [VM] * 3,
+        [pltpu.VMEM((C, C, Z), F32)] * 2,
+        moved=3 << 19,
+    )(out_mid, sum_low, sum_high)
+    sum_low = trade(first, "bx", 0)
+    sum_high = trade(second, "bx", 1)
+    rest_mid, first, second = call(
+        add_rest,
+        [(9, C, Z), (8, C, Z), (8, C, Z)],
+        [VM] * 3 + [ANY],
+        flops=1 << 34,
+        moved=1 << 26,
+    )(rest_mid, more_low, more_high, out_mid)
+    more_low = trade(first, "bx", 0)
+    more_high = trade(second, "bx", 1)
     last = pl.BlockSpec((8, Z), lambda i: (8 * V, 0))
     (scale,) = call(
         weigh, [(C, C, Z)], [VM, VM, VM, last, last], grid=(1,), moved=1 << 19
     )(norm, estimate, marks, far, near)
-    out_mid, first, second = call(
-        add_rows,
-        [(C, C, Z)] * 3,
-        [VM] * 6,
-        [pltpu.VMEM((C, C, Z), F32)] * 2,
-        moved=3 << 19,
-    )(out_mid, sum_low, sum_high, rest_mid, more_low, more_high)
-    sum_low = trade(first, "bx", 0)
-    sum_high = trade(second, "bx", 1)
-    (out,) = call(finish, [(C, C, Z)], [VM] * 4, moved=3 << 18)(
-        scale, out_mid, sum_low, sum_high
+    (out,) = call(finish, [(C, C, Z)], [VM] * 7, moved=3 << 18)(
+        scale, out_mid, sum_low, sum_high, rest_mid, more_low, more_high
     )
     return out
 

time: 66.4 us -> 65.7 us (0.989)
  waiting for transfers between devices: 19.2 us -> 16 us
  starting transfers between devices: 27.2 us -> 29.7 us
    ppermute x4, waiting for transfers between devices: 3.33 us -> 0.29 us  [swap(): return lax.ppermute(block, ('by', 'bz'), pairs)]
    ppermute x4, starting transfers between devices: 4.1 us -> 7.14 us  [swap(): return lax.ppermute(block, ('by', 'bz'), pairs)]
    ppermute x14 -> x16, starting transfers between devices: 23.1 us -> 22.5 us  [trade(): return lax.ppermute(block, (axis, 'bz'), pairs)]
    ppermute x14 -> x16, waiting for transfers between devices: 15.8 us -> 15.7 us  [trade(): return lax.ppermute(block, (axis, 'bz'), pairs)]
  transfers between devices with their start and end apart: 18 -> 20, of which waited for: 9 -> 9; matrix products, arithmetic and copies ran while one was open for 0% -> 0% of each run, Pallas kernels for 20% -> 20%
where the time goes in v5:
time: 65.7 us; the launch traced here: 65.4 us
  starting transfers between devices  29.7 us (45%)
  waiting for transfers between devices  16 us (24%)
  Pallas kernels  15.6 us (24%)
  local copies, waits for them, and re-layouts  4.09 us (6%)
    ppermute x16, starting transfers between devices, trade(): return lax.ppermute(block, (axis, 'bz'), pairs)  22.5 us
    ppermute x16, waiting for transfers between devices, trade(): return lax.ppermute(block, (axis, 'bz'), pairs)  15.7 us
    ppermute x4, starting transfers between devices, swap(): return lax.ppermute(block, ('by', 'bz'), pairs)  7.14 us
    unnamed x18, local copies, waits for them, and re-layouts  4.09 us
    pallas_call x1, Pallas kernels, on_device(): call(forward, [full, (64 * V + 8, Z), (64 * V + 8, Z)], [VM] * 5 + [SM, A...  2.85 us
    pallas_call x1, Pallas kernels, on_device(): call(back_own, [(N, C, Z)] * 3, [VM] * 4, [pltpu.VMEM((N, V * C, Z), F32)...  2.43 us
    pallas_call x1, Pallas kernels, on_device(): call(build, [(3, 8, Z), (V, K, 8, Z), jax.ShapeDtypeStruct((V * C, 2 * Z)...  2.23 us
    pallas_call x1, Pallas kernels, on_device(): call(back_rest, [(N // 2, C, Z)] * 3, [VM] * 5 + [ANY], [pltpu.VMEM((W, W...  1.58 us
  transfers between devices with their start and end apart: 20, of which 9 were waited for; matrix products, arithmetic and copies ran while one was open for 0% of the time, Pallas kernels for 20%

profile of v5, /device:TPU:38, one launch (start us, length us, event | category | flops | bytes accessed | tf_op | source)
XLA Modules:
  0.0 65.4 jit_solution(13633444029834471055)
XLA Ops:
  0.0 0.0 copy-start.8
  0.0 1.5 %collective-permute-start.1 = (f32[16,16,128]{2,1,0:T(8,128)}, f32[16,16,128]{2,1,0:T(8,128)S(1)}, u32[]{:S(2)}, u32[]{:S(2)}) collective-permute-start(f32[16,16,128]{2,1,0:T(8,128)} %estimate.1), channel_id=1, source_target_pairs={{0,1},{1,0},{2,3},{3,2},{32,64},{33,65},{34,66},{35,67},{64,32},{6... | collective-permute-start | bytes 393224 | tf_op jit(solution)/shard_map/ppermute | solution.py:72
  1.5 0.0 collective-permute-start
  1.5 1.1 %copy-done = f32[6,16,16,128]{3,2,1,0:T(8,128)S(1)} copy-done((f32[6,16,16,128]{3,2,1,0:T(8,128)S(1)}, f32[6,16,16,128]{3,2,1,0:T(8,128)}, u32[]{:S(2)}) %copy-start) | copy-done | bytes 786456
  2.6 0.7 copy-done.7
  3.3 0.6 shard_map.57
  3.9 2.1 %collective-permute-start.2 = (f32[49,16,128]{2,1,0:T(8,128)S(1)}, f32[49,16,128]{2,1,0:T(8,128)S(1)}, u32[]{:S(2)}, u32[]{:S(2)}) collective-permute-start(f32[49,16,128]{2,1,0:T(8,128)S(1)} %get-tuple-element.40), channel_id=1, source_target_pairs={{0,32},{1,33},{2,34},{3,35},{32,0},{33,1},{34,2},{35,3},{64,96},{6... | collective-permute-start | bytes 1204232 | tf_op jit(solution)/shard_map/ppermute | solution.py:72
  6.0 2.6 %collective-permute-start.3 = (f32[49,16,128]{2,1,0:T(8,128)S(1)}, f32[49,16,128]{2,1,0:T(8,128)S(1)}, u32[]{:S(2)}, u32[]{:S(2)}) collective-permute-start(f32[49,16,128]{2,1,0:T(8,128)S(1)} %get-tuple-element.41), channel_id=1, source_target_pairs={{0,1},{1,0},{2,3},{3,2},{32,64},{33,65},{34,66},{35,67},{64,32},{6... | collective-permute-start | bytes 1204232 | tf_op jit(solution)/shard_map/ppermute | solution.py:72
  8.6 0.0 collective-permute-done.1.high
  8.6 0.0 collective-permute-done.low
  8.6 0.9 %copy-done.2 = f32[16,16,128]{2,1,0:T(8,128)S(1)} copy-done((f32[16,16,128]{2,1,0:T(8,128)S(1)}, f32[16,16,128]{2,1,0:T(8,128)}, u32[]{:S(2)}) %copy-start.2) | copy-done | bytes 131096
  9.5 0.2 shard_map.55.after.own
  9.7 2.0 %collective-permute-start.7 = (f32[46,16,128]{2,1,0:T(8,128)S(1)}, f32[46,16,128]{2,1,0:T(8,128)S(1)}, u32[]{:S(2)}, u32[]{:S(2)}) collective-permute-start(f32[46,16,128]{2,1,0:T(8,128)S(1)} %shard_map.55.after.own), channel_id=1, source_target_pairs={{0,1},{1,0},{2,3},{3,2},{4,8},{5,9},{6,10},{7,11},{8,4},{9,5},{10,... | collective-permute-start | bytes 1130504 | tf_op jit(solution)/shard_map/ppermute | solution.py:72
  11.7 0.0 collective-permute-start.6
  11.7 0.7 %copy-done.4 = s32[6,3]{0,1:T(4,128)S(1)} copy-done((s32[6,3]{0,1:T(4,128)S(1)}, s32[6,3]{0,1:T(4,128)}, u32[]{:S(2)}) %copy-start.4) | copy-done | bytes 96
  12.4 0.7 %copy-done.6 = f32[6,3,31]{2,1,0:T(4,128)S(1)} copy-done((f32[6,3,31]{2,1,0:T(4,128)S(1)}, f32[6,3,31]{2,1,0:T(4,128)}, u32[]{:S(2)}) %copy-start.6) | copy-done | bytes 2256
  13.1 2.2 %shard_map.56 = (f32[3,8,128]{2,1,0:T(8,128)S(1)}, f32[6,31,8,128]{3,2,1,0:T(8,128)S(1)}, bf16[96,256]{1,0:T(8,128)(2,1)S(1)}, bf16[96,256]{1,0:T(8,128)(2,1)S(1...) custom-call(s32[3,6]{1,0:T(4,128)S(1)} %bitcast.2, ...), custom_call_target="tpu_custom_call" | custom-call | bytes 8388608 | tf_op jit(solution)/shard_map/pallas_call | solution.py:488
  15.3 0.0 collective-permute-done.2.low
  15.4 2.9 %collective-permute-done.3.high = f32[49,16,128]{2,1,0:T(8,128)S(1)} collective-permute-done((f32[49,16,128]{2,1,0:T(8,128)S(1)}, f32[49,16,128]{2,1,0:T(8,128)S(1)}, u32[]{:S(2)}, u32[]{:S(2)}) %collective-permute-start.3) | collective-permute-done | bytes 401440 | tf_op jit(solution)/shard_map/ppermute | solution.py:72
  18.3 0.0 copy-done.8
  18.3 0.0 copy-done.1
  18.3 0.8 %shard_map.58 = (f32[6,16,32,128]{3,2,1,0:T(8,128)S(1)}, f32[97,8,128]{2,1,0:T(8,128)S(1)}, f32[97,8,128]{2,1,0:T(8,128)S(1)}, f32[8,128]{1,0:T(8,128)S(1)}) custom-call(s32[3,6]{1,0:T(4,128)S(1)} %bitcast.3, s32[6]{0:T(128)S(1)} %bitcast.7, f32[6,16,16,128]{3,2,1,0:T(8,128)S(1)} %copy-done.1, f32[49,16,128]{2,1,0:T(8,128)S(1)} %collective-permute-done.2.low, ...), custom_call_target="tpu_custom_call" | custom-call | bytes 67108864 | tf_op jit(solution)/shard_map/pallas_call | solution.py:506
  19.1 0.2 collective-permute-start.4
  19.3 3.7 %collective-permute-start.5 = (f32[97,8,128]{2,1,0:T(8,128)S(1)}, f32[97,8,128]{2,1,0:T(8,128)S(1)}, u32[]{:S(2)}, u32[]{:S(2)}) collective-permute-start(f32[97,8,128]{2,1,0:T(8,128)S(1)} %get-tuple-element.44), channel_id=1, source_target_pairs={{0,1},{1,0},{2,3},{3,2},{4,8},{5,9},{6,10},{7,11},{8,4},{9,5},{10,... | collective-permute-start | bytes 1191944 | tf_op jit(solution)/shard_map/ppermute | solution.py:72
  23.0 0.0 collective-permute-done.7.high
  23.0 0.0 collective-permute-done.6.low
  23.0 2.8 %shard_map.59 = (f32[6,16,16,128]{3,2,1,0:T(8,128)S(1)}, f32[392,128]{1,0:T(8,128)S(1)}, f32[392,128]{1,0:T(8,128)S(1)}) custom-call(f32[6,31,8,128]{3,2,1,0:T(8,128)S(1)} %get-tuple-element.46.table, bf16[96,256]{1,0:T(8,128)(2,1)S(1)} %get-tuple-element.47.fan_in, f32[46,16,128]{2,1,0:T(8,128)S(1)} %shard_map.55.after.own, ...), custom_call_target="tpu_custom_call" | custom-call | flops 17179869184 | bytes 67108864 | tf_op jit(solution)/shard_map/pallas_call | solution.py:521
  25.9 0.1 collective-permute-start.8
  26.0 3.0 %collective-permute-start.9 = (f32[392,128]{1,0:T(8,128)S(1)}, f32[392,128]{1,0:T(8,128)S(1)}, u32[]{:S(2)}, u32[]{:S(2)}) collective-permute-start(f32[392,128]{1,0:T(8,128)S(1)} %get-tuple-element.53), channel_id=1, source_target_pairs={{0,1},{1,0},{2,3},{3,2},{4,5},{5,4},{6,7},{7,6},{8,9},{9,8},{10,11... | collective-permute-start | bytes 602120 | tf_op jit(solution)/shard_map/ppermute | solution.py:83
  29.0 0.3 collective-permute-done.4.low
  29.3 0.8 %collective-permute-done.5.high = f32[97,8,128]{2,1,0:T(8,128)S(1)} collective-permute-done((f32[97,8,128]{2,1,0:T(8,128)S(1)}, f32[97,8,128]{2,1,0:T(8,128)S(1)}, u32[]{:S(2)}, u32[]{:S(2)}) %collective-permute-start.5) | collective-permute-done | bytes 397344 | tf_op jit(solution)/shard_map/ppermute | solution.py:72
  30.2 0.0 copy-done.5
  30.2 0.7 %shard_map.60 = (f32[6,16,16,128]{3,2,1,0:T(8,128)S(1)}, f32[8,128]{1,0:T(8,128)S(1)}, f32[6,16,32,128]{3,2,1,0:T(8,128)S(1)}) custom-call(s32[3,6]{1,0:T(4,128)S(1)} %bitcast.4, f32[6,16,32,128]{3,2,1,0:T(8,128)S(1)} %get-tuple-element.42.held, f32[97,8,128]{2,1,0:T(8,128)S(1)} %collective-permute-done.4.low, ...), custom_call_target="tpu_custom_call", output_to_operand_aliasing={{2}: (1, {})} | custom-call | bytes 67108864 | tf_op jit(solution)/shard_map/pallas_call | solution.py:531
  30.9 0.5 shard_map.61.model
  31.4 0.3 collective-permute-done.8.high
  31.7 0.0 collective-permute-done.9.low
  31.7 1.5 %shard_map.62 = (f32[6,16,16,128]{3,2,1,0:T(8,128)S(1)}, f32[392,128]{1,0:T(8,128)S(1)}, f32[392,128]{1,0:T(8,128)S(1)}) custom-call(s32[3,6]{1,0:T(4,128)S(1)} %bitcast.5, s32[6]{0:T(128)S(1)} %bitcast.9, f32[6,256,128]{2,1,0:T(8,128)S(1)} %get-tuple-element.50.forward_z, f32[6,16,16,128]{3,2,1,0:T(8,128)S(1)} %shard_map.61.model, ...), custom_call_target="tpu_custom_call" | custom-call | flops 17179869184 | bytes 67108864 | tf_op jit(solution)/shard_map/pallas_call | solution.py:542
  33.2 0.2 collective-permute-start.10
  33.4 3.9 %collective-permute-start.11 = (f32[392,128]{1,0:T(8,128)S(1)}, f32[392,128]{1,0:T(8,128)S(1)}, u32[]{:S(2)}, u32[]{:S(2)}) collective-permute-start(f32[392,128]{1,0:T(8,128)S(1)} %get-tuple-element.55), channel_id=1, source_target_pairs={{0,1},{1,0},{2,3},{3,2},{4,5},{5,4},{6,7},{7,6},{8,9},{9,8},{10,11... | collective-permute-start | bytes 602120 | tf_op jit(solution)/shard_map/ppermute | solution.py:83
  37.3 2.4 %shard_map.64 = (f32[46,16,128]{2,1,0:T(8,128)S(1)}, f32[46,16,128]{2,1,0:T(8,128)S(1)}, f32[46,16,128]{2,1,0:T(8,128)S(1)}) custom-call(f32[6,31,8,128]{3,2,1,0:T(8,128)S(1)} %get-tuple-element.46.table, bf16[96,256]{1,0:T(8,128)(2,1)S(1)} %get-tuple-element.56.fan_out, f32[6,128,128]{2,1,0:T(8,128)S(1)} %get-tuple-element.57.backward_z, ...), custom_call_target="tpu_custom_call" | custom-call | flops 17179869184 | bytes 67108864 | tf_op jit(solution)/shard_map/pallas_call | solution.py:551
  39.7 0.2 collective-permute-start.12
  39.9 5.5 %collective-permute-start.13 = (f32[46,16,128]{2,1,0:T(8,128)S(1)}, f32[46,16,128]{2,1,0:T(8,128)S(1)}, u32[]{:S(2)}, u32[]{:S(2)}) collective-permute-start(f32[46,16,128]{2,1,0:T(8,128)S(1)} %get-tuple-element.61), channel_id=1, source_target_pairs={{0,1},{1,0},{2,3},{3,2},{4,8},{5,9},{6,10},{7,11},{8,4},{9,5},{10,... | collective-permute-start | bytes 1130504 | tf_op jit(solution)/shard_map/ppermute | solution.py:72
  45.3 0.0 collective-permute-done.10.far_marks.far
  45.3 0.0 collective-permute-done.11.near_marks.near
  45.3 1.6 %shard_map.66 = (f32[23,16,128]{2,1,0:T(8,128)S(1)}, f32[23,16,128]{2,1,0:T(8,128)S(1)}, f32[23,16,128]{2,1,0:T(8,128)S(1)}) custom-call(f32[6,31,8,128]{3,2,1,0:T(8,128)S(1)} %get-tuple-element.46.table, bf16[96,256]{1,0:T(8,128)(2,1)S(1)} %get-tuple-element.65.fan_pair, f32[6,128,128]{2,1,0:T(8,128)S(1)} %get-tuple-element.66.rest_z, ...), custom_call_target="tpu_custom_call" | custom-call | flops 17179869184 | bytes 67108864 | tf_op jit(solution)/shard_map/pallas_call | solution.py:561
  46.9 0.1 collective-permute-start.16
  47.0 1.9 %collective-permute-start.17 = (f32[23,16,128]{2,1,0:T(8,128)S(1)}, f32[23,16,128]{2,1,0:T(8,128)S(1)}, u32[]{:S(2)}, u32[]{:S(2)}) collective-permute-start(f32[23,16,128]{2,1,0:T(8,128)S(1)} %get-tuple-element.69), channel_id=1, source_target_pairs={{0,1},{1,0},{2,3},{3,2},{4,8},{5,9},{6,10},{7,11},{8,4},{9,5},{10,... | collective-permute-start | bytes 565256 | tf_op jit(solution)/shard_map/ppermute | solution.py:72
  49.0 2.4 %collective-permute-done.12.from_low = f32[46,16,128]{2,1,0:T(8,128)S(1)} collective-permute-done((f32[46,16,128]{2,1,0:T(8,128)S(1)}, f32[46,16,128]{2,1,0:T(8,128)S(1)}, u32[]{:S(2)}, u32[]{:S(2)}) %collective-permute-start.12) | collective-permute-done | bytes 376864 | tf_op jit(solution)/shard_map/ppermute | solution.py:72
  51.4 3.5 %collective-permute-done.13.from_high = f32[46,16,128]{2,1,0:T(8,128)S(1)} collective-permute-done((f32[46,16,128]{2,1,0:T(8,128)S(1)}, f32[46,16,128]{2,1,0:T(8,128)S(1)}, u32[]{:S(2)}, u32[]{:S(2)}) %collective-permute-start.13) | collective-permute-done | bytes 376864 | tf_op jit(solution)/shard_map/ppermute | solution.py:72
  54.9 0.1 shard_map.65
  55.1 0.1 collective-permute-start.14
  55.2 1.0 %collective-permute-start.15 = (f32[16,16,128]{2,1,0:T(8,128)S(1)}, f32[16,16,128]{2,1,0:T(8,128)S(1)}, u32[]{:S(2)}, u32[]{:S(2)}) collective-permute-start(f32[16,16,128]{2,1,0:T(8,128)S(1)} %get-tuple-element.64), channel_id=1, source_target_pairs={{0,1},{1,0},{2,3},{3,2},{32,64},{33,65},{34,66},{35,67},{64,32},{6... | collective-permute-start | bytes 393224 | tf_op jit(solution)/shard_map/ppermute | solution.py:72
  56.2 0.0 collective-permute-done.16.from_low
  56.2 1.8 %collective-permute-done.17.from_high = f32[23,16,128]{2,1,0:T(8,128)S(1)} collective-permute-done((f32[23,16,128]{2,1,0:T(8,128)S(1)}, f32[23,16,128]{2,1,0:T(8,128)S(1)}, u32[]{:S(2)}, u32[]{:S(2)}) %collective-permute-start.17) | collective-permute-done | bytes 188448 | tf_op jit(solution)/shard_map/ppermute | solution.py:72
  58.0 0.1 shard_map.67
  58.1 0.1 collective-permute-start.18
  58.2 1.5 %collective-permute-start.19 = (f32[8,16,128]{2,1,0:T(8,128)S(1)}, f32[8,16,128]{2,1,0:T(8,128)S(1)}, u32[]{:S(2)}, u32[]{:S(2)}) collective-permute-start(f32[8,16,128]{2,1,0:T(8,128)S(1)} %get-tuple-element.72), channel_id=1, source_target_pairs={{0,1},{1,0},{2,3},{3,2},{32,64},{33,65},{34,66},{35,67},{64,32},{6... | collective-permute-start | bytes 196616 | tf_op jit(solution)/shard_map/ppermute | solution.py:72
  59.6 0.0 copy-done.3
  59.7 1.2 %shard_map.63.scale = f32[16,16,128]{2,1,0:T(8,128)S(1)} custom-call(f32[3,8,128]{2,1,0:T(8,128)S(1)} %get-tuple-element.39.after.norm, f32[16,16,128]{2,1,0:T(8,128)S(1)} %copy-done.3, f32[8,128]{1,0:T(8,128)S(1)} %get-tuple-element.49.marks, f32[392,128]{1,0:T(8,128)S(1)} %collective-permute-done.10.far_marks.far, ...), custom_call_target="tpu_custom_call" | custom-call | bytes 524288 | tf_op jit(solution)/shard_map/pallas_call | solution.py:590
  60.9 1.6 %collective-permute-done.18.rest_low = f32[8,16,128]{2,1,0:T(8,128)S(1)} collective-permute-done((f32[8,16,128]{2,1,0:T(8,128)S(1)}, f32[8,16,128]{2,1,0:T(8,128)S(1)}, u32[]{:S(2)}, u32[]{:S(2)}) %collective-permute-start.18) | collective-permute-done | bytes 65568 | tf_op jit(solution)/shard_map/ppermute | solution.py:72
  62.4 2.2 %collective-permute-done.19.rest_high = f32[8,16,128]{2,1,0:T(8,128)S(1)} collective-permute-done((f32[8,16,128]{2,1,0:T(8,128)S(1)}, f32[8,16,128]{2,1,0:T(8,128)S(1)}, u32[]{:S(2)}, u32[]{:S(2)}) %collective-permute-start.19) | collective-permute-done | bytes 65568 | tf_op jit(solution)/shard_map/ppermute | solution.py:72
  64.7 0.0 collective-permute-done.14.from_low
  64.7 0.0 collective-permute-done.15.from_high
  64.7 0.8 %shard_map.68 = f32[16,16,128]{2,1,0:T(8,128)} custom-call(f32[16,16,128]{2,1,0:T(8,128)S(1)} %shard_map.63.scale, f32[16,16,128]{2,1,0:T(8,128)S(1)} %get-tuple-element.62.after.mid, f32[16,16,128]{2,1,0:T(8,128)S(1)} %collective-permute-done.14.from_low, f32[16,16,128]{2,1,0:T(8,128)S(1)} %collective-permute-done.15.from_high, ...), custom_call_target="tpu_custom_call" | custom-call | bytes 786432 | tf_op jit(solution)/shard_map/pallas_call | solution.py:593
  (8 shorter events, 0.0 us)
Async XLA Ops:
  0.0 18.3 %copy-start.8 = (s32[6,1,1,1]{0,3,2,1:T(1,128)S(1)}, s32[6,1,1,1]{0,3,2,1:T(1,128)}, u32[]{:S(2)}) copy-start(s32[6,1,1,1]{0,3,2,1:T(1,128)} %param.9) | copy-start | bytes 76
  0.0 8.6 %collective-permute-start.1 = (f32[16,16,128]{2,1,0:T(8,128)}, f32[16,16,128]{2,1,0:T(8,128)S(1)}, u32[]{:S(2)}, u32[]{:S(2)}) collective-permute-start(f32[16,16,128]{2,1,0:T(8,128)} %estimate.1), channel_id=1, source_target_pairs={{0,1},{1,0},{2,3},{3,2},{32,64},{33,65},{34,66},{35,67},{64,32},{6... | collective-permute-start | bytes 393224 | tf_op jit(solution)/shard_map/ppermute | solution.py:72
  1.5 7.1 %collective-permute-start = (f32[16,16,128]{2,1,0:T(8,128)}, f32[16,16,128]{2,1,0:T(8,128)S(1)}, u32[]{:S(2)}, u32[]{:S(2)}) collective-permute-start(f32[16,16,128]{2,1,0:T(8,128)} %estimate.1), channel_id=1, source_target_pairs={{0,32},{1,33},{2,34},{3,35},{32,0},{33,1},{34,2},{35,3},{64,96},{6... | collective-permute-start | bytes 393224 | tf_op jit(solution)/shard_map/ppermute | solution.py:72
  1.5 1.1 %copy-start = (f32[6,16,16,128]{3,2,1,0:T(8,128)S(1)}, f32[6,16,16,128]{3,2,1,0:T(8,128)}, u32[]{:S(2)}) copy-start(f32[6,16,16,128]{3,2,1,0:T(8,128)} %raw.3) | copy-start | bytes 2359300
  2.6 0.7 %copy-start.7 = (s32[6,1,1,1]{0,3,2,1:T(1,128)S(1)}, s32[6,1,1,1]{0,3,2,1:T(1,128)}, u32[]{:S(2)}) copy-start(s32[6,1,1,1]{0,3,2,1:T(1,128)} %param.9) | copy-start | bytes 76
  3.3 15.0 %copy-start.1 = (f32[6,16,16,128]{3,2,1,0:T(8,128)S(1)}, f32[6,16,16,128]{3,2,1,0:T(8,128)}, u32[]{:S(2)}) copy-start(f32[6,16,16,128]{3,2,1,0:T(8,128)} %raw.3) | copy-start | bytes 2359300
  3.9 11.5 %collective-permute-start.2 = (f32[49,16,128]{2,1,0:T(8,128)S(1)}, f32[49,16,128]{2,1,0:T(8,128)S(1)}, u32[]{:S(2)}, u32[]{:S(2)}) collective-permute-start(f32[49,16,128]{2,1,0:T(8,128)S(1)} %get-tuple-element.40), channel_id=1, source_target_pairs={{0,32},{1,33},{2,34},{3,35},{32,0},{33,1},{34,2},{35,3},{64,96},{6... | collective-permute-start | bytes 1204232 | tf_op jit(solution)/shard_map/ppermute | solution.py:72
  6.0 12.3 %collective-permute-start.3 = (f32[49,16,128]{2,1,0:T(8,128)S(1)}, f32[49,16,128]{2,1,0:T(8,128)S(1)}, u32[]{:S(2)}, u32[]{:S(2)}) collective-permute-start(f32[49,16,128]{2,1,0:T(8,128)S(1)} %get-tuple-element.41), channel_id=1, source_target_pairs={{0,1},{1,0},{2,3},{3,2},{32,64},{33,65},{34,66},{35,67},{64,32},{6... | collective-permute-start | bytes 1204232 | tf_op jit(solution)/shard_map/ppermute | solution.py:72
  8.6 0.9 %copy-start.2 = (f32[16,16,128]{2,1,0:T(8,128)S(1)}, f32[16,16,128]{2,1,0:T(8,128)}, u32[]{:S(2)}) copy-start(f32[16,16,128]{2,1,0:T(8,128)} %estimate.1) | copy-start | bytes 393220
  9.7 13.3 %collective-permute-start.7 = (f32[46,16,128]{2,1,0:T(8,128)S(1)}, f32[46,16,128]{2,1,0:T(8,128)S(1)}, u32[]{:S(2)}, u32[]{:S(2)}) collective-permute-start(f32[46,16,128]{2,1,0:T(8,128)S(1)} %shard_map.55.after.own), channel_id=1, source_target_pairs={{0,1},{1,0},{2,3},{3,2},{4,8},{5,9},{6,10},{7,11},{8,4},{9,5},{10,... | collective-permute-start | bytes 1130504 | tf_op jit(solution)/shard_map/ppermute | solution.py:72
  11.7 11.3 %collective-permute-start.6 = (f32[46,16,128]{2,1,0:T(8,128)S(1)}, f32[46,16,128]{2,1,0:T(8,128)S(1)}, u32[]{:S(2)}, u32[]{:S(2)}) collective-permute-start(f32[46,16,128]{2,1,0:T(8,128)S(1)} %shard_map.55.after.own), channel_id=1, source_target_pairs={{0,4},{1,5},{2,6},{3,7},{4,0},{5,1},{6,2},{7,3},{8,12},{9,13},{10,... | collective-permute-start | bytes 1130504 | tf_op jit(solution)/shard_map/ppermute | solution.py:72
  11.7 0.7 %copy-start.4 = (s32[6,3]{0,1:T(4,128)S(1)}, s32[6,3]{0,1:T(4,128)}, u32[]{:S(2)}) copy-start(s32[6,3]{0,1:T(4,128)} %param.8) | copy-start | bytes 220
  12.4 0.7 %copy-start.6 = (f32[6,3,31]{2,1,0:T(4,128)S(1)}, f32[6,3,31]{2,1,0:T(4,128)}, u32[]{:S(2)}) copy-start(f32[6,3,31]{2,1,0:T(4,128)} %psf.1) | copy-start | bytes 6700
  19.1 10.2 %collective-permute-start.4 = (f32[97,8,128]{2,1,0:T(8,128)S(1)}, f32[97,8,128]{2,1,0:T(8,128)S(1)}, u32[]{:S(2)}, u32[]{:S(2)}) collective-permute-start(f32[97,8,128]{2,1,0:T(8,128)S(1)} %get-tuple-element.43), channel_id=1, source_target_pairs={{0,4},{1,5},{2,6},{3,7},{4,0},{5,1},{6,2},{7,3},{8,12},{9,13},{10,... | collective-permute-start | bytes 1191944 | tf_op jit(solution)/shard_map/ppermute | solution.py:72
  19.3 10.9 %collective-permute-start.5 = (f32[97,8,128]{2,1,0:T(8,128)S(1)}, f32[97,8,128]{2,1,0:T(8,128)S(1)}, u32[]{:S(2)}, u32[]{:S(2)}) collective-permute-start(f32[97,8,128]{2,1,0:T(8,128)S(1)} %get-tuple-element.44), channel_id=1, source_target_pairs={{0,1},{1,0},{2,3},{3,2},{4,8},{5,9},{6,10},{7,11},{8,4},{9,5},{10,... | collective-permute-start | bytes 1191944 | tf_op jit(solution)/shard_map/ppermute | solution.py:72
  23.0 7.2 %copy-start.5 = (s32[6,3]{0,1:T(4,128)S(1)}, s32[6,3]{0,1:T(4,128)}, u32[]{:S(2)}) copy-start(s32[6,3]{0,1:T(4,128)} %param.8) | copy-start | bytes 220
  25.9 5.8 %collective-permute-start.8 = (f32[392,128]{1,0:T(8,128)S(1)}, f32[392,128]{1,0:T(8,128)S(1)}, u32[]{:S(2)}, u32[]{:S(2)}) collective-permute-start(f32[392,128]{1,0:T(8,128)S(1)} %get-tuple-element.52), channel_id=1, source_target_pairs={{0,4},{1,2},{2,1},{3,7},{4,0},{5,6},{6,5},{7,3},{8,12},{9,10},{10,... | collective-permute-start | bytes 602120 | tf_op jit(solution)/shard_map/ppermute | solution.py:83
  26.0 5.7 %collective-permute-start.9 = (f32[392,128]{1,0:T(8,128)S(1)}, f32[392,128]{1,0:T(8,128)S(1)}, u32[]{:S(2)}, u32[]{:S(2)}) collective-permute-start(f32[392,128]{1,0:T(8,128)S(1)} %get-tuple-element.53), channel_id=1, source_target_pairs={{0,1},{1,0},{2,3},{3,2},{4,5},{5,4},{6,7},{7,6},{8,9},{9,8},{10,11... | collective-permute-start | bytes 602120 | tf_op jit(solution)/shard_map/ppermute | solution.py:83
  33.2 12.1 %collective-permute-start.10 = (f32[392,128]{1,0:T(8,128)S(1)}, f32[392,128]{1,0:T(8,128)S(1)}, u32[]{:S(2)}, u32[]{:S(2)}) collective-permute-start(f32[392,128]{1,0:T(8,128)S(1)} %get-tuple-element.54), channel_id=1, source_target_pairs={{0,4},{1,2},{2,1},{3,7},{4,0},{5,6},{6,5},{7,3},{8,12},{9,10},{10,... | collective-permute-start | bytes 602120 | tf_op jit(solution)/shard_map/ppermute | solution.py:83
  33.4 11.9 %collective-permute-start.11 = (f32[392,128]{1,0:T(8,128)S(1)}, f32[392,128]{1,0:T(8,128)S(1)}, u32[]{:S(2)}, u32[]{:S(2)}) collective-permute-start(f32[392,128]{1,0:T(8,128)S(1)} %get-tuple-element.55), channel_id=1, source_target_pairs={{0,1},{1,0},{2,3},{3,2},{4,5},{5,4},{6,7},{7,6},{8,9},{9,8},{10,11... | collective-permute-start | bytes 602120 | tf_op jit(solution)/shard_map/ppermute | solution.py:83
  39.7 11.7 %collective-permute-start.12 = (f32[46,16,128]{2,1,0:T(8,128)S(1)}, f32[46,16,128]{2,1,0:T(8,128)S(1)}, u32[]{:S(2)}, u32[]{:S(2)}) collective-permute-start(f32[46,16,128]{2,1,0:T(8,128)S(1)} %get-tuple-element.60), channel_id=1, source_target_pairs={{0,4},{1,5},{2,6},{3,7},{4,0},{5,1},{6,2},{7,3},{8,12},{9,13},{10,... | collective-permute-start | bytes 1130504 | tf_op jit(solution)/shard_map/ppermute | solution.py:72
  39.9 15.1 %collective-permute-start.13 = (f32[46,16,128]{2,1,0:T(8,128)S(1)}, f32[46,16,128]{2,1,0:T(8,128)S(1)}, u32[]{:S(2)}, u32[]{:S(2)}) collective-permute-start(f32[46,16,128]{2,1,0:T(8,128)S(1)} %get-tuple-element.61), channel_id=1, source_target_pairs={{0,1},{1,0},{2,3},{3,2},{4,8},{5,9},{6,10},{7,11},{8,4},{9,5},{10,... | collective-permute-start | bytes 1130504 | tf_op jit(solution)/shard_map/ppermute | solution.py:72
  46.9 9.2 %collective-permute-start.16 = (f32[23,16,128]{2,1,0:T(8,128)S(1)}, f32[23,16,128]{2,1,0:T(8,128)S(1)}, u32[]{:S(2)}, u32[]{:S(2)}) collective-permute-start(f32[23,16,128]{2,1,0:T(8,128)S(1)} %get-tuple-element.68), channel_id=1, source_target_pairs={{0,4},{1,5},{2,6},{3,7},{4,0},{5,1},{6,2},{7,3},{8,12},{9,13},{10,... | collective-permute-start | bytes 565256 | tf_op jit(solution)/shard_map/ppermute | solution.py:72
  47.0 11.0 %collective-permute-start.17 = (f32[23,16,128]{2,1,0:T(8,128)S(1)}, f32[23,16,128]{2,1,0:T(8,128)S(1)}, u32[]{:S(2)}, u32[]{:S(2)}) collective-permute-start(f32[23,16,128]{2,1,0:T(8,128)S(1)} %get-tuple-element.69), channel_id=1, source_target_pairs={{0,1},{1,0},{2,3},{3,2},{4,8},{5,9},{6,10},{7,11},{8,4},{9,5},{10,... | collective-permute-start | bytes 565256 | tf_op jit(solution)/shard_map/ppermute | solution.py:72
  55.1 9.6 %collective-permute-start.14 = (f32[16,16,128]{2,1,0:T(8,128)S(1)}, f32[16,16,128]{2,1,0:T(8,128)S(1)}, u32[]{:S(2)}, u32[]{:S(2)}) collective-permute-start(f32[16,16,128]{2,1,0:T(8,128)S(1)} %get-tuple-element.63), channel_id=1, source_target_pairs={{0,32},{1,33},{2,34},{3,35},{32,0},{33,1},{34,2},{35,3},{64,96},{6... | collective-permute-start | bytes 393224 | tf_op jit(solution)/shard_map/ppermute | solution.py:72
  55.2 9.5 %collective-permute-start.15 = (f32[16,16,128]{2,1,0:T(8,128)S(1)}, f32[16,16,128]{2,1,0:T(8,128)S(1)}, u32[]{:S(2)}, u32[]{:S(2)}) collective-permute-start(f32[16,16,128]{2,1,0:T(8,128)S(1)} %get-tuple-element.64), channel_id=1, source_target_pairs={{0,1},{1,0},{2,3},{3,2},{32,64},{33,65},{34,66},{35,67},{64,32},{6... | collective-permute-start | bytes 393224 | tf_op jit(solution)/shard_map/ppermute | solution.py:72
  58.0 1.6 %copy-start.3 = (f32[16,16,128]{2,1,0:T(8,128)S(1)}, f32[16,16,128]{2,1,0:T(8,128)}, u32[]{:S(2)}) copy-start(f32[16,16,128]{2,1,0:T(8,128)} %estimate.1) | copy-start | bytes 393220
  58.1 4.4 %collective-permute-start.18 = (f32[8,16,128]{2,1,0:T(8,128)S(1)}, f32[8,16,128]{2,1,0:T(8,128)S(1)}, u32[]{:S(2)}, u32[]{:S(2)}) collective-permute-start(f32[8,16,128]{2,1,0:T(8,128)S(1)} %get-tuple-element.71), channel_id=1, source_target_pairs={{0,32},{1,33},{2,34},{3,35},{32,0},{33,1},{34,2},{35,3},{64,96},{6... | collective-permute-start | bytes 196616 | tf_op jit(solution)/shard_map/ppermute | solution.py:72
  58.2 6.5 %collective-permute-start.19 = (f32[8,16,128]{2,1,0:T(8,128)S(1)}, f32[8,16,128]{2,1,0:T(8,128)S(1)}, u32[]{:S(2)}, u32[]{:S(2)}) collective-permute-start(f32[8,16,128]{2,1,0:T(8,128)S(1)} %get-tuple-element.72), channel_id=1, source_target_pairs={{0,1},{1,0},{2,3},{3,2},{32,64},{33,65},{34,66},{35,67},{64,32},{6... | collective-permute-start | bytes 196616 | tf_op jit(solution)/shard_map/ppermute | solution.py:72

commit v6 on v5

--- a/solution.py
+++ b/solution.py
@@ -73,14 +73,14 @@
 
 
 def swap(block, first):
-    count, depth = lax.axis_size("by"), lax.axis_size("bz")
+    count, depth = lax.axis_size("bx"), lax.axis_size("bz")
     pairs = []
     for x in range(count):
         for z in range(depth):
             to = z + 1 if (z - first) % 2 == 0 else z - 1
             target = x * depth + to if 0 <= to < depth else (x ^ 1) * depth + z
             pairs.append((x * depth + z, target))
-    return lax.ppermute(block, ("by", "bz"), pairs)
+    return lax.ppermute(block, ("bx", "bz"), pairs)
 
 
 def lanes(rows):

time: 65.7 us -> 65.7 us (level)
  starting transfers between devices: 29.7 us -> 28.3 us
  waiting for transfers between devices: 16 us -> 17.3 us
    ppermute x16, starting transfers between devices: 22.5 us -> 21.2 us  [trade(): return lax.ppermute(block, (axis, 'bz'), pairs)]
    ppermute x16, waiting for transfers between devices: 15.7 us -> 17 us  [trade(): return lax.ppermute(block, (axis, 'bz'), pairs)]
where the time goes in v6:
time: 65.7 us; the launch traced here: 65.4 us
  starting transfers between devices  28.3 us (43%)
  waiting for transfers between devices  17.3 us (26%)
  Pallas kernels  15.6 us (24%)
  local copies, waits for them, and re-layouts  4.09 us (6%)
    ppermute x16, starting transfers between devices, trade(): return lax.ppermute(block, (axis, 'bz'), pairs)  21.2 us
    ppermute x16, waiting for transfers between devices, trade(): return lax.ppermute(block, (axis, 'bz'), pairs)  17 us
    ppermute x4, starting transfers between devices, swap(): return lax.ppermute(block, ('bx', 'bz'), pairs)  7.14 us
    unnamed x18, local copies, waits for them, and re-layouts  4.09 us
    pallas_call x1, Pallas kernels, on_device(): call(forward, [full, (64 * V + 8, Z), (64 * V + 8, Z)], [VM] * 5 + [SM, A...  2.85 us
    pallas_call x1, Pallas kernels, on_device(): call(back_own, [(N, C, Z)] * 3, [VM] * 4, [pltpu.VMEM((N, V * C, Z), F32)...  2.43 us
    pallas_call x1, Pallas kernels, on_device(): call(build, [(3, 8, Z), (V, K, 8, Z), jax.ShapeDtypeStruct((V * C, 2 * Z)...  2.23 us
    pallas_call x1, Pallas kernels, on_device(): call(back_rest, [(N // 2, C, Z)] * 3, [VM] * 5 + [ANY], [pltpu.VMEM((W, W...  1.58 us
  transfers between devices with their start and end apart: 20, of which 9 were waited for; matrix products, arithmetic and copies ran while one was open for 0% of the time, Pallas kernels for 20%

profile of v6, /device:TPU:38, one launch (start us, length us, event | category | flops | bytes accessed | tf_op | source)
XLA Modules:
  0.0 65.4 jit_solution(3081256637751285992)
XLA Ops:
  0.0 0.0 copy-start.8
  0.0 1.5 %collective-permute-start.1 = (f32[16,16,128]{2,1,0:T(8,128)}, f32[16,16,128]{2,1,0:T(8,128)S(1)}, u32[]{:S(2)}, u32[]{:S(2)}) collective-permute-start(f32[16,16,128]{2,1,0:T(8,128)} %estimate.1), channel_id=1, source_target_pairs={{0,1},{1,0},{2,3},{3,2},{32,64},{33,65},{34,66},{35,67},{64,32},{6... | collective-permute-start | bytes 393224 | tf_op jit(solution)/shard_map/ppermute | solution.py:72
  1.5 0.0 collective-permute-start
  1.5 1.1 %copy-done = f32[6,16,16,128]{3,2,1,0:T(8,128)S(1)} copy-done((f32[6,16,16,128]{3,2,1,0:T(8,128)S(1)}, f32[6,16,16,128]{3,2,1,0:T(8,128)}, u32[]{:S(2)}) %copy-start) | copy-done | bytes 786456
  2.6 0.7 copy-done.7
  3.3 0.6 shard_map.57
  3.9 2.1 %collective-permute-start.2 = (f32[49,16,128]{2,1,0:T(8,128)S(1)}, f32[49,16,128]{2,1,0:T(8,128)S(1)}, u32[]{:S(2)}, u32[]{:S(2)}) collective-permute-start(f32[49,16,128]{2,1,0:T(8,128)S(1)} %get-tuple-element.40), channel_id=1, source_target_pairs={{0,32},{1,33},{2,34},{3,35},{32,0},{33,1},{34,2},{35,3},{64,96},{6... | collective-permute-start | bytes 1204232 | tf_op jit(solution)/shard_map/ppermute | solution.py:72
  6.0 2.6 %collective-permute-start.3 = (f32[49,16,128]{2,1,0:T(8,128)S(1)}, f32[49,16,128]{2,1,0:T(8,128)S(1)}, u32[]{:S(2)}, u32[]{:S(2)}) collective-permute-start(f32[49,16,128]{2,1,0:T(8,128)S(1)} %get-tuple-element.41), channel_id=1, source_target_pairs={{0,1},{1,0},{2,3},{3,2},{32,64},{33,65},{34,66},{35,67},{64,32},{6... | collective-permute-start | bytes 1204232 | tf_op jit(solution)/shard_map/ppermute | solution.py:72
  8.6 0.0 collective-permute-done.1.high
  8.6 0.0 collective-permute-done.low
  8.6 0.9 %copy-done.2 = f32[16,16,128]{2,1,0:T(8,128)S(1)} copy-done((f32[16,16,128]{2,1,0:T(8,128)S(1)}, f32[16,16,128]{2,1,0:T(8,128)}, u32[]{:S(2)}) %copy-start.2) | copy-done | bytes 131096
  9.5 0.2 shard_map.55.after.own
  9.7 2.0 %collective-permute-start.7 = (f32[46,16,128]{2,1,0:T(8,128)S(1)}, f32[46,16,128]{2,1,0:T(8,128)S(1)}, u32[]{:S(2)}, u32[]{:S(2)}) collective-permute-start(f32[46,16,128]{2,1,0:T(8,128)S(1)} %shard_map.55.after.own), channel_id=1, source_target_pairs={{0,1},{1,0},{2,3},{3,2},{4,8},{5,9},{6,10},{7,11},{8,4},{9,5},{10,... | collective-permute-start | bytes 1130504 | tf_op jit(solution)/shard_map/ppermute | solution.py:72
  11.7 0.0 collective-permute-start.6
  11.7 0.7 %copy-done.4 = s32[6,3]{0,1:T(4,128)S(1)} copy-done((s32[6,3]{0,1:T(4,128)S(1)}, s32[6,3]{0,1:T(4,128)}, u32[]{:S(2)}) %copy-start.4) | copy-done | bytes 96
  12.4 0.7 %copy-done.6 = f32[6,3,31]{2,1,0:T(4,128)S(1)} copy-done((f32[6,3,31]{2,1,0:T(4,128)S(1)}, f32[6,3,31]{2,1,0:T(4,128)}, u32[]{:S(2)}) %copy-start.6) | copy-done | bytes 2256
  13.1 2.2 %shard_map.56 = (f32[3,8,128]{2,1,0:T(8,128)S(1)}, f32[6,31,8,128]{3,2,1,0:T(8,128)S(1)}, bf16[96,256]{1,0:T(8,128)(2,1)S(1)}, bf16[96,256]{1,0:T(8,128)(2,1)S(1...) custom-call(s32[3,6]{1,0:T(4,128)S(1)} %bitcast.2, ...), custom_call_target="tpu_custom_call" | custom-call | bytes 8388608 | tf_op jit(solution)/shard_map/pallas_call | solution.py:488
  15.3 0.0 collective-permute-done.2.low
  15.4 2.9 %collective-permute-done.3.high = f32[49,16,128]{2,1,0:T(8,128)S(1)} collective-permute-done((f32[49,16,128]{2,1,0:T(8,128)S(1)}, f32[49,16,128]{2,1,0:T(8,128)S(1)}, u32[]{:S(2)}, u32[]{:S(2)}) %collective-permute-start.3) | collective-permute-done | bytes 401440 | tf_op jit(solution)/shard_map/ppermute | solution.py:72
  18.3 0.0 copy-done.8
  18.3 0.0 copy-done.1
  18.3 0.8 %shard_map.58 = (f32[6,16,32,128]{3,2,1,0:T(8,128)S(1)}, f32[97,8,128]{2,1,0:T(8,128)S(1)}, f32[97,8,128]{2,1,0:T(8,128)S(1)}, f32[8,128]{1,0:T(8,128)S(1)}) custom-call(s32[3,6]{1,0:T(4,128)S(1)} %bitcast.3, s32[6]{0:T(128)S(1)} %bitcast.7, f32[6,16,16,128]{3,2,1,0:T(8,128)S(1)} %copy-done.1, f32[49,16,128]{2,1,0:T(8,128)S(1)} %collective-permute-done.2.low, ...), custom_call_target="tpu_custom_call" | custom-call | bytes 67108864 | tf_op jit(solution)/shard_map/pallas_call | solution.py:506
  19.1 0.2 collective-permute-start.4
  19.3 3.7 %collective-permute-start.5 = (f32[97,8,128]{2,1,0:T(8,128)S(1)}, f32[97,8,128]{2,1,0:T(8,128)S(1)}, u32[]{:S(2)}, u32[]{:S(2)}) collective-permute-start(f32[97,8,128]{2,1,0:T(8,128)S(1)} %get-tuple-element.44), channel_id=1, source_target_pairs={{0,1},{1,0},{2,3},{3,2},{4,8},{5,9},{6,10},{7,11},{8,4},{9,5},{10,... | collective-permute-start | bytes 1191944 | tf_op jit(solution)/shard_map/ppermute | solution.py:72
  23.0 0.0 collective-permute-done.7.high
  23.0 0.0 collective-permute-done.6.low
  23.0 2.8 %shard_map.59 = (f32[6,16,16,128]{3,2,1,0:T(8,128)S(1)}, f32[392,128]{1,0:T(8,128)S(1)}, f32[392,128]{1,0:T(8,128)S(1)}) custom-call(f32[6,31,8,128]{3,2,1,0:T(8,128)S(1)} %get-tuple-element.46.table, bf16[96,256]{1,0:T(8,128)(2,1)S(1)} %get-tuple-element.47.fan_in, f32[46,16,128]{2,1,0:T(8,128)S(1)} %shard_map.55.after.own, ...), custom_call_target="tpu_custom_call" | custom-call | flops 17179869184 | bytes 67108864 | tf_op jit(solution)/shard_map/pallas_call | solution.py:521
  25.9 0.1 collective-permute-start.8
  26.0 3.0 %collective-permute-start.9 = (f32[392,128]{1,0:T(8,128)S(1)}, f32[392,128]{1,0:T(8,128)S(1)}, u32[]{:S(2)}, u32[]{:S(2)}) collective-permute-start(f32[392,128]{1,0:T(8,128)S(1)} %get-tuple-element.53), channel_id=1, source_target_pairs={{0,1},{1,0},{2,3},{3,2},{32,33},{33,32},{34,35},{35,34},{64,65},{6... | collective-permute-start | bytes 602120 | tf_op jit(solution)/shard_map/ppermute | solution.py:83
  29.0 0.3 collective-permute-done.4.low
  29.3 0.8 %collective-permute-done.5.high = f32[97,8,128]{2,1,0:T(8,128)S(1)} collective-permute-done((f32[97,8,128]{2,1,0:T(8,128)S(1)}, f32[97,8,128]{2,1,0:T(8,128)S(1)}, u32[]{:S(2)}, u32[]{:S(2)}) %collective-permute-start.5) | collective-permute-done | bytes 397344 | tf_op jit(solution)/shard_map/ppermute | solution.py:72
  30.2 0.0 copy-done.5
  30.2 0.7 %shard_map.60 = (f32[6,16,16,128]{3,2,1,0:T(8,128)S(1)}, f32[8,128]{1,0:T(8,128)S(1)}, f32[6,16,32,128]{3,2,1,0:T(8,128)S(1)}) custom-call(s32[3,6]{1,0:T(4,128)S(1)} %bitcast.4, f32[6,16,32,128]{3,2,1,0:T(8,128)S(1)} %get-tuple-element.42.held, f32[97,8,128]{2,1,0:T(8,128)S(1)} %collective-permute-done.4.low, ...), custom_call_target="tpu_custom_call", output_to_operand_aliasing={{2}: (1, {})} | custom-call | bytes 67108864 | tf_op jit(solution)/shard_map/pallas_call | solution.py:531
  30.9 0.5 shard_map.61.model
  31.4 0.3 collective-permute-done.8.high
  31.7 0.0 collective-permute-done.9.low
  31.7 1.5 %shard_map.62 = (f32[6,16,16,128]{3,2,1,0:T(8,128)S(1)}, f32[392,128]{1,0:T(8,128)S(1)}, f32[392,128]{1,0:T(8,128)S(1)}) custom-call(s32[3,6]{1,0:T(4,128)S(1)} %bitcast.5, s32[6]{0:T(128)S(1)} %bitcast.9, f32[6,256,128]{2,1,0:T(8,128)S(1)} %get-tuple-element.50.forward_z, f32[6,16,16,128]{3,2,1,0:T(8,128)S(1)} %shard_map.61.model, ...), custom_call_target="tpu_custom_call" | custom-call | flops 17179869184 | bytes 67108864 | tf_op jit(solution)/shard_map/pallas_call | solution.py:542
  33.2 0.1 collective-permute-start.10
  33.3 3.9 %collective-permute-start.11 = (f32[392,128]{1,0:T(8,128)S(1)}, f32[392,128]{1,0:T(8,128)S(1)}, u32[]{:S(2)}, u32[]{:S(2)}) collective-permute-start(f32[392,128]{1,0:T(8,128)S(1)} %get-tuple-element.55), channel_id=1, source_target_pairs={{0,1},{1,0},{2,3},{3,2},{32,33},{33,32},{34,35},{35,34},{64,65},{6... | collective-permute-start | bytes 602120 | tf_op jit(solution)/shard_map/ppermute | solution.py:83
  37.3 2.4 %shard_map.64 = (f32[46,16,128]{2,1,0:T(8,128)S(1)}, f32[46,16,128]{2,1,0:T(8,128)S(1)}, f32[46,16,128]{2,1,0:T(8,128)S(1)}) custom-call(f32[6,31,8,128]{3,2,1,0:T(8,128)S(1)} %get-tuple-element.46.table, bf16[96,256]{1,0:T(8,128)(2,1)S(1)} %get-tuple-element.56.fan_out, f32[6,128,128]{2,1,0:T(8,128)S(1)} %get-tuple-element.57.backward_z, ...), custom_call_target="tpu_custom_call" | custom-call | flops 17179869184 | bytes 67108864 | tf_op jit(solution)/shard_map/pallas_call | solution.py:551
  39.7 0.1 collective-permute-start.12
  39.8 5.5 %collective-permute-start.13 = (f32[46,16,128]{2,1,0:T(8,128)S(1)}, f32[46,16,128]{2,1,0:T(8,128)S(1)}, u32[]{:S(2)}, u32[]{:S(2)}) collective-permute-start(f32[46,16,128]{2,1,0:T(8,128)S(1)} %get-tuple-element.61), channel_id=1, source_target_pairs={{0,1},{1,0},{2,3},{3,2},{4,8},{5,9},{6,10},{7,11},{8,4},{9,5},{10,... | collective-permute-start | bytes 1130504 | tf_op jit(solution)/shard_map/ppermute | solution.py:72
  45.3 0.0 collective-permute-done.10.far_marks.far
  45.3 0.0 collective-permute-done.11.near_marks.near
  45.3 1.6 %shard_map.66 = (f32[23,16,128]{2,1,0:T(8,128)S(1)}, f32[23,16,128]{2,1,0:T(8,128)S(1)}, f32[23,16,128]{2,1,0:T(8,128)S(1)}) custom-call(f32[6,31,8,128]{3,2,1,0:T(8,128)S(1)} %get-tuple-element.46.table, bf16[96,256]{1,0:T(8,128)(2,1)S(1)} %get-tuple-element.65.fan_pair, f32[6,128,128]{2,1,0:T(8,128)S(1)} %get-tuple-element.66.rest_z, ...), custom_call_target="tpu_custom_call" | custom-call | flops 17179869184 | bytes 67108864 | tf_op jit(solution)/shard_map/pallas_call | solution.py:561
  46.9 0.1 collective-permute-start.16
  47.0 0.6 collective-permute-start.17
  47.7 3.8 %collective-permute-done.12.from_low = f32[46,16,128]{2,1,0:T(8,128)S(1)} collective-permute-done((f32[46,16,128]{2,1,0:T(8,128)S(1)}, f32[46,16,128]{2,1,0:T(8,128)S(1)}, u32[]{:S(2)}, u32[]{:S(2)}) %collective-permute-start.12) | collective-permute-done | bytes 376864 | tf_op jit(solution)/shard_map/ppermute | solution.py:72
  51.4 3.5 %collective-permute-done.13.from_high = f32[46,16,128]{2,1,0:T(8,128)S(1)} collective-permute-done((f32[46,16,128]{2,1,0:T(8,128)S(1)}, f32[46,16,128]{2,1,0:T(8,128)S(1)}, u32[]{:S(2)}, u32[]{:S(2)}) %collective-permute-start.13) | collective-permute-done | bytes 376864 | tf_op jit(solution)/shard_map/ppermute | solution.py:72
  54.9 0.1 shard_map.65
  55.1 0.1 collective-permute-start.14
  55.2 1.0 %collective-permute-start.15 = (f32[16,16,128]{2,1,0:T(8,128)S(1)}, f32[16,16,128]{2,1,0:T(8,128)S(1)}, u32[]{:S(2)}, u32[]{:S(2)}) collective-permute-start(f32[16,16,128]{2,1,0:T(8,128)S(1)} %get-tuple-element.64), channel_id=1, source_target_pairs={{0,1},{1,0},{2,3},{3,2},{32,64},{33,65},{34,66},{35,67},{64,32},{6... | collective-permute-start | bytes 393224 | tf_op jit(solution)/shard_map/ppermute | solution.py:72
  56.2 0.0 collective-permute-done.16.from_low
  56.2 1.8 %collective-permute-done.17.from_high = f32[23,16,128]{2,1,0:T(8,128)S(1)} collective-permute-done((f32[23,16,128]{2,1,0:T(8,128)S(1)}, f32[23,16,128]{2,1,0:T(8,128)S(1)}, u32[]{:S(2)}, u32[]{:S(2)}) %collective-permute-start.17) | collective-permute-done | bytes 188448 | tf_op jit(solution)/shard_map/ppermute | solution.py:72
  58.0 0.1 shard_map.67
  58.1 0.1 collective-permute-start.18
  58.2 1.5 %collective-permute-start.19 = (f32[8,16,128]{2,1,0:T(8,128)S(1)}, f32[8,16,128]{2,1,0:T(8,128)S(1)}, u32[]{:S(2)}, u32[]{:S(2)}) collective-permute-start(f32[8,16,128]{2,1,0:T(8,128)S(1)} %get-tuple-element.72), channel_id=1, source_target_pairs={{0,1},{1,0},{2,3},{3,2},{32,64},{33,65},{34,66},{35,67},{64,32},{6... | collective-permute-start | bytes 196616 | tf_op jit(solution)/shard_map/ppermute | solution.py:72
  59.6 0.0 copy-done.3
  59.7 1.2 %shard_map.63.scale = f32[16,16,128]{2,1,0:T(8,128)S(1)} custom-call(f32[3,8,128]{2,1,0:T(8,128)S(1)} %get-tuple-element.39.after.norm, f32[16,16,128]{2,1,0:T(8,128)S(1)} %copy-done.3, f32[8,128]{1,0:T(8,128)S(1)} %get-tuple-element.49.marks, f32[392,128]{1,0:T(8,128)S(1)} %collective-permute-done.10.far_marks.far, ...), custom_call_target="tpu_custom_call" | custom-call | bytes 524288 | tf_op jit(solution)/shard_map/pallas_call | solution.py:590
  60.9 1.6 %collective-permute-done.18.rest_low = f32[8,16,128]{2,1,0:T(8,128)S(1)} collective-permute-done((f32[8,16,128]{2,1,0:T(8,128)S(1)}, f32[8,16,128]{2,1,0:T(8,128)S(1)}, u32[]{:S(2)}, u32[]{:S(2)}) %collective-permute-start.18) | collective-permute-done | bytes 65568 | tf_op jit(solution)/shard_map/ppermute | solution.py:72
  62.4 2.2 %collective-permute-done.19.rest_high = f32[8,16,128]{2,1,0:T(8,128)S(1)} collective-permute-done((f32[8,16,128]{2,1,0:T(8,128)S(1)}, f32[8,16,128]{2,1,0:T(8,128)S(1)}, u32[]{:S(2)}, u32[]{:S(2)}) %collective-permute-start.19) | collective-permute-done | bytes 65568 | tf_op jit(solution)/shard_map/ppermute | solution.py:72
  64.7 0.0 collective-permute-done.14.from_low
  64.7 0.0 collective-permute-done.15.from_high
  64.7 0.8 %shard_map.68 = f32[16,16,128]{2,1,0:T(8,128)} custom-call(f32[16,16,128]{2,1,0:T(8,128)S(1)} %shard_map.63.scale, f32[16,16,128]{2,1,0:T(8,128)S(1)} %get-tuple-element.62.after.mid, f32[16,16,128]{2,1,0:T(8,128)S(1)} %collective-permute-done.14.from_low, f32[16,16,128]{2,1,0:T(8,128)S(1)} %collective-permute-done.15.from_high, ...), custom_call_target="tpu_custom_call" | custom-call | bytes 786432 | tf_op jit(solution)/shard_map/pallas_call | solution.py:593
  (8 shorter events, 0.0 us)
Async XLA Ops:
  0.0 18.3 %copy-start.8 = (s32[6,1,1,1]{0,3,2,1:T(1,128)S(1)}, s32[6,1,1,1]{0,3,2,1:T(1,128)}, u32[]{:S(2)}) copy-start(s32[6,1,1,1]{0,3,2,1:T(1,128)} %param.9) | copy-start | bytes 76
  0.0 8.6 %collective-permute-start.1 = (f32[16,16,128]{2,1,0:T(8,128)}, f32[16,16,128]{2,1,0:T(8,128)S(1)}, u32[]{:S(2)}, u32[]{:S(2)}) collective-permute-start(f32[16,16,128]{2,1,0:T(8,128)} %estimate.1), channel_id=1, source_target_pairs={{0,1},{1,0},{2,3},{3,2},{32,64},{33,65},{34,66},{35,67},{64,32},{6... | collective-permute-start | bytes 393224 | tf_op jit(solution)/shard_map/ppermute | solution.py:72
  1.5 7.1 %collective-permute-start = (f32[16,16,128]{2,1,0:T(8,128)}, f32[16,16,128]{2,1,0:T(8,128)S(1)}, u32[]{:S(2)}, u32[]{:S(2)}) collective-permute-start(f32[16,16,128]{2,1,0:T(8,128)} %estimate.1), channel_id=1, source_target_pairs={{0,32},{1,33},{2,34},{3,35},{32,0},{33,1},{34,2},{35,3},{64,96},{6... | collective-permute-start | bytes 393224 | tf_op jit(solution)/shard_map/ppermute | solution.py:72
  1.5 1.1 %copy-start = (f32[6,16,16,128]{3,2,1,0:T(8,128)S(1)}, f32[6,16,16,128]{3,2,1,0:T(8,128)}, u32[]{:S(2)}) copy-start(f32[6,16,16,128]{3,2,1,0:T(8,128)} %raw.3) | copy-start | bytes 2359300
  2.6 0.7 %copy-start.7 = (s32[6,1,1,1]{0,3,2,1:T(1,128)S(1)}, s32[6,1,1,1]{0,3,2,1:T(1,128)}, u32[]{:S(2)}) copy-start(s32[6,1,1,1]{0,3,2,1:T(1,128)} %param.9) | copy-start | bytes 76
  3.3 15.0 %copy-start.1 = (f32[6,16,16,128]{3,2,1,0:T(8,128)S(1)}, f32[6,16,16,128]{3,2,1,0:T(8,128)}, u32[]{:S(2)}) copy-start(f32[6,16,16,128]{3,2,1,0:T(8,128)} %raw.3) | copy-start | bytes 2359300
  3.9 11.5 %collective-permute-start.2 = (f32[49,16,128]{2,1,0:T(8,128)S(1)}, f32[49,16,128]{2,1,0:T(8,128)S(1)}, u32[]{:S(2)}, u32[]{:S(2)}) collective-permute-start(f32[49,16,128]{2,1,0:T(8,128)S(1)} %get-tuple-element.40), channel_id=1, source_target_pairs={{0,32},{1,33},{2,34},{3,35},{32,0},{33,1},{34,2},{35,3},{64,96},{6... | collective-permute-start | bytes 1204232 | tf_op jit(solution)/shard_map/ppermute | solution.py:72
  6.0 12.3 %collective-permute-start.3 = (f32[49,16,128]{2,1,0:T(8,128)S(1)}, f32[49,16,128]{2,1,0:T(8,128)S(1)}, u32[]{:S(2)}, u32[]{:S(2)}) collective-permute-start(f32[49,16,128]{2,1,0:T(8,128)S(1)} %get-tuple-element.41), channel_id=1, source_target_pairs={{0,1},{1,0},{2,3},{3,2},{32,64},{33,65},{34,66},{35,67},{64,32},{6... | collective-permute-start | bytes 1204232 | tf_op jit(solution)/shard_map/ppermute | solution.py:72
  8.6 0.9 %copy-start.2 = (f32[16,16,128]{2,1,0:T(8,128)S(1)}, f32[16,16,128]{2,1,0:T(8,128)}, u32[]{:S(2)}) copy-start(f32[16,16,128]{2,1,0:T(8,128)} %estimate.1) | copy-start | bytes 393220
  9.7 13.3 %collective-permute-start.7 = (f32[46,16,128]{2,1,0:T(8,128)S(1)}, f32[46,16,128]{2,1,0:T(8,128)S(1)}, u32[]{:S(2)}, u32[]{:S(2)}) collective-permute-start(f32[46,16,128]{2,1,0:T(8,128)S(1)} %shard_map.55.after.own), channel_id=1, source_target_pairs={{0,1},{1,0},{2,3},{3,2},{4,8},{5,9},{6,10},{7,11},{8,4},{9,5},{10,... | collective-permute-start | bytes 1130504 | tf_op jit(solution)/shard_map/ppermute | solution.py:72
  11.7 11.3 %collective-permute-start.6 = (f32[46,16,128]{2,1,0:T(8,128)S(1)}, f32[46,16,128]{2,1,0:T(8,128)S(1)}, u32[]{:S(2)}, u32[]{:S(2)}) collective-permute-start(f32[46,16,128]{2,1,0:T(8,128)S(1)} %shard_map.55.after.own), channel_id=1, source_target_pairs={{0,4},{1,5},{2,6},{3,7},{4,0},{5,1},{6,2},{7,3},{8,12},{9,13},{10,... | collective-permute-start | bytes 1130504 | tf_op jit(solution)/shard_map/ppermute | solution.py:72
  11.7 0.7 %copy-start.4 = (s32[6,3]{0,1:T(4,128)S(1)}, s32[6,3]{0,1:T(4,128)}, u32[]{:S(2)}) copy-start(s32[6,3]{0,1:T(4,128)} %param.8) | copy-start | bytes 220
  12.4 0.7 %copy-start.6 = (f32[6,3,31]{2,1,0:T(4,128)S(1)}, f32[6,3,31]{2,1,0:T(4,128)}, u32[]{:S(2)}) copy-start(f32[6,3,31]{2,1,0:T(4,128)} %psf.1) | copy-start | bytes 6700
  19.1 10.2 %collective-permute-start.4 = (f32[97,8,128]{2,1,0:T(8,128)S(1)}, f32[97,8,128]{2,1,0:T(8,128)S(1)}, u32[]{:S(2)}, u32[]{:S(2)}) collective-permute-start(f32[97,8,128]{2,1,0:T(8,128)S(1)} %get-tuple-element.43), channel_id=1, source_target_pairs={{0,4},{1,5},{2,6},{3,7},{4,0},{5,1},{6,2},{7,3},{8,12},{9,13},{10,... | collective-permute-start | bytes 1191944 | tf_op jit(solution)/shard_map/ppermute | solution.py:72
  19.3 10.9 %collective-permute-start.5 = (f32[97,8,128]{2,1,0:T(8,128)S(1)}, f32[97,8,128]{2,1,0:T(8,128)S(1)}, u32[]{:S(2)}, u32[]{:S(2)}) collective-permute-start(f32[97,8,128]{2,1,0:T(8,128)S(1)} %get-tuple-element.44), channel_id=1, source_target_pairs={{0,1},{1,0},{2,3},{3,2},{4,8},{5,9},{6,10},{7,11},{8,4},{9,5},{10,... | collective-permute-start | bytes 1191944 | tf_op jit(solution)/shard_map/ppermute | solution.py:72
  23.0 7.2 %copy-start.5 = (s32[6,3]{0,1:T(4,128)S(1)}, s32[6,3]{0,1:T(4,128)}, u32[]{:S(2)}) copy-start(s32[6,3]{0,1:T(4,128)} %param.8) | copy-start | bytes 220
  25.9 5.8 %collective-permute-start.8 = (f32[392,128]{1,0:T(8,128)S(1)}, f32[392,128]{1,0:T(8,128)S(1)}, u32[]{:S(2)}, u32[]{:S(2)}) collective-permute-start(f32[392,128]{1,0:T(8,128)S(1)} %get-tuple-element.52), channel_id=1, source_target_pairs={{0,32},{1,2},{2,1},{3,35},{32,0},{33,34},{34,33},{35,3},{64,96},{6... | collective-permute-start | bytes 602120 | tf_op jit(solution)/shard_map/ppermute | solution.py:83
  26.0 5.7 %collective-permute-start.9 = (f32[392,128]{1,0:T(8,128)S(1)}, f32[392,128]{1,0:T(8,128)S(1)}, u32[]{:S(2)}, u32[]{:S(2)}) collective-permute-start(f32[392,128]{1,0:T(8,128)S(1)} %get-tuple-element.53), channel_id=1, source_target_pairs={{0,1},{1,0},{2,3},{3,2},{32,33},{33,32},{34,35},{35,34},{64,65},{6... | collective-permute-start | bytes 602120 | tf_op jit(solution)/shard_map/ppermute | solution.py:83
  33.2 12.1 %collective-permute-start.10 = (f32[392,128]{1,0:T(8,128)S(1)}, f32[392,128]{1,0:T(8,128)S(1)}, u32[]{:S(2)}, u32[]{:S(2)}) collective-permute-start(f32[392,128]{1,0:T(8,128)S(1)} %get-tuple-element.54), channel_id=1, source_target_pairs={{0,32},{1,2},{2,1},{3,35},{32,0},{33,34},{34,33},{35,3},{64,96},{6... | collective-permute-start | bytes 602120 | tf_op jit(solution)/shard_map/ppermute | solution.py:83
  33.3 12.0 %collective-permute-start.11 = (f32[392,128]{1,0:T(8,128)S(1)}, f32[392,128]{1,0:T(8,128)S(1)}, u32[]{:S(2)}, u32[]{:S(2)}) collective-permute-start(f32[392,128]{1,0:T(8,128)S(1)} %get-tuple-element.55), channel_id=1, source_target_pairs={{0,1},{1,0},{2,3},{3,2},{32,33},{33,32},{34,35},{35,34},{64,65},{6... | collective-permute-start | bytes 602120 | tf_op jit(solution)/shard_map/ppermute | solution.py:83
  39.7 11.7 %collective-permute-start.12 = (f32[46,16,128]{2,1,0:T(8,128)S(1)}, f32[46,16,128]{2,1,0:T(8,128)S(1)}, u32[]{:S(2)}, u32[]{:S(2)}) collective-permute-start(f32[46,16,128]{2,1,0:T(8,128)S(1)} %get-tuple-element.60), channel_id=1, source_target_pairs={{0,4},{1,5},{2,6},{3,7},{4,0},{5,1},{6,2},{7,3},{8,12},{9,13},{10,... | collective-permute-start | bytes 1130504 | tf_op jit(solution)/shard_map/ppermute | solution.py:72
  39.8 15.1 %collective-permute-start.13 = (f32[46,16,128]{2,1,0:T(8,128)S(1)}, f32[46,16,128]{2,1,0:T(8,128)S(1)}, u32[]{:S(2)}, u32[]{:S(2)}) collective-permute-start(f32[46,16,128]{2,1,0:T(8,128)S(1)} %get-tuple-element.61), channel_id=1, source_target_pairs={{0,1},{1,0},{2,3},{3,2},{4,8},{5,9},{6,10},{7,11},{8,4},{9,5},{10,... | collective-permute-start | bytes 1130504 | tf_op jit(solution)/shard_map/ppermute | solution.py:72
  46.9 9.2 %collective-permute-start.16 = (f32[23,16,128]{2,1,0:T(8,128)S(1)}, f32[23,16,128]{2,1,0:T(8,128)S(1)}, u32[]{:S(2)}, u32[]{:S(2)}) collective-permute-start(f32[23,16,128]{2,1,0:T(8,128)S(1)} %get-tuple-element.68), channel_id=1, source_target_pairs={{0,4},{1,5},{2,6},{3,7},{4,0},{5,1},{6,2},{7,3},{8,12},{9,13},{10,... | collective-permute-start | bytes 565256 | tf_op jit(solution)/shard_map/ppermute | solution.py:72
  47.0 11.0 %collective-permute-start.17 = (f32[23,16,128]{2,1,0:T(8,128)S(1)}, f32[23,16,128]{2,1,0:T(8,128)S(1)}, u32[]{:S(2)}, u32[]{:S(2)}) collective-permute-start(f32[23,16,128]{2,1,0:T(8,128)S(1)} %get-tuple-element.69), channel_id=1, source_target_pairs={{0,1},{1,0},{2,3},{3,2},{4,8},{5,9},{6,10},{7,11},{8,4},{9,5},{10,... | collective-permute-start | bytes 565256 | tf_op jit(solution)/shard_map/ppermute | solution.py:72
  55.1 9.6 %collective-permute-start.14 = (f32[16,16,128]{2,1,0:T(8,128)S(1)}, f32[16,16,128]{2,1,0:T(8,128)S(1)}, u32[]{:S(2)}, u32[]{:S(2)}) collective-permute-start(f32[16,16,128]{2,1,0:T(8,128)S(1)} %get-tuple-element.63), channel_id=1, source_target_pairs={{0,32},{1,33},{2,34},{3,35},{32,0},{33,1},{34,2},{35,3},{64,96},{6... | collective-permute-start | bytes 393224 | tf_op jit(solution)/shard_map/ppermute | solution.py:72
  55.2 9.5 %collective-permute-start.15 = (f32[16,16,128]{2,1,0:T(8,128)S(1)}, f32[16,16,128]{2,1,0:T(8,128)S(1)}, u32[]{:S(2)}, u32[]{:S(2)}) collective-permute-start(f32[16,16,128]{2,1,0:T(8,128)S(1)} %get-tuple-element.64), channel_id=1, source_target_pairs={{0,1},{1,0},{2,3},{3,2},{32,64},{33,65},{34,66},{35,67},{64,32},{6... | collective-permute-start | bytes 393224 | tf_op jit(solution)/shard_map/ppermute | solution.py:72
  58.0 1.6 %copy-start.3 = (f32[16,16,128]{2,1,0:T(8,128)S(1)}, f32[16,16,128]{2,1,0:T(8,128)}, u32[]{:S(2)}) copy-start(f32[16,16,128]{2,1,0:T(8,128)} %estimate.1) | copy-start | bytes 393220
  58.1 4.4 %collective-permute-start.18 = (f32[8,16,128]{2,1,0:T(8,128)S(1)}, f32[8,16,128]{2,1,0:T(8,128)S(1)}, u32[]{:S(2)}, u32[]{:S(2)}) collective-permute-start(f32[8,16,128]{2,1,0:T(8,128)S(1)} %get-tuple-element.71), channel_id=1, source_target_pairs={{0,32},{1,33},{2,34},{3,35},{32,0},{33,1},{34,2},{35,3},{64,96},{6... | collective-permute-start | bytes 196616 | tf_op jit(solution)/shard_map/ppermute | solution.py:72
  58.2 6.5 %collective-permute-start.19 = (f32[8,16,128]{2,1,0:T(8,128)S(1)}, f32[8,16,128]{2,1,0:T(8,128)S(1)}, u32[]{:S(2)}, u32[]{:S(2)}) collective-permute-start(f32[8,16,128]{2,1,0:T(8,128)S(1)} %get-tuple-element.72), channel_id=1, source_target_pairs={{0,1},{1,0},{2,3},{3,2},{32,64},{33,65},{34,66},{35,67},{64,32},{6... | collective-permute-start | bytes 196616 | tf_op jit(solution)/shard_map/ppermute | solution.py:72
